TPU v7x, 32 devices: a whole 2x2x4 slice. The times are simulated.
32 devices in a mesh: vv: 8 (over y, x, core), oo: 4 (over z).
Axes of the slice: x: 2, y: 2, z: 4, core: 2. Of those that a mesh axis runs over, the one named last changes fastest.
Arguments:
- amplitudes: bfloat16 [24, 512, 128], P('vv', 'oo'), may hold values from -6 to 6
- tile_counts: int32 [24], P('vv'), may hold values from 1 to 48, as said below
- tile_lists: int32 [24, 48], P('vv', 'oo'), may hold values from 0 to 23, as said below
- integrals: bfloat16 [24, 48, 128, 128], P('vv', 'oo'), may hold values from -0.078125 to 0.078125
Outputs:
- ladder: float32 [512, 3072], P('oo', 'vv')
Inputs may be any that keep to these rules, and one draw needn't show every extreme that they name: `tile_counts`: every tile's list has at least one live slot, and some tile's list is full. `tile_lists`: a list may name a tile more than once; slots at or after the row's count name tiles too but are not live.
All inputs are finite; a program needn't handle non-finite values.
Results may differ from a plain program's by a relative error of at most 0.0003.
Values may be sent and summed in bfloat16 or wider, within the bound.
No kernel may reach another device: no remote copies, remote signals or barrier semaphores. Data moves between devices by JAX's collectives and lax.ppermute only.
A program may use at most 64 MiB of HBM per device.

v0:
```python
import jax
import jax.numpy as jnp
from jax import lax
from jax.sharding import PartitionSpec as P


def on_device(amplitudes, tile_counts, tile_lists, integrals):
    tile_dev, slot_dev = tile_lists.shape
    group_index = lax.axis_index("oo")
    live_counts = jnp.clip(tile_counts - group_index * slot_dev, 0, slot_dev)
    slot_ids = jnp.arange(slot_dev, dtype=jnp.int32)
    living = slot_ids[None, :] < live_counts[:, None]
    full_rows = lax.all_gather(amplitudes, "oo", axis=1, tiled=True)
    pairs = full_rows.shape[1]
    everything = lax.all_gather(full_rows, "vv", axis=0, tiled=True)
    picked = jnp.take(everything, tile_lists, axis=0)
    masked = jnp.where(living[:, :, None, None], picked, jnp.zeros_like(picked))
    partial_value = jnp.einsum(
        "alpc,alqc->paq", masked, integrals, preferred_element_type=jnp.float32
    )
    partial_value = partial_value.reshape(pairs, tile_dev * integrals.shape[2])
    return lax.psum_scatter(partial_value, "oo", scatter_dimension=0, tiled=True)


def solution(mesh):
    placed = (P("vv", "oo", None), P("vv"), P("vv", "oo"), P("vv", "oo", None, None))
    return jax.shard_map(
        on_device, mesh=mesh, in_specs=placed, out_specs=P("oo", "vv"), check_vma=False
    )
```

profile of v0, /device:TPU:0, one launch (start us, length us, event | category | flops | bytes accessed | tf_op | source)
XLA Modules:
  0.0 99.1 jit_solution(9208176181967071141)
XLA Ops:
  6.5 0.0 copy-start
  6.5 0.0 all-gather.2.cloned.1.call-start
  6.5 18.3 %all_gather.6 = bf16[3,512,128]{2,1,0:T(8,128)(2,1)} all-gather(bf16[3,128,128]{2,1,0:T(8,128)(2,1)} %param.4), channel_id=1, replica_groups=mesh['vv'=8,'oo'=4] {'oo'}, dimensions={1}, use_global_device_ids=true | all-gather | bytes 491520 | tf_op jit(solution)/shard_map/all_gather | solution.py:13
  24.8 0.0 all-gather.2.cloned.1.call-update
  24.8 0.0 reduce-scatter.2.cloned.1.call-start
  24.9 0.7 compare_select_fusion
  25.6 0.1 reshape.32
  25.7 0.7 subtract_clamp_fusion
  26.3 0.8 iota_compare_fusion
  27.1 30.1 %all-gather.2.cloned.1.call-done = bf16[24,512,128]{2,1,0:T(8,128)(2,1)} async-done(((bf16[3,512,128]{2,1,0:T(8,128)(2,1)}), bf16[24,512,128]{2,1,0:T(8,128)(2,1)}) %all-gather.2.cloned.1.call-update) | async-done | bytes 3145744 | tf_op jit(solution)/shard_map/all_gather | solution.py:15
  57.2 6.3 %gather_fusion = bf16[36,512,128]{2,1,0:T(8,128)(2,1)} fusion(bf16[24,512,128]{2,1,0:T(8,128)(2,1)} %all-gather.2.cloned.1.call-done, s32[1024]{0:T(1024)S(1)} %pad_clamp_fusion), kind=kCustom, calls=%fused_computation | custom fusion | bytes 9437328 | tf_op jit(solution)/shard_map/jit(_take)/gather | solution.py:16
  63.5 0.0 copy-done
  63.5 4.1 %fusion = f32[3,512,128,1]{1,2,3,0:T(8,128)S(1)} fusion(bf16[3,12,128,128]{3,2,1,0:T(8,128)(2,1)S(1)} %copy-done, bf16[3,12,512,128]{3,2,1,0:T(8,128)(2,1)} %bitcast.8, pred[3,12]{1,0:T(4,128)(4,1)S(1)} %get-tuple-element.6, pred[3,12]{1,0:T(4,128)(4,1)S(1)} %get-tuple-element.5), kind=kOutput, calls=%fused_computation.1 | convolution fusion | flops 608698368 | bytes 6684744 | tf_op jit(solution)/shard_map/alpc,alqc->paq/dot_general | solution.py:18
  67.6 1.2 %copy.6 = f32[512,384]{1,0:T(8,128)} copy(f32[512,384]{0,1:T(8,128)S(1)} %bitcast.9) | data formatting | bytes 1572864 | tf_op jit(solution)/shard_map/reshape | solution.py:21
  68.8 0.0 reduce-scatter.2.cloned.1.call-update
  68.8 23.4 %reduce-scatter.2.cloned.1.call-done = f32[128,384]{1,0:T(8,128)} async-done(((f32[512,384]{1,0:T(8,128)}), f32[128,384]{1,0:T(8,128)}) %reduce-scatter.2.cloned.1.call-update) | async-done | bytes 196624 | tf_op jit(solution)/shard_map/reduce_scatter | solution.py:22
  (1 shorter events, 0.0 us)
Async XLA Ops:
  6.5 57.0 %copy-start = (bf16[3,12,128,128]{3,2,1,0:T(8,128)(2,1)S(1)}, bf16[3,12,128,128]{3,2,1,0:T(8,128)(2,1)}, u32[]{:S(2)}) copy-start(bf16[3,12,128,128]{3,2,1,0:T(8,128)(2,1)} %param.7) | copy-start | bytes 3538948
  6.5 50.7 %all-gather.2.cloned.1.call-start = ((), (), s32[]{:S(2)}) async-start(), calls=%async_computation.1 | async-start | bytes 3538944 | tf_op jit(solution)/shard_map/all_gather | solution.py:15
  24.8 67.4 %reduce-scatter.2.cloned.1.call-start = ((), (), s32[]{:S(2)}) async-start(), calls=%async_computation.2 | async-start | bytes 983040 | tf_op jit(solution)/shard_map/reduce_scatter | solution.py:22
Sparse Core Ops, SparseCore 0:
  25.0 32.2 all-gather.1
  68.9 23.2 reduce-scatter.1
where the time goes:
time: 99.3 us; the launch traced here: 99.1 us
  waiting for transfers between devices  53.6 us (54%)
  blocking collectives  18.3 us (18%)
  between operations  13.4 us (13%)
  local copies, waits for them, and re-layouts  7.58 us (8%)
  matrix products  4.05 us (4%)
  other arithmetic  2.11 us (2%)
    all_gather x1, waiting for transfers between devices, on_device(): everything = lax.all_gather(full_rows, 'vv', axis=0, tiled=True)  30.1 us
    reduce_scatter x1, waiting for transfers between devices, on_device(): lax.psum_scatter(partial_value, 'oo', scatter_dimension=0, tiled=True)  23.4 us
    all_gather x1, blocking collectives, on_device(): full_rows = lax.all_gather(amplitudes, 'oo', axis=1, tiled=True)  18.3 us
    gather x1, local copies, waits for them, and re-layouts, on_device(): picked = jnp.take(everything, tile_lists, axis=0)  6.32 us
    dot_general x1, matrix products, on_device(): jnp.einsum('alpc,alqc->paq', masked, integrals, preferred_element_type=jn...  4.05 us
  transfers between devices with their start and end apart: 2, of which 2 were waited for; matrix products, arithmetic and copies ran while one was open for 2% of the time, Pallas kernels for 0%

commit v1 on v0

v1 whole, which is shorter than its diff:
```python
import jax
import jax.numpy as jnp
from jax import lax
from jax.experimental import pallas as pl
from jax.experimental.pallas import tpu as pltpu
from jax.sharding import PartitionSpec as P

VMEM_BYTES = 48 * 1024 * 1024


def shift(value, axis, size, mask):
    return lax.ppermute(value, axis, [(j, j ^ mask) for j in range(size)])


def contract(lists_ref, live_ref, stage, integrals_ref, out_ref):
    tile_dev, slots, width, depth = integrals_ref.shape
    blocks, _, rows, _ = stage.shape
    dims = (((1,), (1,)), ((), ()))
    for a in range(tile_dev):
        live = live_ref[a]

        def step(pair, total, a=a, live=live):
            s = 2 * pair
            left = stage[:, lists_ref[a, s]].reshape(blocks * rows, depth)
            right = stage[:, lists_ref[a, jnp.minimum(s + 1, slots - 1)]].reshape(blocks * rows, depth)
            second = jnp.where(s + 1 < live, integrals_ref[a, jnp.minimum(s + 1, slots - 1)], jnp.zeros((width, depth), integrals_ref.dtype))
            both = jnp.concatenate([left, right], axis=1)
            weights = jnp.concatenate([integrals_ref[a, s], second], axis=1)
            return total + lax.dot_general(both, weights, dims, preferred_element_type=jnp.float32)

        total = lax.fori_loop(0, (live + 1) // 2, step, jnp.zeros((blocks * rows, width), jnp.float32))
        for k in range(blocks):
            out_ref[k, :, a * width:(a + 1) * width] = total[k * rows:(k + 1) * rows]


def ladder_kernel(lists_ref, live_ref, place_ref, *refs, layout):
    count = len(layout)
    pieces, integrals_ref, out_ref, stage, sems = refs[:count], refs[count], refs[count + 1], refs[count + 2], refs[count + 3]
    copies = []
    for n, (mask, first) in enumerate(layout):
        piece = pieces[n]
        base = (place_ref[0] ^ mask) * piece.shape[1]
        copy = pltpu.make_async_copy(
            piece, stage.at[pl.ds(first, piece.shape[0]), pl.ds(base, piece.shape[1])], sems.at[n]
        )
        copy.start()
        copies.append(copy)
    for copy in copies:
        copy.wait()
    contract(lists_ref, live_ref, stage, integrals_ref, out_ref)


def partials(lists, live, place, pieces, layout, integrals, blocks, tiles):
    tile_dev, _, width, depth = integrals.shape
    rows = pieces[0].shape[2]
    smem = pl.BlockSpec(memory_space=pltpu.SMEM)
    return pl.pallas_call(
        lambda *refs: ladder_kernel(*refs, layout=layout),
        out_shape=jax.ShapeDtypeStruct((blocks, rows, tile_dev * width), jnp.float32),
        in_specs=[smem] * 3 + [pl.BlockSpec(memory_space=pl.ANY)] * len(pieces) + [pl.BlockSpec(memory_space=pltpu.VMEM)],
        out_specs=pl.BlockSpec(memory_space=pltpu.VMEM),
        scratch_shapes=[
            pltpu.VMEM((blocks, tiles, rows, depth), integrals.dtype),
            pltpu.SemaphoreType.DMA((len(pieces),)),
        ],
        compiler_params=pltpu.CompilerParams(vmem_limit_bytes=VMEM_BYTES),
    )(lists, live, place, *pieces, integrals)


def on_device(amplitudes, tile_counts, tile_lists, integrals, n_vv, n_oo):
    slots = tile_lists.shape[1]
    tiles = n_vv * amplitudes.shape[0]
    group = lax.axis_index("oo")
    live = jnp.clip(tile_counts - group * slots, 0, slots)
    if (n_vv, n_oo) == (8, 4):
        far = [shift(amplitudes, "oo", n_oo, k) for k in (2, 3)]
        near = shift(amplitudes, "oo", n_oo, 1)
        own = jnp.stack([amplitudes, near] + far)
        by_x = shift(own, "vv", n_vv, 2)
        by_y = shift(own, "vv", n_vv, 4)
        low = shift(by_x[:2], "vv", n_vv, 4)
        high = shift(by_y[2:], "vv", n_vv, 2)
        pieces = [own, by_x, by_y, low, high]
        layout = [(0, 0), (2, 0), (4, 0), (6, 0), (6, 2)]
        pieces = pieces + [shift(p, "vv", n_vv, 1) for p in pieces]
        layout = layout + [(m ^ 1, f) for m, f in layout]
        place = lax.axis_index("vv").astype(jnp.int32).reshape(1)
        parts = partials(tile_lists, live, place, pieces, layout, integrals, n_oo, tiles)
        total = parts[0]
        for k in (2, 3, 1):
            total = total + shift(parts[k], "oo", n_oo, k)
        return total
    rows = lax.all_gather(amplitudes, "oo", axis=0, tiled=False)
    everything = lax.all_gather(rows, "vv", axis=1, tiled=True)
    place = jnp.zeros((1,), jnp.int32)
    parts = partials(tile_lists, live, place, [everything], [(0, 0)], integrals, n_oo, tiles)
    return lax.psum_scatter(parts.reshape(-1, parts.shape[2]), "oo", scatter_dimension=0, tiled=True)


def solution(mesh):
    n_vv, n_oo = mesh.shape["vv"], mesh.shape["oo"]
    placed = (P("vv", "oo", None), P("vv"), P("vv", "oo"), P("vv", "oo", None, None))
    return jax.shard_map(
        lambda *args: on_device(*args, n_vv, n_oo),
        mesh=mesh, in_specs=placed, out_specs=P("oo", "vv"), check_vma=False,
    )
```

time: 99.3 us -> 59.3 us (0.60)
  waiting for transfers between devices: 53.6 us -> 34 us
  blocking collectives: 18.3 us -> 0 us
  starting transfers between devices: 0.04 us -> 16.7 us
  between operations: 13.4 us -> 0.08 us
  local copies, waits for them, and re-layouts: 7.58 us -> 1.44 us
  Pallas kernels: 0 us -> 5.48 us
  matrix products: 4.05 us -> 0 us
    ppermute x0 -> x15, waiting for transfers between devices: none -> 34 us  [shift(): return lax.ppermute(value, axis, [(j, j ^ mask) for j in range(size)])]
    all_gather x1 -> x0, waiting for transfers between devices: 30.1 us -> none  [on_device(): everything = lax.all_gather(full_rows, 'vv', axis=0, tiled=True)]
    reduce_scatter x1 -> x0, waiting for transfers between devices: 23.4 us -> none  [on_device(): lax.psum_scatter(partial_value, 'oo', scatter_dimension=0, tiled=True)]
    all_gather x1 -> x0, blocking collectives: 18.3 us -> none  [on_device(): full_rows = lax.all_gather(amplitudes, 'oo', axis=1, tiled=True)]
    ppermute x0 -> x15, starting transfers between devices: none -> 16.7 us  [shift(): return lax.ppermute(value, axis, [(j, j ^ mask) for j in range(size)])]
    gather x1 -> x0, local copies, waits for them, and re-layouts: 6.32 us -> none  [on_device(): picked = jnp.take(everything, tile_lists, axis=0)]
    pallas_call x0 -> x1, Pallas kernels: none -> 5.48 us  [partials(): pl.pallas_call(lambda *refs: ladder_kernel(*refs, layout=layout), out_sha...]
    dot_general x1 -> x0, matrix products: 4.05 us -> none  [on_device(): jnp.einsum('alpc,alqc->paq', masked, integrals, preferred_element_type=jn...]
  transfers between devices with their start and end apart: 2 -> 15, of which waited for: 2 -> 9; matrix products, arithmetic and copies ran while one was open for 2% -> 2% of each run, Pallas kernels for 0% -> 0%
where the time goes in v1:
time: 59.3 us; the launch traced here: 59.4 us
  waiting for transfers between devices  34 us (57%)
  starting transfers between devices  16.7 us (28%)
  Pallas kernels  5.48 us (9%)
  other arithmetic  1.68 us (3%)
  local copies, waits for them, and re-layouts  1.44 us (2%)
    ppermute x15, waiting for transfers between devices, shift(): return lax.ppermute(value, axis, [(j, j ^ mask) for j in range(size)])  34 us
    ppermute x15, starting transfers between devices, shift(): return lax.ppermute(value, axis, [(j, j ^ mask) for j in range(size)])  16.7 us
    pallas_call x1, Pallas kernels, partials(): pl.pallas_call(lambda *refs: ladder_kernel(*refs, layout=layout), out_sha...  5.48 us
  transfers between devices with their start and end apart: 15, of which 9 were waited for; matrix products, arithmetic and copies ran while one was open for 2% of the time, Pallas kernels for 0%

profile of v1, /device:TPU:0, one launch (start us, length us, event | category | flops | bytes accessed | tf_op | source)
XLA Modules:
  0.0 59.4 jit_solution(6903444648854811403)
XLA Ops:
  0.0 3.1 %collective-permute-start = (bf16[3,128,128]{2,1,0:T(8,128)(2,1)}, bf16[3,128,128]{2,1,0:T(8,128)(2,1)S(1)}, u32[]{:S(2)}, u32[]{:S(2)}) collective-permute-start(bf16[3,128,128]{2,1,0:T(8,128)(2,1)} %param.4), channel_id=1, source_target_pairs={{0,1},{1,0},{2,3},{3,2},{4,5},{5,4},{6,7},{7,6},{8,9},{9,8},{10,11... | collective-permute-start | bytes 294920 | tf_op jit(solution)/shard_map/ppermute | solution.py:12
  3.1 2.5 %collective-permute-start.2 = (bf16[3,128,128]{2,1,0:T(8,128)(2,1)}, bf16[3,128,128]{2,1,0:T(8,128)(2,1)S(1)}, u32[]{:S(2)}, u32[]{:S(2)}) collective-permute-start(bf16[3,128,128]{2,1,0:T(8,128)(2,1)} %param.4), channel_id=1, source_target_pairs={{0,3},{1,2},{2,1},{3,0},{4,7},{5,6},{6,5},{7,4},{8,11},{9,10},{10,... | collective-permute-start | bytes 294920 | tf_op jit(solution)/shard_map/ppermute | solution.py:12
  5.6 0.1 collective-permute-start.1
  5.7 0.4 collective-permute-done
  6.1 5.4 %collective-permute-done.2 = bf16[3,128,128]{2,1,0:T(8,128)(2,1)S(1)} collective-permute-done((bf16[3,128,128]{2,1,0:T(8,128)(2,1)}, bf16[3,128,128]{2,1,0:T(8,128)(2,1)S(1)}, u32[]{:S(2)}, u32[]{:S(2)}) %collective-permute-start.2) | collective-permute-done | bytes 98336 | tf_op jit(solution)/shard_map/ppermute | solution.py:12
  11.5 3.3 %collective-permute-done.1 = bf16[3,128,128]{2,1,0:T(8,128)(2,1)S(1)} collective-permute-done((bf16[3,128,128]{2,1,0:T(8,128)(2,1)}, bf16[3,128,128]{2,1,0:T(8,128)(2,1)S(1)}, u32[]{:S(2)}, u32[]{:S(2)}) %collective-permute-start.1) | collective-permute-done | bytes 98336 | tf_op jit(solution)/shard_map/ppermute | solution.py:12
  14.8 0.9 %pad_maximum_fusion.refs_3_ = bf16[4,3,128,128]{3,2,1,0:T(8,128)(2,1)S(1)} fusion(bf16[1,3,128,128]{3,2,1,0:T(8,128)(2,1)S(1)} %bitcast.21, bf16[1,3,128,128]{3,2,1,0:T(8,128)(2,1)S(1)} %bitcast.22, bf16[1,3,128,128]{3,2,1,0:T(8,128)(2,1)S(1)} %bitcast.20, bf16[1,3,128,128]{3,2,1,0:T(8,128)(2,1)} %bitcast.19), kind=kLoop, calls=%fused_computation | loop fusion | flops 589824 | bytes 786432 | tf_op jit(solution)/shard_map/stack | solution.py:78
  15.7 1.6 %collective-permute-start.4 = (bf16[4,3,128,128]{3,2,1,0:T(8,128)(2,1)S(1)}, bf16[4,3,128,128]{3,2,1,0:T(8,128)(2,1)S(1)}, u32[]{:S(2)}, u32[]{:S(2)}) collective-permute-start(bf16[4,3,128,128]{3,2,1,0:T(8,128)(2,1)S(1)} %pad_maximum_fusion.refs_3_), channel_id=1, source_target_pairs={{0,16},{4,20},{8,24},{12,28},{16,0},{20,4},{24,8},{28,12},{1,17},{... | collective-permute-start | bytes 1179656 | tf_op jit(solution)/shard_map/ppermute | solution.py:12
  17.3 1.5 %collective-permute-start.3 = (bf16[4,3,128,128]{3,2,1,0:T(8,128)(2,1)S(1)}, bf16[4,3,128,128]{3,2,1,0:T(8,128)(2,1)S(1)}, u32[]{:S(2)}, u32[]{:S(2)}) collective-permute-start(bf16[4,3,128,128]{3,2,1,0:T(8,128)(2,1)S(1)} %pad_maximum_fusion.refs_3_), channel_id=1, source_target_pairs={{0,8},{4,12},{8,0},{12,4},{16,24},{20,28},{24,16},{28,20},{1,9},{5... | collective-permute-start | bytes 1179656 | tf_op jit(solution)/shard_map/ppermute | solution.py:12
  18.8 7.6 %collective-permute-done.4.refs_5_ = bf16[4,3,128,128]{3,2,1,0:T(8,128)(2,1)S(1)} collective-permute-done((bf16[4,3,128,128]{3,2,1,0:T(8,128)(2,1)S(1)}, bf16[4,3,128,128]{3,2,1,0:T(8,128)(2,1)S(1)}, u32[]{:S(2)}, u32[]{:S(2)}) %collective-permute-start.4) | collective-permute-done | bytes 393248 | tf_op jit(solution)/shard_map/ppermute | solution.py:12
  26.3 0.7 %slice.25 = bf16[2,3,128,128]{3,2,1,0:T(8,128)(2,1)} slice(bf16[4,3,128,128]{3,2,1,0:T(8,128)(2,1)S(1)} %collective-permute-done.4.refs_5_), slice={[2:4], [0:3], [0:128], [0:128]} | slice | bytes 393216 | tf_op jit(solution)/shard_map/slice | solution.py:82
  27.0 1.5 %collective-permute-start.6 = (bf16[2,3,128,128]{3,2,1,0:T(8,128)(2,1)}, bf16[2,3,128,128]{3,2,1,0:T(8,128)(2,1)}, u32[]{:S(2)}, u32[]{:S(2)}) collective-permute-start(bf16[2,3,128,128]{3,2,1,0:T(8,128)(2,1)} %slice.25), channel_id=1, source_target_pairs={{0,8},{4,12},{8,0},{12,4},{16,24},{20,28},{24,16},{28,20},{1,9},{5... | collective-permute-start | bytes 589832 | tf_op jit(solution)/shard_map/ppermute | solution.py:12
  28.5 0.7 %slice.24 = bf16[2,3,128,128]{3,2,1,0:T(8,128)(2,1)} slice(bf16[4,3,128,128]{3,2,1,0:T(8,128)(2,1)S(1)} %collective-permute-done.3.refs_4_), slice={[0:2], [0:3], [0:128], [0:128]} | slice | bytes 393216 | tf_op jit(solution)/shard_map/slice | solution.py:81
  29.2 1.5 %collective-permute-start.5 = (bf16[2,3,128,128]{3,2,1,0:T(8,128)(2,1)}, bf16[2,3,128,128]{3,2,1,0:T(8,128)(2,1)}, u32[]{:S(2)}, u32[]{:S(2)}) collective-permute-start(bf16[2,3,128,128]{3,2,1,0:T(8,128)(2,1)} %slice.24), channel_id=1, source_target_pairs={{0,16},{4,20},{8,24},{12,28},{16,0},{20,4},{24,8},{28,12},{1,17},{... | collective-permute-start | bytes 589832 | tf_op jit(solution)/shard_map/ppermute | solution.py:12
  30.8 0.5 collective-permute-start.9
  31.3 1.8 %collective-permute-done.6.refs_7_ = bf16[2,3,128,128]{3,2,1,0:T(8,128)(2,1)} collective-permute-done((bf16[2,3,128,128]{3,2,1,0:T(8,128)(2,1)}, bf16[2,3,128,128]{3,2,1,0:T(8,128)(2,1)}, u32[]{:S(2)}, u32[]{:S(2)}) %collective-permute-start.6) | collective-permute-done | bytes 196640 | tf_op jit(solution)/shard_map/ppermute | solution.py:12
  33.0 2.2 %collective-permute-done.5.refs_6_ = bf16[2,3,128,128]{3,2,1,0:T(8,128)(2,1)} collective-permute-done((bf16[2,3,128,128]{3,2,1,0:T(8,128)(2,1)}, bf16[2,3,128,128]{3,2,1,0:T(8,128)(2,1)}, u32[]{:S(2)}, u32[]{:S(2)}) %collective-permute-start.5) | collective-permute-done | bytes 196640 | tf_op jit(solution)/shard_map/ppermute | solution.py:12
  35.3 1.6 %collective-permute-done.10.refs_11_ = bf16[2,3,128,128]{3,2,1,0:T(8,128)(2,1)S(1)} collective-permute-done((bf16[2,3,128,128]{3,2,1,0:T(8,128)(2,1)}, bf16[2,3,128,128]{3,2,1,0:T(8,128)(2,1)S(1)}, u32[]{:S(2)}, u32[]{:S(2)}) %collective-permute-start.10) | collective-permute-done | bytes 196640 | tf_op jit(solution)/shard_map/ppermute | solution.py:12
  36.9 5.5 %shard_map.46 = f32[4,128,384]{2,1,0:T(8,128)S(1)} custom-call(s32[3,12]{1,0:T(4,128)S(1)} %copy-done.1, s32[3]{0:T(128)S(1)} %subtract_clamp_fusion.refs_1_, s32[1]{0:T(128)} %bitcast.refs_2_, bf16[4,3,128,128]{3,2,1,0:T(8,128)(2,1)S(1)} %pad_maximum_fusion.refs_3_, bf16[4,3,128,128]{3,2,1,0:T(8,128)(2,1)S(1)} %collective-permute-done.3.refs_4_, ...), custom_call_target="tpu_custom_call" | custom-call | tf_op jit(solution)/shard_map/pallas_call | solution.py:57
  42.5 0.8 %collective-permute-start.14 = (f32[128,384]{1,0:T(8,128)S(1)}, f32[128,384]{1,0:T(8,128)S(1)}, u32[]{:S(2)}, u32[]{:S(2)}) collective-permute-start(f32[128,384]{1,0:T(8,128)S(1)} %get-tuple-element.6), channel_id=1, source_target_pairs={{0,1},{1,0},{2,3},{3,2},{4,5},{5,4},{6,7},{7,6},{8,9},{9,8},{10,11... | collective-permute-start | bytes 589832 | tf_op jit(solution)/shard_map/ppermute | solution.py:12
  43.3 3.6 %collective-permute-start.13 = (f32[128,384]{1,0:T(8,128)S(1)}, f32[128,384]{1,0:T(8,128)S(1)}, u32[]{:S(2)}, u32[]{:S(2)}) collective-permute-start(f32[128,384]{1,0:T(8,128)S(1)} %get-tuple-element.7), channel_id=1, source_target_pairs={{0,3},{1,2},{2,1},{3,0},{4,7},{5,6},{6,5},{7,4},{8,11},{9,10},{10,... | collective-permute-start | bytes 589832 | tf_op jit(solution)/shard_map/ppermute | solution.py:12
  46.9 5.1 %collective-permute-done.12 = f32[128,384]{1,0:T(8,128)S(1)} collective-permute-done((f32[128,384]{1,0:T(8,128)S(1)}, f32[128,384]{1,0:T(8,128)S(1)}, u32[]{:S(2)}, u32[]{:S(2)}) %collective-permute-start.12) | collective-permute-done | bytes 196640 | tf_op jit(solution)/shard_map/ppermute | solution.py:12
  52.0 6.7 %collective-permute-done.14 = f32[128,384]{1,0:T(8,128)S(1)} collective-permute-done((f32[128,384]{1,0:T(8,128)S(1)}, f32[128,384]{1,0:T(8,128)S(1)}, u32[]{:S(2)}, u32[]{:S(2)}) %collective-permute-start.14) | collective-permute-done | bytes 196640 | tf_op jit(solution)/shard_map/ppermute | solution.py:12
  58.7 0.7 %fusion.2 = f32[128,384]{1,0:T(8,128)} fusion(f32[128,384]{1,0:T(8,128)S(1)} %collective-permute-done.14, f32[128,384]{1,0:T(8,128)S(1)} %collective-permute-done.13, f32[128,384]{1,0:T(8,128)S(1)} %collective-permute-done.12, f32[4,128,384]{2,1,0:T(8,128)S(1)} %shard_map.46), kind=kLoop, calls=%fused_computation.7 | loop fusion | flops 147456 | bytes 983040 | tf_op jit(solution)/shard_map/add | solution.py:91
  (19 shorter events, 0.2 us)
Async XLA Ops:
  0.0 35.2 %copy-start.2 = (s32[3]{0:T(128)S(1)}, s32[3]{0:T(128)}, u32[]{:S(2)}) copy-start(s32[3]{0:T(128)} %param.5) | copy-start | bytes 40
  0.0 36.9 %copy-start = (bf16[3,12,128,128]{3,2,1,0:T(8,128)(2,1)S(1)}, bf16[3,12,128,128]{3,2,1,0:T(8,128)(2,1)}, u32[]{:S(2)}) copy-start(bf16[3,12,128,128]{3,2,1,0:T(8,128)(2,1)} %refs_13_.1) | copy-start | bytes 3538948
  0.0 36.9 %copy-start.1 = (s32[3,12]{1,0:T(4,128)S(1)}, s32[3,12]{1,0:T(4,128)}, u32[]{:S(2)}) copy-start(s32[3,12]{1,0:T(4,128)} %refs_0_.1) | copy-start | bytes 436
  0.0 6.1 %collective-permute-start = (bf16[3,128,128]{2,1,0:T(8,128)(2,1)}, bf16[3,128,128]{2,1,0:T(8,128)(2,1)S(1)}, u32[]{:S(2)}, u32[]{:S(2)}) collective-permute-start(bf16[3,128,128]{2,1,0:T(8,128)(2,1)} %param.4), channel_id=1, source_target_pairs={{0,1},{1,0},{2,3},{3,2},{4,5},{5,4},{6,7},{7,6},{8,9},{9,8},{10,11... | collective-permute-start | bytes 294920 | tf_op jit(solution)/shard_map/ppermute | solution.py:12
  3.1 8.4 %collective-permute-start.2 = (bf16[3,128,128]{2,1,0:T(8,128)(2,1)}, bf16[3,128,128]{2,1,0:T(8,128)(2,1)S(1)}, u32[]{:S(2)}, u32[]{:S(2)}) collective-permute-start(bf16[3,128,128]{2,1,0:T(8,128)(2,1)} %param.4), channel_id=1, source_target_pairs={{0,3},{1,2},{2,1},{3,0},{4,7},{5,6},{6,5},{7,4},{8,11},{9,10},{10,... | collective-permute-start | bytes 294920 | tf_op jit(solution)/shard_map/ppermute | solution.py:12
  5.6 9.2 %collective-permute-start.1 = (bf16[3,128,128]{2,1,0:T(8,128)(2,1)}, bf16[3,128,128]{2,1,0:T(8,128)(2,1)S(1)}, u32[]{:S(2)}, u32[]{:S(2)}) collective-permute-start(bf16[3,128,128]{2,1,0:T(8,128)(2,1)} %param.4), channel_id=1, source_target_pairs={{0,2},{1,3},{2,0},{3,1},{4,6},{5,7},{6,4},{7,5},{8,10},{9,11},{10,... | collective-permute-start | bytes 294920 | tf_op jit(solution)/shard_map/ppermute | solution.py:12
  15.7 10.6 %collective-permute-start.4 = (bf16[4,3,128,128]{3,2,1,0:T(8,128)(2,1)S(1)}, bf16[4,3,128,128]{3,2,1,0:T(8,128)(2,1)S(1)}, u32[]{:S(2)}, u32[]{:S(2)}) collective-permute-start(bf16[4,3,128,128]{3,2,1,0:T(8,128)(2,1)S(1)} %pad_maximum_fusion.refs_3_), channel_id=1, source_target_pairs={{0,16},{4,20},{8,24},{12,28},{16,0},{20,4},{24,8},{28,12},{1,17},{... | collective-permute-start | bytes 1179656 | tf_op jit(solution)/shard_map/ppermute | solution.py:12
  17.3 11.2 %collective-permute-start.3 = (bf16[4,3,128,128]{3,2,1,0:T(8,128)(2,1)S(1)}, bf16[4,3,128,128]{3,2,1,0:T(8,128)(2,1)S(1)}, u32[]{:S(2)}, u32[]{:S(2)}) collective-permute-start(bf16[4,3,128,128]{3,2,1,0:T(8,128)(2,1)S(1)} %pad_maximum_fusion.refs_3_), channel_id=1, source_target_pairs={{0,8},{4,12},{8,0},{12,4},{16,24},{20,28},{24,16},{28,20},{1,9},{5... | collective-permute-start | bytes 1179656 | tf_op jit(solution)/shard_map/ppermute | solution.py:12
  27.0 6.0 %collective-permute-start.6 = (bf16[2,3,128,128]{3,2,1,0:T(8,128)(2,1)}, bf16[2,3,128,128]{3,2,1,0:T(8,128)(2,1)}, u32[]{:S(2)}, u32[]{:S(2)}) collective-permute-start(bf16[2,3,128,128]{3,2,1,0:T(8,128)(2,1)} %slice.25), channel_id=1, source_target_pairs={{0,8},{4,12},{8,0},{12,4},{16,24},{20,28},{24,16},{28,20},{1,9},{5... | collective-permute-start | bytes 589832 | tf_op jit(solution)/shard_map/ppermute | solution.py:12
  29.2 6.0 %collective-permute-start.5 = (bf16[2,3,128,128]{3,2,1,0:T(8,128)(2,1)}, bf16[2,3,128,128]{3,2,1,0:T(8,128)(2,1)}, u32[]{:S(2)}, u32[]{:S(2)}) collective-permute-start(bf16[2,3,128,128]{3,2,1,0:T(8,128)(2,1)} %slice.24), channel_id=1, source_target_pairs={{0,16},{4,20},{8,24},{12,28},{16,0},{20,4},{24,8},{28,12},{1,17},{... | collective-permute-start | bytes 589832 | tf_op jit(solution)/shard_map/ppermute | solution.py:12
  30.7 4.5 %collective-permute-start.7 = (bf16[4,3,128,128]{3,2,1,0:T(8,128)(2,1)S(1)}, bf16[4,3,128,128]{3,2,1,0:T(8,128)(2,1)S(1)}, u32[]{:S(2)}, u32[]{:S(2)}) collective-permute-start(bf16[4,3,128,128]{3,2,1,0:T(8,128)(2,1)S(1)} %pad_maximum_fusion.refs_3_), channel_id=1, source_target_pairs={{0,4},{4,0},{8,12},{12,8},{16,20},{20,16},{24,28},{28,24},{1,5},{5... | collective-permute-start | bytes 1179656 | tf_op jit(solution)/shard_map/ppermute | solution.py:12
  30.8 4.5 %collective-permute-start.9 = (bf16[4,3,128,128]{3,2,1,0:T(8,128)(2,1)S(1)}, bf16[4,3,128,128]{3,2,1,0:T(8,128)(2,1)S(1)}, u32[]{:S(2)}, u32[]{:S(2)}) collective-permute-start(bf16[4,3,128,128]{3,2,1,0:T(8,128)(2,1)S(1)} %collective-permute-done.4.refs_5_), channel_id=1, source_target_pairs={{0,4},{4,0},{8,12},{12,8},{16,20},{20,16},{24,28},{28,24},{1,5},{5... | collective-permute-start | bytes 1179656 | tf_op jit(solution)/shard_map/ppermute | solution.py:12
  31.3 5.6 %collective-permute-start.8 = (bf16[4,3,128,128]{3,2,1,0:T(8,128)(2,1)S(1)}, bf16[4,3,128,128]{3,2,1,0:T(8,128)(2,1)S(1)}, u32[]{:S(2)}, u32[]{:S(2)}) collective-permute-start(bf16[4,3,128,128]{3,2,1,0:T(8,128)(2,1)S(1)} %collective-permute-done.3.refs_4_), channel_id=1, source_target_pairs={{0,4},{4,0},{8,12},{12,8},{16,20},{20,16},{24,28},{28,24},{1,5},{5... | collective-permute-start | bytes 1179656 | tf_op jit(solution)/shard_map/ppermute | solution.py:12
  33.0 2.2 %collective-permute-start.11 = (bf16[2,3,128,128]{3,2,1,0:T(8,128)(2,1)}, bf16[2,3,128,128]{3,2,1,0:T(8,128)(2,1)S(1)}, u32[]{:S(2)}, u32[]{:S(2)}) collective-permute-start(bf16[2,3,128,128]{3,2,1,0:T(8,128)(2,1)} %collective-permute-done.6.refs_7_), channel_id=1, source_target_pairs={{0,4},{4,0},{8,12},{12,8},{16,20},{20,16},{24,28},{28,24},{1,5},{5... | collective-permute-start | bytes 589832 | tf_op jit(solution)/shard_map/ppermute | solution.py:12
  35.2 1.7 %collective-permute-start.10 = (bf16[2,3,128,128]{3,2,1,0:T(8,128)(2,1)}, bf16[2,3,128,128]{3,2,1,0:T(8,128)(2,1)S(1)}, u32[]{:S(2)}, u32[]{:S(2)}) collective-permute-start(bf16[2,3,128,128]{3,2,1,0:T(8,128)(2,1)} %collective-permute-done.5.refs_6_), channel_id=1, source_target_pairs={{0,4},{4,0},{8,12},{12,8},{16,20},{20,16},{24,28},{28,24},{1,5},{5... | collective-permute-start | bytes 589832 | tf_op jit(solution)/shard_map/ppermute | solution.py:12
  42.4 9.5 %collective-permute-start.12 = (f32[128,384]{1,0:T(8,128)S(1)}, f32[128,384]{1,0:T(8,128)S(1)}, u32[]{:S(2)}, u32[]{:S(2)}) collective-permute-start(f32[128,384]{1,0:T(8,128)S(1)} %get-tuple-element.5), channel_id=1, source_target_pairs={{0,2},{1,3},{2,0},{3,1},{4,6},{5,7},{6,4},{7,5},{8,10},{9,11},{10,... | collective-permute-start | bytes 589832 | tf_op jit(solution)/shard_map/ppermute | solution.py:12
  42.5 16.2 %collective-permute-start.14 = (f32[128,384]{1,0:T(8,128)S(1)}, f32[128,384]{1,0:T(8,128)S(1)}, u32[]{:S(2)}, u32[]{:S(2)}) collective-permute-start(f32[128,384]{1,0:T(8,128)S(1)} %get-tuple-element.6), channel_id=1, source_target_pairs={{0,1},{1,0},{2,3},{3,2},{4,5},{5,4},{6,7},{7,6},{8,9},{9,8},{10,11... | collective-permute-start | bytes 589832 | tf_op jit(solution)/shard_map/ppermute | solution.py:12
  43.3 15.4 %collective-permute-start.13 = (f32[128,384]{1,0:T(8,128)S(1)}, f32[128,384]{1,0:T(8,128)S(1)}, u32[]{:S(2)}, u32[]{:S(2)}) collective-permute-start(f32[128,384]{1,0:T(8,128)S(1)} %get-tuple-element.7), channel_id=1, source_target_pairs={{0,3},{1,2},{2,1},{3,0},{4,7},{5,6},{6,5},{7,4},{8,11},{9,10},{10,... | collective-permute-start | bytes 589832 | tf_op jit(solution)/shard_map/ppermute | solution.py:12

commit v2 on v0

v2 whole, which is shorter than its diff:
```python
import jax
import jax.numpy as jnp
from jax import lax
from jax.experimental import pallas as pl
from jax.experimental.pallas import tpu as pltpu
from jax.sharding import PartitionSpec as P

VMEM_BYTES = 48 * 1024 * 1024
UNROLL = 4
OWN_FLOPS = 4000000000
SMEM = pl.BlockSpec(memory_space=pltpu.SMEM)
VMEM = pl.BlockSpec(memory_space=pltpu.VMEM)
ANY = pl.BlockSpec(memory_space=pl.ANY)


def shift(value, axis, size, mask):
    return lax.ppermute(value, axis, [(j, j ^ mask) for j in range(size)])


def contract(total, lists_ref, a, live, stage, blocks_of):
    blocks, _, rows, depth = stage.shape
    slots = lists_ref.shape[1]
    dims = (((1,), (1,)), ((), ()))

    def pair(s):
        sides, weights = [], []
        for slot in (s, s + 1):
            safe = jnp.minimum(slot, slots - 1)
            block = blocks_of(safe)
            sides.append(stage[:, lists_ref[a, safe]].reshape(blocks * rows, depth))
            weights.append(jnp.where(slot < live, block, jnp.zeros_like(block)))
        return lax.dot_general(
            jnp.concatenate(sides, axis=1), jnp.concatenate(weights, axis=1), dims, preferred_element_type=jnp.float32
        )

    def step(group, total):
        for offset in range(0, UNROLL, 2):
            total = total + pair(UNROLL * group + offset)
        return total

    return lax.fori_loop(0, (live + UNROLL - 1) // UNROLL, step, total)


def gather_pieces(place_ref, pieces, layout, stage, sems):
    copies = []
    for n, (mask, first) in enumerate(layout):
        piece = pieces[n]
        base = (place_ref[0] ^ mask) * piece.shape[1]
        copy = pltpu.make_async_copy(
            piece, stage.at[pl.ds(first, piece.shape[0]), pl.ds(base, piece.shape[1])], sems.at[n]
        )
        copy.start()
        copies.append(copy)
    for copy in copies:
        copy.wait()


def plain_kernel(lists_ref, live_ref, place_ref, piece, integrals_ref, out_ref, stage, sems):
    gather_pieces(place_ref, [piece], [(0, 0)], stage, sems)
    tile_dev, _, width, _ = integrals_ref.shape
    blocks, _, rows, _ = stage.shape
    for a in range(tile_dev):
        zero = jnp.zeros((blocks * rows, width), jnp.float32)
        total = contract(zero, lists_ref, a, live_ref[a], stage, lambda s, a=a: integrals_ref[a, s])
        for k in range(blocks):
            out_ref[k, :, a * width:(a + 1) * width] = total[k * rows:(k + 1) * rows]


def plain_partials(lists, live, everything, integrals):
    blocks, tiles, rows, depth = everything.shape
    tile_dev, _, width, _ = integrals.shape
    return pl.pallas_call(
        plain_kernel,
        out_shape=jax.ShapeDtypeStruct((blocks, rows, tile_dev * width), jnp.float32),
        in_specs=[SMEM] * 3 + [ANY, VMEM],
        out_specs=VMEM,
        scratch_shapes=[pltpu.VMEM((blocks, tiles, rows, depth), everything.dtype), pltpu.SemaphoreType.DMA((1,))],
        compiler_params=pltpu.CompilerParams(vmem_limit_bytes=VMEM_BYTES),
    )(lists, live, jnp.zeros((1,), jnp.int32), everything, integrals)


def cut_kernel(whole, head, tail, sems):
    copies = [
        pltpu.make_async_copy(whole.at[pl.ds(0, head.shape[0])], head, sems.at[0]),
        pltpu.make_async_copy(whole.at[pl.ds(head.shape[0], tail.shape[0])], tail, sems.at[1]),
    ]
    for copy in copies:
        copy.start()
    for copy in copies:
        copy.wait()


def cut(whole, first):
    count = whole.shape[0]
    return pl.pallas_call(
        cut_kernel,
        out_shape=tuple(jax.ShapeDtypeStruct((n,) + whole.shape[1:], whole.dtype) for n in (first, count - first)),
        in_specs=[ANY],
        out_specs=(VMEM,) * 2,
        scratch_shapes=[pltpu.SemaphoreType.DMA((2,))],
        compiler_params=pltpu.CompilerParams(vmem_limit_bytes=VMEM_BYTES),
    )(whole)


def live_slots(counts_ref, a, group, slots):
    return jnp.clip(counts_ref[a] - group * slots, 0, slots)


def own_kernel(layout, counts_ref, lists_ref, place_ref, *refs):
    count = len(layout)
    pieces, integrals_ref = refs[:count], refs[count]
    sums_ref, stage, sems = refs[count + 1:]
    gather_pieces(place_ref, pieces, layout, stage, sems)
    tile_dev, slots, width, _ = integrals_ref.shape
    blocks, _, rows, _ = stage.shape
    for a in range(tile_dev):
        total = jnp.zeros((blocks * rows, width), jnp.float32)
        live = live_slots(counts_ref, a, place_ref[1], slots)
        sums_ref[a] = contract(total, lists_ref, a, live, stage, lambda s, a=a: integrals_ref[a, s])


def other_kernel(first, counts_ref, other_ref, place_ref, stage, sums_ref, others, own_ref, far_ref):
    rows = own_ref.shape[0]
    count, slots, width, _ = others.shape
    for n in range(count):
        live = live_slots(counts_ref, first + n, place_ref[1] ^ 1, slots)
        total = contract(sums_ref[first + n], other_ref, first + n, live, stage, lambda s, n=n: others[n, s])
        own_ref[:, n * width:(n + 1) * width] = total[:rows]
        far_ref[:, n * width:(n + 1) * width] = total[rows:]


def on_pairs(amplitudes, tile_counts, tile_lists, integrals, n_vv, n_oo):
    tile_dev, slots, width, depth = integrals.shape
    rows = amplitudes.shape[1]
    tiles = n_vv * tile_dev
    ready = tile_dev - 1
    place = jnp.stack([lax.axis_index("vv"), lax.axis_index("oo")]).astype(jnp.int32)

    far = shift(amplitudes, "oo", n_oo, 2)
    head, tail = (shift(part, "oo", n_oo, 1) for part in cut(integrals, ready))
    far, amplitudes, sent = lax.optimization_barrier((far, amplitudes, tile_lists))
    other_lists = shift(sent, "oo", n_oo, 1)
    pieces, layout = [], []
    for first, block in enumerate((amplitudes[None], far[None])):
        for mask in (0, 2, 4, 6):
            piece = shift(block, "vv", n_vv, mask) if mask else block
            pieces += [piece, shift(piece, "vv", n_vv, 1)]
            layout += [(mask, first), (mask ^ 1, first)]
    params = pltpu.CompilerParams(vmem_limit_bytes=VMEM_BYTES)
    sums, stage = pl.pallas_call(
        lambda *refs: own_kernel(layout, *refs),
        out_shape=(
            jax.ShapeDtypeStruct((tile_dev, 2 * rows, width), jnp.float32),
            jax.ShapeDtypeStruct((2, tiles, rows, depth), amplitudes.dtype),
        ),
        in_specs=[SMEM] * 3 + [ANY] * len(pieces) + [VMEM],
        out_specs=(VMEM,) * 2,
        scratch_shapes=[pltpu.SemaphoreType.DMA((len(pieces),))],
        compiler_params=params,
        cost_estimate=pl.CostEstimate(flops=OWN_FLOPS, bytes_accessed=2**22, transcendentals=0),
    )(tile_counts, tile_lists, place, *pieces, integrals)
    results = []
    for first, others in ((0, head), (ready, tail)):
        part = jax.ShapeDtypeStruct((rows, others.shape[0] * width), jnp.float32)
        own, away = pl.pallas_call(
            lambda *refs, first=first: other_kernel(first, *refs),
            out_shape=(part,) * 2,
            in_specs=[SMEM] * 3 + [VMEM] * 3,
            out_specs=(VMEM,) * 2,
            compiler_params=params,
            cost_estimate=pl.CostEstimate(flops=2**28, bytes_accessed=2**21, transcendentals=0),
        )(tile_counts, other_lists, place, stage, sums, others)
        results.append(own + shift(away, "oo", n_oo, 2))
    return jnp.concatenate(results, axis=1)


def on_device(amplitudes, tile_counts, tile_lists, integrals, n_vv, n_oo):
    if (n_vv, n_oo) == (8, 4):
        return on_pairs(amplitudes, tile_counts, tile_lists, integrals, n_vv, n_oo)
    slots = tile_lists.shape[1]
    live = jnp.clip(tile_counts - lax.axis_index("oo") * slots, 0, slots)
    rows = lax.all_gather(amplitudes, "oo", axis=0, tiled=False)
    everything = lax.all_gather(rows, "vv", axis=1, tiled=True)
    parts = plain_partials(tile_lists, live, everything, integrals)
    return lax.psum_scatter(parts.reshape(-1, parts.shape[2]), "oo", scatter_dimension=0, tiled=True)


def solution(mesh):
    n_vv, n_oo = mesh.shape["vv"], mesh.shape["oo"]
    placed = (P("vv", "oo", None), P("vv"), P("vv", "oo"), P("vv", "oo", None, None))
    return jax.shard_map(
        lambda *args: on_device(*args, n_vv, n_oo),
        mesh=mesh, in_specs=placed, out_specs=P("oo", "vv"), check_vma=False,
    )
```

time: 99.3 us -> 49 us (0.49)
  waiting for transfers between devices: 53.6 us -> 15.3 us
  starting transfers between devices: 0.04 us -> 19 us
  blocking collectives: 18.3 us -> 0 us
  between operations: 13.4 us -> 0.09 us
  Pallas kernels: 0 us -> 8.31 us
  matrix products: 4.05 us -> 0 us
  local copies, waits for them, and re-layouts: 7.58 us -> 4.77 us
  other arithmetic: 2.11 us -> 0.8 us
    all_gather x1 -> x0, waiting for transfers between devices: 30.1 us -> none  [on_device(): everything = lax.all_gather(full_rows, 'vv', axis=0, tiled=True)]
    reduce_scatter x1 -> x0, waiting for transfers between devices: 23.4 us -> none  [on_device(): lax.psum_scatter(partial_value, 'oo', scatter_dimension=0, tiled=True)]
    ppermute x0 -> x20, starting transfers between devices: none -> 19 us  [shift(): return lax.ppermute(value, axis, [(j, j ^ mask) for j in range(size)])]
    all_gather x1 -> x0, blocking collectives: 18.3 us -> none  [on_device(): full_rows = lax.all_gather(amplitudes, 'oo', axis=1, tiled=True)]
    ppermute x0 -> x20, waiting for transfers between devices: none -> 15.3 us  [shift(): return lax.ppermute(value, axis, [(j, j ^ mask) for j in range(size)])]
    pallas_call x0 -> x4, Pallas kernels: none -> 8.31 us  [the longest x1 5.14 us: on_pairs(): pl.pallas_call(lambda *refs: own_kernel(layout, *refs), out_shape=(jax.Sh...]
    gather x1 -> x0, local copies, waits for them, and re-layouts: 6.32 us -> none  [on_device(): picked = jnp.take(everything, tile_lists, axis=0)]
    unnamed x2 -> x10, local copies, waits for them, and re-layouts: 0.01 us -> 4.77 us
  transfers between devices with their start and end apart: 2 -> 20, of which waited for: 2 -> 8; matrix products, arithmetic and copies ran while one was open for 2% -> 0% of each run, Pallas kernels for 0% -> 17%
where the time goes in v2:
time: 49 us; the launch traced here: 48.2 us
  starting transfers between devices  19 us (39%)
  waiting for transfers between devices  15.3 us (31%)
  Pallas kernels  8.31 us (17%)
  local copies, waits for them, and re-layouts  4.77 us (10%)
  other arithmetic  0.8 us (2%)
    ppermute x20, starting transfers between devices, shift(): return lax.ppermute(value, axis, [(j, j ^ mask) for j in range(size)])  19 us
    ppermute x20, waiting for transfers between devices, shift(): return lax.ppermute(value, axis, [(j, j ^ mask) for j in range(size)])  15.3 us
    pallas_call x1, Pallas kernels, on_pairs(): pl.pallas_call(lambda *refs: own_kernel(layout, *refs), out_shape=(jax.Sh...  5.14 us
    unnamed x10, local copies, waits for them, and re-layouts  4.77 us
    pallas_call x2, Pallas kernels, on_pairs(): pl.pallas_call(lambda *refs, first=first: other_kernel(first, *refs), out...  2.91 us
  transfers between devices with their start and end apart: 20, of which 8 were waited for; matrix products, arithmetic and copies ran while one was open for 0% of the time, Pallas kernels for 17%

profile of v2, /device:TPU:0, one launch (start us, length us, event | category | flops | bytes accessed | tf_op | source)
XLA Modules:
  0.0 48.2 jit_solution(391743060412772461)
XLA Ops:
  0.0 4.0 %collective-permute-start = (bf16[3,128,128]{2,1,0:T(8,128)(2,1)}, bf16[3,128,128]{2,1,0:T(8,128)(2,1)S(1)}, u32[]{:S(2)}, u32[]{:S(2)}) collective-permute-start(bf16[3,128,128]{2,1,0:T(8,128)(2,1)} %param.4), channel_id=1, source_target_pairs={{0,2},{1,3},{2,0},{3,1},{4,6},{5,7},{6,4},{7,5},{8,10},{9,11},{10,... | collective-permute-start | bytes 294920 | tf_op jit(solution)/shard_map/ppermute | solution.py:17
  4.0 1.3 %copy-done = bf16[3,12,128,128]{3,2,1,0:T(8,128)(2,1)S(1)} copy-done((bf16[3,12,128,128]{3,2,1,0:T(8,128)(2,1)S(1)}, bf16[3,12,128,128]{3,2,1,0:T(8,128)(2,1)}, u32[]{:S(2)}) %copy-start) | copy-done | bytes 1179672
  5.6 1.6 %collective-permute-start.16 = (bf16[2,12,128,128]{3,2,1,0:T(8,128)(2,1)S(1)}, bf16[2,12,128,128]{3,2,1,0:T(8,128)(2,1)S(1)}, u32[]{:S(2)}, u32[]{:S(2)}) collective-permute-start(bf16[2,12,128,128]{3,2,1,0:T(8,128)(2,1)S(1)} %get-tuple-element.21), channel_id=1, source_target_pairs={{0,1},{1,0},{2,3},{3,2},{4,5},{5,4},{6,7},{7,6},{8,9},{9,8},{10,11... | collective-permute-start | bytes 2359304 | tf_op jit(solution)/shard_map/ppermute | solution.py:17
  7.2 2.0 %collective-permute-done = bf16[3,128,128]{2,1,0:T(8,128)(2,1)S(1)} collective-permute-done((bf16[3,128,128]{2,1,0:T(8,128)(2,1)}, bf16[3,128,128]{2,1,0:T(8,128)(2,1)S(1)}, u32[]{:S(2)}, u32[]{:S(2)}) %collective-permute-start) | collective-permute-done | bytes 98336 | tf_op jit(solution)/shard_map/ppermute | solution.py:17
  9.3 2.5 %collective-permute-start.7 = (bf16[1,3,128,128]{3,2,1,0:T(8,128)(2,1)}, bf16[1,3,128,128]{3,2,1,0:T(8,128)(2,1)S(1)}, u32[]{:S(2)}, u32[]{:S(2)}) collective-permute-start(bf16[1,3,128,128]{3,2,1,0:T(8,128)(2,1)} %bitcast.4), channel_id=1, source_target_pairs={{0,24},{4,28},{8,16},{12,20},{16,8},{20,12},{24,0},{28,4},{1,25},{... | collective-permute-start | bytes 294920 | tf_op jit(solution)/shard_map/ppermute | solution.py:17
  11.8 0.5 %collective-permute-start.5 = (bf16[1,3,128,128]{3,2,1,0:T(8,128)(2,1)}, bf16[1,3,128,128]{3,2,1,0:T(8,128)(2,1)S(1)}, u32[]{:S(2)}, u32[]{:S(2)}) collective-permute-start(bf16[1,3,128,128]{3,2,1,0:T(8,128)(2,1)} %bitcast.5), channel_id=1, source_target_pairs={{0,16},{4,20},{8,24},{12,28},{16,0},{20,4},{24,8},{28,12},{1,17},{... | collective-permute-start | bytes 294920 | tf_op jit(solution)/shard_map/ppermute | solution.py:17
  12.3 0.5 collective-permute-start.3
  12.7 2.2 %collective-permute-done.7.refs_9_ = bf16[1,3,128,128]{3,2,1,0:T(8,128)(2,1)S(1)} collective-permute-done((bf16[1,3,128,128]{3,2,1,0:T(8,128)(2,1)}, bf16[1,3,128,128]{3,2,1,0:T(8,128)(2,1)S(1)}, u32[]{:S(2)}, u32[]{:S(2)}) %collective-permute-start.7) | collective-permute-done | bytes 98336 | tf_op jit(solution)/shard_map/ppermute | solution.py:17
  15.0 2.6 %collective-permute-start.14 = (bf16[1,3,128,128]{3,2,1,0:T(8,128)(2,1)S(1)}, bf16[1,3,128,128]{3,2,1,0:T(8,128)(2,1)S(1)}, u32[]{:S(2)}, u32[]{:S(2)}) collective-permute-start(bf16[1,3,128,128]{3,2,1,0:T(8,128)(2,1)S(1)} %bitcast.9), channel_id=1, source_target_pairs={{0,24},{4,28},{8,16},{12,20},{16,8},{20,12},{24,0},{28,4},{1,25},{... | collective-permute-start | bytes 294920 | tf_op jit(solution)/shard_map/ppermute | solution.py:17
  18.0 0.6 %collective-permute-start.10 = (bf16[1,3,128,128]{3,2,1,0:T(8,128)(2,1)S(1)}, bf16[1,3,128,128]{3,2,1,0:T(8,128)(2,1)S(1)}, u32[]{:S(2)}, u32[]{:S(2)}) collective-permute-start(bf16[1,3,128,128]{3,2,1,0:T(8,128)(2,1)S(1)} %bitcast.11), channel_id=1, source_target_pairs={{0,8},{4,12},{8,0},{12,4},{16,24},{20,28},{24,16},{28,20},{1,9},{5... | collective-permute-start | bytes 294920 | tf_op jit(solution)/shard_map/ppermute | solution.py:17
  18.6 2.8 %collective-permute-done.14.refs_17_ = bf16[1,3,128,128]{3,2,1,0:T(8,128)(2,1)S(1)} collective-permute-done((bf16[1,3,128,128]{3,2,1,0:T(8,128)(2,1)S(1)}, bf16[1,3,128,128]{3,2,1,0:T(8,128)(2,1)S(1)}, u32[]{:S(2)}, u32[]{:S(2)}) %collective-permute-start.14) | collective-permute-done | bytes 98336 | tf_op jit(solution)/shard_map/ppermute | solution.py:17
  21.5 0.9 %collective-permute-done.12.refs_15_ = bf16[1,3,128,128]{3,2,1,0:T(8,128)(2,1)S(1)} collective-permute-done((bf16[1,3,128,128]{3,2,1,0:T(8,128)(2,1)S(1)}, bf16[1,3,128,128]{3,2,1,0:T(8,128)(2,1)S(1)}, u32[]{:S(2)}, u32[]{:S(2)}) %collective-permute-start.12) | collective-permute-done | bytes 98336 | tf_op jit(solution)/shard_map/ppermute | solution.py:17
  24.0 1.6 %collective-permute-start.18 = (bf16[1,12,128,128]{3,2,1,0:T(8,128)(2,1)S(1)}, bf16[1,12,128,128]{3,2,1,0:T(8,128)(2,1)S(1)}, u32[]{:S(2)}, u32[]{:S(2)}) collective-permute-start(bf16[1,12,128,128]{3,2,1,0:T(8,128)(2,1)S(1)} %get-tuple-element.24), channel_id=1, source_target_pairs={{0,1},{1,0},{2,3},{3,2},{4,5},{5,4},{6,7},{7,6},{8,9},{9,8},{10,11... | collective-permute-start | bytes 1179656 | tf_op jit(solution)/shard_map/ppermute | solution.py:17
  26.0 1.3 %copy-done.1 = bf16[3,12,128,128]{3,2,1,0:T(8,128)(2,1)S(1)} copy-done((bf16[3,12,128,128]{3,2,1,0:T(8,128)(2,1)S(1)}, bf16[3,12,128,128]{3,2,1,0:T(8,128)(2,1)}, u32[]{:S(2)}) %copy-start.1) | copy-done | bytes 1179672
  27.3 0.7 %copy-done.2 = s32[3]{0:T(128)S(1)} copy-done((s32[3]{0:T(128)S(1)}, s32[3]{0:T(128)}, u32[]{:S(2)}) %copy-start.2) | copy-done | bytes 36
  27.9 0.9 %copy-done.3 = bf16[3,128,128]{2,1,0:T(8,128)(2,1)S(1)} copy-done((bf16[3,128,128]{2,1,0:T(8,128)(2,1)S(1)}, bf16[3,128,128]{2,1,0:T(8,128)(2,1)}, u32[]{:S(2)}) %copy-start.3) | copy-done | bytes 98328
  28.8 0.7 %copy-done.4 = s32[3,12]{1,0:T(4,128)S(1)} copy-done((s32[3,12]{1,0:T(4,128)S(1)}, s32[3,12]{1,0:T(4,128)}, u32[]{:S(2)}) %copy-start.4) | copy-done | bytes 168
  29.5 5.1 %shard_map.46 = (f32[3,256,128]{2,1,0:T(8,128)S(1)}, bf16[2,24,128,128]{3,2,1,0:T(8,128)(2,1)S(1)}) custom-call(s32[3]{0:T(128)S(1)} %copy-done.2, s32[3,12]{1,0:T(4,128)S(1)} %copy-done.4, s32[2]{0:T(128)S(1)} %pad_add_fusion.refs_2_, bf16[1,3,128,128]{3,2,1,0:T(8,128)(2,1)S(1)} %bitcast.8, bf16[1,3,128,128]{3,2,1,0:T(8,128)(2,1)S(1)} %collective-permute-done.2.refs_4_, ...), custom_call_target="tpu_custom_call" | custom-call | flops 4000000000 | bytes 4194304 | tf_op jit(solution)/shard_map/pallas_call | solution.py:150
  34.7 0.7 %collective-permute-done.1.refs_1_ = s32[3,12]{1,0:T(4,128)S(1)} collective-permute-done((s32[3,12]{1,0:T(4,128)}, s32[3,12]{1,0:T(4,128)S(1)}, u32[]{:S(2)}, u32[]{:S(2)}) %collective-permute-start.1) | collective-permute-done | bytes 176 | tf_op jit(solution)/shard_map/ppermute | solution.py:17
  35.4 2.1 %shard_map.48 = (f32[128,256]{1,0:T(8,128)S(1)}, f32[128,256]{1,0:T(8,128)S(1)}) custom-call(s32[3]{0:T(128)S(1)} %copy-done.2, s32[3,12]{1,0:T(4,128)S(1)} %collective-permute-done.1.refs_1_, s32[2]{0:T(128)S(1)} %pad_add_fusion.refs_2_, bf16[2,24,128,128]{3,2,1,0:T(8,128)(2,1)S(1)} %get-tuple-element.19.refs_3_, ...), custom_call_target="tpu_custom_call" | custom-call | flops 268435456 | bytes 2097152 | tf_op jit(solution)/shard_map/pallas_call | solution.py:165
  37.4 3.1 %collective-permute-start.17 = (f32[128,256]{1,0:T(8,128)S(1)}, f32[128,256]{1,0:T(8,128)S(1)}, u32[]{:S(2)}, u32[]{:S(2)}) collective-permute-start(f32[128,256]{1,0:T(8,128)S(1)} %get-tuple-element.23), channel_id=1, source_target_pairs={{0,2},{1,3},{2,0},{3,1},{4,6},{5,7},{6,4},{7,5},{8,10},{9,11},{10,... | collective-permute-start | bytes 393224 | tf_op jit(solution)/shard_map/ppermute | solution.py:17
  40.6 0.8 %shard_map.49 = (f32[128,128]{1,0:T(8,128)S(1)}, f32[128,128]{1,0:T(8,128)S(1)}) custom-call(s32[3]{0:T(128)S(1)} %copy-done.2, s32[3,12]{1,0:T(4,128)S(1)} %collective-permute-done.1.refs_1_, s32[2]{0:T(128)S(1)} %pad_add_fusion.refs_2_, bf16[2,24,128,128]{3,2,1,0:T(8,128)(2,1)S(1)} %get-tuple-element.19.refs_3_, ...), custom_call_target="tpu_custom_call" | custom-call | flops 268435456 | bytes 2097152 | tf_op jit(solution)/shard_map/pallas_call | solution.py:165
  41.5 5.9 %collective-permute-done.19 = f32[128,128]{1,0:T(8,128)S(1)} collective-permute-done((f32[128,128]{1,0:T(8,128)S(1)}, f32[128,128]{1,0:T(8,128)S(1)}, u32[]{:S(2)}, u32[]{:S(2)}) %collective-permute-start.19) | collective-permute-done | bytes 65568 | tf_op jit(solution)/shard_map/ppermute | solution.py:17
  47.5 0.7 %pad_maximum_fusion = f32[128,384]{1,0:T(8,128)} fusion(f32[128,128]{1,0:T(8,128)S(1)} %add.7, f32[128,256]{1,0:T(8,128)S(1)} %add.6), kind=kLoop, calls=%fused_computation | loop fusion | flops 49152 | bytes 393216 | tf_op jit(solution)/shard_map/concatenate | solution.py:174
  (34 shorter events, 2.8 us)
Async XLA Ops:
  0.0 9.2 %collective-permute-start = (bf16[3,128,128]{2,1,0:T(8,128)(2,1)}, bf16[3,128,128]{2,1,0:T(8,128)(2,1)S(1)}, u32[]{:S(2)}, u32[]{:S(2)}) collective-permute-start(bf16[3,128,128]{2,1,0:T(8,128)(2,1)} %param.4), channel_id=1, source_target_pairs={{0,2},{1,3},{2,0},{3,1},{4,6},{5,7},{6,4},{7,5},{8,10},{9,11},{10,... | collective-permute-start | bytes 294920 | tf_op jit(solution)/shard_map/ppermute | solution.py:17
  4.0 1.3 %copy-start = (bf16[3,12,128,128]{3,2,1,0:T(8,128)(2,1)S(1)}, bf16[3,12,128,128]{3,2,1,0:T(8,128)(2,1)}, u32[]{:S(2)}) copy-start(bf16[3,12,128,128]{3,2,1,0:T(8,128)(2,1)} %whole.1) | copy-start | bytes 3538948
  5.6 29.8 %collective-permute-start.16 = (bf16[2,12,128,128]{3,2,1,0:T(8,128)(2,1)S(1)}, bf16[2,12,128,128]{3,2,1,0:T(8,128)(2,1)S(1)}, u32[]{:S(2)}, u32[]{:S(2)}) collective-permute-start(bf16[2,12,128,128]{3,2,1,0:T(8,128)(2,1)S(1)} %get-tuple-element.21), channel_id=1, source_target_pairs={{0,1},{1,0},{2,3},{3,2},{4,5},{5,4},{6,7},{7,6},{8,9},{9,8},{10,11... | collective-permute-start | bytes 2359304 | tf_op jit(solution)/shard_map/ppermute | solution.py:17
  9.3 5.7 %collective-permute-start.7 = (bf16[1,3,128,128]{3,2,1,0:T(8,128)(2,1)}, bf16[1,3,128,128]{3,2,1,0:T(8,128)(2,1)S(1)}, u32[]{:S(2)}, u32[]{:S(2)}) collective-permute-start(bf16[1,3,128,128]{3,2,1,0:T(8,128)(2,1)} %bitcast.4), channel_id=1, source_target_pairs={{0,24},{4,28},{8,16},{12,20},{16,8},{20,12},{24,0},{28,4},{1,25},{... | collective-permute-start | bytes 294920 | tf_op jit(solution)/shard_map/ppermute | solution.py:17
  11.8 5.8 %collective-permute-start.5 = (bf16[1,3,128,128]{3,2,1,0:T(8,128)(2,1)}, bf16[1,3,128,128]{3,2,1,0:T(8,128)(2,1)S(1)}, u32[]{:S(2)}, u32[]{:S(2)}) collective-permute-start(bf16[1,3,128,128]{3,2,1,0:T(8,128)(2,1)} %bitcast.5), channel_id=1, source_target_pairs={{0,16},{4,20},{8,24},{12,28},{16,0},{20,4},{24,8},{28,12},{1,17},{... | collective-permute-start | bytes 294920 | tf_op jit(solution)/shard_map/ppermute | solution.py:17
  12.3 5.8 %collective-permute-start.3 = (bf16[1,3,128,128]{3,2,1,0:T(8,128)(2,1)}, bf16[1,3,128,128]{3,2,1,0:T(8,128)(2,1)S(1)}, u32[]{:S(2)}, u32[]{:S(2)}) collective-permute-start(bf16[1,3,128,128]{3,2,1,0:T(8,128)(2,1)} %bitcast.6), channel_id=1, source_target_pairs={{0,8},{4,12},{8,0},{12,4},{16,24},{20,28},{24,16},{28,20},{1,9},{5... | collective-permute-start | bytes 294920 | tf_op jit(solution)/shard_map/ppermute | solution.py:17
  12.7 5.9 %collective-permute-start.2 = (bf16[1,3,128,128]{3,2,1,0:T(8,128)(2,1)}, bf16[1,3,128,128]{3,2,1,0:T(8,128)(2,1)S(1)}, u32[]{:S(2)}, u32[]{:S(2)}) collective-permute-start(bf16[1,3,128,128]{3,2,1,0:T(8,128)(2,1)} %bitcast.7), channel_id=1, source_target_pairs={{0,4},{4,0},{8,12},{12,8},{16,20},{20,16},{24,28},{28,24},{1,5},{5... | collective-permute-start | bytes 294920 | tf_op jit(solution)/shard_map/ppermute | solution.py:17
  15.0 6.5 %collective-permute-start.14 = (bf16[1,3,128,128]{3,2,1,0:T(8,128)(2,1)S(1)}, bf16[1,3,128,128]{3,2,1,0:T(8,128)(2,1)S(1)}, u32[]{:S(2)}, u32[]{:S(2)}) collective-permute-start(bf16[1,3,128,128]{3,2,1,0:T(8,128)(2,1)S(1)} %bitcast.9), channel_id=1, source_target_pairs={{0,24},{4,28},{8,16},{12,20},{16,8},{20,12},{24,0},{28,4},{1,25},{... | collective-permute-start | bytes 294920 | tf_op jit(solution)/shard_map/ppermute | solution.py:17
  17.6 4.8 %collective-permute-start.12 = (bf16[1,3,128,128]{3,2,1,0:T(8,128)(2,1)S(1)}, bf16[1,3,128,128]{3,2,1,0:T(8,128)(2,1)S(1)}, u32[]{:S(2)}, u32[]{:S(2)}) collective-permute-start(bf16[1,3,128,128]{3,2,1,0:T(8,128)(2,1)S(1)} %bitcast.10), channel_id=1, source_target_pairs={{0,16},{4,20},{8,24},{12,28},{16,0},{20,4},{24,8},{28,12},{1,17},{... | collective-permute-start | bytes 294920 | tf_op jit(solution)/shard_map/ppermute | solution.py:17
  18.0 4.6 %collective-permute-start.10 = (bf16[1,3,128,128]{3,2,1,0:T(8,128)(2,1)S(1)}, bf16[1,3,128,128]{3,2,1,0:T(8,128)(2,1)S(1)}, u32[]{:S(2)}, u32[]{:S(2)}) collective-permute-start(bf16[1,3,128,128]{3,2,1,0:T(8,128)(2,1)S(1)} %bitcast.11), channel_id=1, source_target_pairs={{0,8},{4,12},{8,0},{12,4},{16,24},{20,28},{24,16},{28,20},{1,9},{5... | collective-permute-start | bytes 294920 | tf_op jit(solution)/shard_map/ppermute | solution.py:17
  18.6 4.3 %collective-permute-start.9 = (bf16[1,3,128,128]{3,2,1,0:T(8,128)(2,1)S(1)}, bf16[1,3,128,128]{3,2,1,0:T(8,128)(2,1)S(1)}, u32[]{:S(2)}, u32[]{:S(2)}) collective-permute-start(bf16[1,3,128,128]{3,2,1,0:T(8,128)(2,1)S(1)} %bitcast.12), channel_id=1, source_target_pairs={{0,4},{4,0},{8,12},{12,8},{16,20},{20,16},{24,28},{28,24},{1,5},{5... | collective-permute-start | bytes 294920 | tf_op jit(solution)/shard_map/ppermute | solution.py:17
  21.5 1.7 %collective-permute-start.8 = (bf16[1,3,128,128]{3,2,1,0:T(8,128)(2,1)S(1)}, bf16[1,3,128,128]{3,2,1,0:T(8,128)(2,1)S(1)}, u32[]{:S(2)}, u32[]{:S(2)}) collective-permute-start(bf16[1,3,128,128]{3,2,1,0:T(8,128)(2,1)S(1)} %collective-permute-done.7.refs_9_), channel_id=1, source_target_pairs={{0,4},{4,0},{8,12},{12,8},{16,20},{20,16},{24,28},{28,24},{1,5},{5... | collective-permute-start | bytes 294920 | tf_op jit(solution)/shard_map/ppermute | solution.py:17
  22.4 1.3 %collective-permute-start.6 = (bf16[1,3,128,128]{3,2,1,0:T(8,128)(2,1)S(1)}, bf16[1,3,128,128]{3,2,1,0:T(8,128)(2,1)S(1)}, u32[]{:S(2)}, u32[]{:S(2)}) collective-permute-start(bf16[1,3,128,128]{3,2,1,0:T(8,128)(2,1)S(1)} %collective-permute-done.5.refs_7_), channel_id=1, source_target_pairs={{0,4},{4,0},{8,12},{12,8},{16,20},{20,16},{24,28},{28,24},{1,5},{5... | collective-permute-start | bytes 294920 | tf_op jit(solution)/shard_map/ppermute | solution.py:17
  22.7 1.3 %collective-permute-start.4 = (bf16[1,3,128,128]{3,2,1,0:T(8,128)(2,1)S(1)}, bf16[1,3,128,128]{3,2,1,0:T(8,128)(2,1)S(1)}, u32[]{:S(2)}, u32[]{:S(2)}) collective-permute-start(bf16[1,3,128,128]{3,2,1,0:T(8,128)(2,1)S(1)} %collective-permute-done.3.refs_5_), channel_id=1, source_target_pairs={{0,4},{4,0},{8,12},{12,8},{16,20},{20,16},{24,28},{28,24},{1,5},{5... | collective-permute-start | bytes 294920 | tf_op jit(solution)/shard_map/ppermute | solution.py:17
  22.9 2.7 %collective-permute-start.15 = (bf16[1,3,128,128]{3,2,1,0:T(8,128)(2,1)S(1)}, bf16[1,3,128,128]{3,2,1,0:T(8,128)(2,1)S(1)}, u32[]{:S(2)}, u32[]{:S(2)}) collective-permute-start(bf16[1,3,128,128]{3,2,1,0:T(8,128)(2,1)S(1)} %collective-permute-done.14.refs_17_), channel_id=1, source_target_pairs={{0,4},{4,0},{8,12},{12,8},{16,20},{20,16},{24,28},{28,24},{1,5},{5... | collective-permute-start | bytes 294920 | tf_op jit(solution)/shard_map/ppermute | solution.py:17
  23.2 2.8 %collective-permute-start.13 = (bf16[1,3,128,128]{3,2,1,0:T(8,128)(2,1)S(1)}, bf16[1,3,128,128]{3,2,1,0:T(8,128)(2,1)S(1)}, u32[]{:S(2)}, u32[]{:S(2)}) collective-permute-start(bf16[1,3,128,128]{3,2,1,0:T(8,128)(2,1)S(1)} %collective-permute-done.12.refs_15_), channel_id=1, source_target_pairs={{0,4},{4,0},{8,12},{12,8},{16,20},{20,16},{24,28},{28,24},{1,5},{5... | collective-permute-start | bytes 294920 | tf_op jit(solution)/shard_map/ppermute | solution.py:17
  23.7 2.3 %collective-permute-start.11 = (bf16[1,3,128,128]{3,2,1,0:T(8,128)(2,1)S(1)}, bf16[1,3,128,128]{3,2,1,0:T(8,128)(2,1)S(1)}, u32[]{:S(2)}, u32[]{:S(2)}) collective-permute-start(bf16[1,3,128,128]{3,2,1,0:T(8,128)(2,1)S(1)} %collective-permute-done.10.refs_13_), channel_id=1, source_target_pairs={{0,4},{4,0},{8,12},{12,8},{16,20},{20,16},{24,28},{28,24},{1,5},{5... | collective-permute-start | bytes 294920 | tf_op jit(solution)/shard_map/ppermute | solution.py:17
  24.0 16.6 %collective-permute-start.18 = (bf16[1,12,128,128]{3,2,1,0:T(8,128)(2,1)S(1)}, bf16[1,12,128,128]{3,2,1,0:T(8,128)(2,1)S(1)}, u32[]{:S(2)}, u32[]{:S(2)}) collective-permute-start(bf16[1,12,128,128]{3,2,1,0:T(8,128)(2,1)S(1)} %get-tuple-element.24), channel_id=1, source_target_pairs={{0,1},{1,0},{2,3},{3,2},{4,5},{5,4},{6,7},{7,6},{8,9},{9,8},{10,11... | collective-permute-start | bytes 1179656 | tf_op jit(solution)/shard_map/ppermute | solution.py:17
  25.6 9.8 %collective-permute-start.1 = (s32[3,12]{1,0:T(4,128)}, s32[3,12]{1,0:T(4,128)S(1)}, u32[]{:S(2)}, u32[]{:S(2)}) collective-permute-start(s32[3,12]{1,0:T(4,128)} %refs_1_.1), channel_id=1, source_target_pairs={{0,1},{1,0},{2,3},{3,2},{4,5},{5,4},{6,7},{7,6},{8,9},{9,8},{10,11... | collective-permute-start | bytes 440 | tf_op jit(solution)/shard_map/ppermute | solution.py:17
  26.0 1.3 %copy-start.1 = (bf16[3,12,128,128]{3,2,1,0:T(8,128)(2,1)S(1)}, bf16[3,12,128,128]{3,2,1,0:T(8,128)(2,1)}, u32[]{:S(2)}) copy-start(bf16[3,12,128,128]{3,2,1,0:T(8,128)(2,1)} %whole.1) | copy-start | bytes 3538948
  27.9 0.9 %copy-start.3 = (bf16[3,128,128]{2,1,0:T(8,128)(2,1)S(1)}, bf16[3,128,128]{2,1,0:T(8,128)(2,1)}, u32[]{:S(2)}) copy-start(bf16[3,128,128]{2,1,0:T(8,128)(2,1)} %param.4) | copy-start | bytes 294916
  28.8 0.7 %copy-start.4 = (s32[3,12]{1,0:T(4,128)S(1)}, s32[3,12]{1,0:T(4,128)}, u32[]{:S(2)}) copy-start(s32[3,12]{1,0:T(4,128)} %refs_1_.1) | copy-start | bytes 436
  37.4 10.0 %collective-permute-start.17 = (f32[128,256]{1,0:T(8,128)S(1)}, f32[128,256]{1,0:T(8,128)S(1)}, u32[]{:S(2)}, u32[]{:S(2)}) collective-permute-start(f32[128,256]{1,0:T(8,128)S(1)} %get-tuple-element.23), channel_id=1, source_target_pairs={{0,2},{1,3},{2,0},{3,1},{4,6},{5,7},{6,4},{7,5},{8,10},{9,11},{10,... | collective-permute-start | bytes 393224 | tf_op jit(solution)/shard_map/ppermute | solution.py:17
  41.4 6.0 %collective-permute-start.19 = (f32[128,128]{1,0:T(8,128)S(1)}, f32[128,128]{1,0:T(8,128)S(1)}, u32[]{:S(2)}, u32[]{:S(2)}) collective-permute-start(f32[128,128]{1,0:T(8,128)S(1)} %get-tuple-element.26), channel_id=1, source_target_pairs={{0,2},{1,3},{2,0},{3,1},{4,6},{5,7},{6,4},{7,5},{8,10},{9,11},{10,... | collective-permute-start | bytes 196616 | tf_op jit(solution)/shard_map/ppermute | solution.py:17
  (1 other events, 0.7 us)

commit v3 on v2

v3 whole, which is shorter than its diff:
```python
import jax
import jax.numpy as jnp
from jax import lax
from jax.experimental import pallas as pl
from jax.experimental.pallas import tpu as pltpu
from jax.sharding import PartitionSpec as P

VMEM_BYTES = 48 * 1024 * 1024
UNROLL = 4
OWN_FLOPS = 4000000000
HEAD_FLOPS = 250000000
TABLE_ROWS = 16
SMEM = pl.BlockSpec(memory_space=pltpu.SMEM)
VMEM = pl.BlockSpec(memory_space=pltpu.VMEM)
ANY = pl.BlockSpec(memory_space=pl.ANY)
HBM = pl.BlockSpec(memory_space=pltpu.HBM)


def shift(value, axis, size, mask):
    return lax.ppermute(value, axis, [(j, j ^ mask) for j in range(size)])


def contract(total, lists_ref, a, live, slots, stage, blocks_of):
    blocks, _, rows, depth = stage.shape
    dims = (((1,), (1,)), ((), ()))

    def pair(s):
        sides, weights = [], []
        for slot in (s, s + 1):
            safe = jnp.minimum(slot, slots - 1)
            block = blocks_of(safe)
            sides.append(stage[:, lists_ref[a, safe]].reshape(blocks * rows, depth))
            weights.append(jnp.where(slot < live, block, jnp.zeros_like(block)))
        return lax.dot_general(
            jnp.concatenate(sides, axis=1), jnp.concatenate(weights, axis=1), dims, preferred_element_type=jnp.float32
        )

    def step(group, total):
        for offset in range(0, UNROLL, 2):
            total = total + pair(UNROLL * group + offset)
        return total

    return lax.fori_loop(0, (live + UNROLL - 1) // UNROLL, step, total)


def gather_pieces(place_ref, pieces, layout, stage, sems):
    copies = []
    for n, (mask, first) in enumerate(layout):
        piece = pieces[n]
        base = (place_ref[0] ^ mask) * piece.shape[1]
        copy = pltpu.make_async_copy(
            piece, stage.at[pl.ds(first, piece.shape[0]), pl.ds(base, piece.shape[1])], sems.at[n]
        )
        copy.start()
        copies.append(copy)
    for copy in copies:
        copy.wait()


def plain_kernel(lists_ref, live_ref, place_ref, piece, integrals_ref, out_ref, stage, sems):
    gather_pieces(place_ref, [piece], [(0, 0)], stage, sems)
    tile_dev, _, width, _ = integrals_ref.shape
    blocks, _, rows, _ = stage.shape
    for a in range(tile_dev):
        zero = jnp.zeros((blocks * rows, width), jnp.float32)
        total = contract(zero, lists_ref, a, live_ref[a], lists_ref.shape[1], stage, lambda s, a=a: integrals_ref[a, s])
        for k in range(blocks):
            out_ref[k, :, a * width:(a + 1) * width] = total[k * rows:(k + 1) * rows]


def plain_partials(lists, live, everything, integrals):
    blocks, tiles, rows, depth = everything.shape
    tile_dev, _, width, _ = integrals.shape
    return pl.pallas_call(
        plain_kernel,
        out_shape=jax.ShapeDtypeStruct((blocks, rows, tile_dev * width), jnp.float32),
        in_specs=[SMEM] * 3 + [ANY, VMEM],
        out_specs=VMEM,
        scratch_shapes=[pltpu.VMEM((blocks, tiles, rows, depth), everything.dtype), pltpu.SemaphoreType.DMA((1,))],
        compiler_params=pltpu.CompilerParams(vmem_limit_bytes=VMEM_BYTES),
    )(lists, live, jnp.zeros((1,), jnp.int32), everything, integrals)


def cut_kernel(whole, amplitudes, lists, counts, head, tail, amplitudes_out, table, lists_v, counts_s, sems):
    tile_dev, slots = lists_v.shape
    ready = head.shape[0] // slots
    small = [pltpu.make_async_copy(lists, lists_v, sems.at[0]), pltpu.make_async_copy(counts, counts_s, sems.at[1])]
    targets = [head.at[pl.ds(n * slots, slots)] for n in range(ready)]
    targets += [tail.at[pl.ds(n * slots, slots)] for n in range(tile_dev - ready)]
    large = [pltpu.make_async_copy(whole.at[a], target, sems.at[2 + a]) for a, target in enumerate(targets)]
    large.append(pltpu.make_async_copy(amplitudes, amplitudes_out, sems.at[2 + tile_dev]))
    for copy in small + large:
        copy.start()
    head[ready * slots] = jnp.zeros(head.shape[1:], head.dtype)
    for copy in small:
        copy.wait()
    lane = lax.broadcasted_iota(jnp.int32, table.shape, 1)
    values = jnp.zeros(table.shape, jnp.int32)
    for a in range(tile_dev):
        values = jnp.where(lane == a, counts_s[a], values)
    table[...] = values
    table[:tile_dev, :slots] = lists_v[...]
    head[ready * slots, :TABLE_ROWS] = table[...].astype(jnp.float32).astype(head.dtype)
    for copy in large:
        copy.wait()


def cut(whole, amplitudes, lists, counts, ready):
    tile_dev, slots = lists.shape
    sizes = (ready * slots + 1, (tile_dev - ready) * slots)
    placed = [pltpu.with_memory_space_constraint(x, pltpu.HBM) for x in (whole, amplitudes, lists, counts)]
    return pl.pallas_call(
        cut_kernel,
        out_shape=tuple(jax.ShapeDtypeStruct((n,) + whole.shape[2:], whole.dtype) for n in sizes)
        + (
            jax.ShapeDtypeStruct(amplitudes.shape, amplitudes.dtype),
            jax.ShapeDtypeStruct((TABLE_ROWS, whole.shape[3]), jnp.int32),
        ),
        in_specs=[HBM] * 4,
        out_specs=(VMEM,) * 4,
        scratch_shapes=[
            pltpu.VMEM(lists.shape, lists.dtype),
            pltpu.SMEM(counts.shape, counts.dtype),
            pltpu.SemaphoreType.DMA((3 + tile_dev,)),
        ],
        compiler_params=pltpu.CompilerParams(vmem_limit_bytes=VMEM_BYTES),
    )(*placed)


def live_slots(table_ref, a, group, slots):
    return jnp.clip(table_ref[TABLE_ROWS - 1, a] - group * slots, 0, slots)


def own_kernel(layout, slots, place_ref, table_v, *refs):
    count = len(layout)
    pieces, (head, tail, sums_ref, stage, table, sem) = refs[:count], refs[count:]
    ready = head.shape[0] // slots
    blocks, _, rows, _ = stage.shape
    tile_dev, _, width = sums_ref.shape
    copy = pltpu.make_async_copy(table_v, table, sem)
    copy.start()
    for piece, (mask, first) in zip(pieces, layout):
        tiles = piece.shape[0]
        stage[first, pl.ds((place_ref[0] ^ mask) * tiles, tiles)] = piece[...]
    copy.wait()
    for a in range(tile_dev):
        part, base = (head, a * slots) if a < ready else (tail, (a - ready) * slots)
        total = jnp.zeros((blocks * rows, width), jnp.float32)
        live = live_slots(table, a, place_ref[1], slots)
        blocks_of = lambda s, part=part, base=base: part[base + s]
        sums_ref[a] = contract(total, table, a, live, slots, stage, blocks_of)


def add_other(tiles, slots, table, place_ref, stage, sums_ref, others, own_ref, far_ref):
    rows, width = own_ref.shape[0], sums_ref.shape[2]
    for n, a in enumerate(tiles):
        live = live_slots(table, a, place_ref[1] ^ 1, slots)
        blocks_of = lambda s, n=n: others[n * slots + s]
        total = contract(sums_ref[a], table, a, live, slots, stage, blocks_of)
        own_ref[:, n * width:(n + 1) * width] = total[:rows]
        far_ref[:, n * width:(n + 1) * width] = total[rows:]


def head_kernel(tiles, slots, place_ref, stage, sums_ref, others, own_ref, far_ref, table_v, table, sem):
    table_v[...] = others[len(tiles) * slots, :TABLE_ROWS].astype(jnp.float32).astype(jnp.int32)
    copy = pltpu.make_async_copy(table_v, table, sem)
    copy.start()
    copy.wait()
    add_other(tiles, slots, table, place_ref, stage, sums_ref, others, own_ref, far_ref)


def tail_kernel(tiles, slots, place_ref, table_v, stage, sums_ref, others, own_ref, far_ref, table, sem):
    copy = pltpu.make_async_copy(table_v, table, sem)
    copy.start()
    copy.wait()
    add_other(tiles, slots, table, place_ref, stage, sums_ref, others, own_ref, far_ref)


def on_pairs(amplitudes, tile_counts, tile_lists, integrals, n_vv, n_oo):
    tile_dev, slots, width, depth = integrals.shape
    rows = amplitudes.shape[1]
    tiles = n_vv * tile_dev
    ready = tile_dev - 1
    place = jnp.stack([lax.axis_index("vv"), lax.axis_index("oo")]).astype(jnp.int32)

    far = shift(amplitudes, "oo", n_oo, 2)
    head, tail, amplitudes, table = cut(integrals, amplitudes, tile_lists, tile_counts, ready)
    head_other, tail_other = shift(head, "oo", n_oo, 1), shift(tail, "oo", n_oo, 1)
    far, amplitudes = lax.optimization_barrier((far, amplitudes))
    pieces, layout = [], []
    for first, block in enumerate((amplitudes, far)):
        for mask in (0, 2, 4, 6):
            piece = shift(block, "vv", n_vv, mask) if mask else block
            pieces += [piece, shift(piece, "vv", n_vv, 1)]
            layout += [(mask, first), (mask ^ 1, first)]
    params = pltpu.CompilerParams(vmem_limit_bytes=VMEM_BYTES)
    table_type = jax.ShapeDtypeStruct(table.shape, table.dtype)
    scratch = [pltpu.SMEM(table.shape, table.dtype), pltpu.SemaphoreType.DMA]
    sums, stage = pl.pallas_call(
        lambda *refs: own_kernel(layout, slots, *refs),
        out_shape=(
            jax.ShapeDtypeStruct((tile_dev, 2 * rows, width), jnp.float32),
            jax.ShapeDtypeStruct((2, tiles, rows, depth), amplitudes.dtype),
        ),
        in_specs=[SMEM] + [VMEM] * (len(pieces) + 3),
        out_specs=(VMEM,) * 2,
        scratch_shapes=scratch,
        compiler_params=params,
        cost_estimate=pl.CostEstimate(flops=OWN_FLOPS, bytes_accessed=2**22, transcendentals=0),
    )(place, table, *pieces, head, tail)

    def part(count):
        return jax.ShapeDtypeStruct((rows, count * width), jnp.float32)

    own_head, far_head, table = pl.pallas_call(
        lambda *refs: head_kernel(range(ready), slots, *refs),
        out_shape=(part(ready), part(ready), table_type),
        in_specs=[SMEM] + [VMEM] * 3,
        out_specs=(VMEM,) * 3,
        scratch_shapes=scratch,
        compiler_params=params,
        cost_estimate=pl.CostEstimate(flops=HEAD_FLOPS, bytes_accessed=2**21, transcendentals=0),
    )(place, stage, sums, head_other)
    own_tail, far_tail = pl.pallas_call(
        lambda *refs: tail_kernel(range(ready, tile_dev), slots, *refs),
        out_shape=(part(tile_dev - ready),) * 2,
        in_specs=[SMEM] + [VMEM] * 4,
        out_specs=(VMEM,) * 2,
        scratch_shapes=scratch,
        compiler_params=params,
        cost_estimate=pl.CostEstimate(flops=2**28, bytes_accessed=2**21, transcendentals=0),
    )(place, table, stage, sums, tail_other)
    left = own_head + shift(far_head, "oo", n_oo, 2)
    right = own_tail + shift(far_tail, "oo", n_oo, 2)
    return jnp.concatenate([left, right], axis=1)


def on_device(amplitudes, tile_counts, tile_lists, integrals, n_vv, n_oo):
    if (n_vv, n_oo) == (8, 4):
        return on_pairs(amplitudes, tile_counts, tile_lists, integrals, n_vv, n_oo)
    slots = tile_lists.shape[1]
    live = jnp.clip(tile_counts - lax.axis_index("oo") * slots, 0, slots)
    rows = lax.all_gather(amplitudes, "oo", axis=0, tiled=False)
    everything = lax.all_gather(rows, "vv", axis=1, tiled=True)
    parts = plain_partials(tile_lists, live, everything, integrals)
    return lax.psum_scatter(parts.reshape(-1, parts.shape[2]), "oo", scatter_dimension=0, tiled=True)


def solution(mesh):
    n_vv, n_oo = mesh.shape["vv"], mesh.shape["oo"]
    placed = (P("vv", "oo", None), P("vv"), P("vv", "oo"), P("vv", "oo", None, None))
    return jax.shard_map(
        lambda *args: on_device(*args, n_vv, n_oo),
        mesh=mesh, in_specs=placed, out_specs=P("oo", "vv"), check_vma=False,
    )
```

time: 49 us -> 46.1 us (0.941)
  local copies, waits for them, and re-layouts: 4.77 us -> 0 us
  waiting for transfers between devices: 15.3 us -> 16.8 us
  starting transfers between devices: 19 us -> 19.9 us
  Pallas kernels: 8.31 us -> 7.76 us
    unnamed x10 -> x0, local copies, waits for them, and re-layouts: 4.77 us -> none
    pallas_call x3, Pallas kernels: 8.05 us -> 6.45 us  [the longest x1 3.22 us: on_pairs(): pl.pallas_call(lambda *refs: own_kernel(layout, slots, *refs), out_shape=...]
    ppermute x20 -> x19, waiting for transfers between devices: 15.3 us -> 16.8 us  [shift(): return lax.ppermute(value, axis, [(j, j ^ mask) for j in range(size)])]
    pallas_call x1, Pallas kernels: 0.26 us -> 1.31 us  [cut(): pl.pallas_call(cut_kernel, out_shape=tuple((jax.ShapeDtypeStruct((n,) + w...]
    ppermute x20 -> x19, starting transfers between devices: 19 us -> 19.9 us  [shift(): return lax.ppermute(value, axis, [(j, j ^ mask) for j in range(size)])]
  transfers between devices with their start and end apart: 20 -> 19, of which waited for: 8 -> 8; matrix products, arithmetic and copies ran while one was open for 0% -> 0% of each run, Pallas kernels for 17% -> 17%
where the time goes in v3:
time: 46.1 us; the launch traced here: 45.4 us
  starting transfers between devices  19.9 us (43%)
  waiting for transfers between devices  16.8 us (36%)
  Pallas kernels  7.76 us (17%)
  other arithmetic  0.8 us (2%)
    ppermute x19, starting transfers between devices, shift(): return lax.ppermute(value, axis, [(j, j ^ mask) for j in range(size)])  19.9 us
    ppermute x19, waiting for transfers between devices, shift(): return lax.ppermute(value, axis, [(j, j ^ mask) for j in range(size)])  16.8 us
    pallas_call x1, Pallas kernels, on_pairs(): pl.pallas_call(lambda *refs: own_kernel(layout, slots, *refs), out_shape=...  3.22 us
    pallas_call x1, Pallas kernels, on_pairs(): pl.pallas_call(lambda *refs: head_kernel(range(ready), slots, *refs), out...  1.99 us
    pallas_call x1, Pallas kernels, cut(): pl.pallas_call(cut_kernel, out_shape=tuple((jax.ShapeDtypeStruct((n,) + w...  1.31 us
    pallas_call x1, Pallas kernels, on_pairs(): pl.pallas_call(lambda *refs: tail_kernel(range(ready, tile_dev), slots, *...  1.24 us
  transfers between devices with their start and end apart: 19, of which 8 were waited for; matrix products, arithmetic and copies ran while one was open for 0% of the time, Pallas kernels for 17%

profile of v3, /device:TPU:0, one launch (start us, length us, event | category | flops | bytes accessed | tf_op | source)
XLA Modules:
  0.0 45.4 jit_solution(10226142818982902024)
XLA Ops:
  0.0 4.0 %collective-permute-start = (bf16[3,128,128]{2,1,0:T(8,128)(2,1)}, bf16[3,128,128]{2,1,0:T(8,128)(2,1)S(1)}, u32[]{:S(2)}, u32[]{:S(2)}) collective-permute-start(bf16[3,128,128]{2,1,0:T(8,128)(2,1)} %amplitudes.1), channel_id=1, source_target_pairs={{0,2},{1,3},{2,0},{3,1},{4,6},{5,7},{6,4},{7,5},{8,10},{9,11},{10,... | collective-permute-start | bytes 294920 | tf_op jit(solution)/shard_map/ppermute | solution.py:20
  4.0 1.3 %shard_map.46 = (bf16[25,128,128]{2,1,0:T(8,128)(2,1)S(1)}, bf16[12,128,128]{2,1,0:T(8,128)(2,1)S(1)}, bf16[3,128,128]{2,1,0:T(8,128)(2,1)S(1)}, s32[16,128]{1,0:T(8,128)S(1)}) custom-call(bf16[3,12,128,128]{3,2,1,0:T(8,128)(2,1)} %whole.1, bf16[3,128,128]{2,1,0:T(8,128)(2,1)} %amplitudes.1, s32[3,12]{1,0:T(4,128)} %lists.1, s32[3]{0:T(128)} %counts.1), custom_call_target="tpu_custom_call" | custom-call | tf_op jit(solution)/shard_map/pallas_call | solution.py:112
  5.4 1.6 %collective-permute-start.15 = (bf16[25,128,128]{2,1,0:T(8,128)(2,1)S(1)}, bf16[25,128,128]{2,1,0:T(8,128)(2,1)S(1)}, u32[]{:S(2)}, u32[]{:S(2)}) collective-permute-start(bf16[25,128,128]{2,1,0:T(8,128)(2,1)S(1)} %get-tuple-element.22.refs_18_), channel_id=1, source_target_pairs={{0,1},{1,0},{2,3},{3,2},{4,5},{5,4},{6,7},{7,6},{8,9},{9,8},{10,11... | collective-permute-start | bytes 2457608 | tf_op jit(solution)/shard_map/ppermute | solution.py:20
  7.0 2.2 %collective-permute-done.refs_10_ = bf16[3,128,128]{2,1,0:T(8,128)(2,1)S(1)} collective-permute-done((bf16[3,128,128]{2,1,0:T(8,128)(2,1)}, bf16[3,128,128]{2,1,0:T(8,128)(2,1)S(1)}, u32[]{:S(2)}, u32[]{:S(2)}) %collective-permute-start) | collective-permute-done | bytes 98336 | tf_op jit(solution)/shard_map/ppermute | solution.py:20
  9.3 2.5 %collective-permute-start.6 = (bf16[3,128,128]{2,1,0:T(8,128)(2,1)S(1)}, bf16[3,128,128]{2,1,0:T(8,128)(2,1)S(1)}, u32[]{:S(2)}, u32[]{:S(2)}) collective-permute-start(bf16[3,128,128]{2,1,0:T(8,128)(2,1)S(1)} %get-tuple-element.20.refs_2_), channel_id=1, source_target_pairs={{0,24},{4,28},{8,16},{12,20},{16,8},{20,12},{24,0},{28,4},{1,25},{... | collective-permute-start | bytes 294920 | tf_op jit(solution)/shard_map/ppermute | solution.py:20
  11.8 0.5 %collective-permute-start.4 = (bf16[3,128,128]{2,1,0:T(8,128)(2,1)S(1)}, bf16[3,128,128]{2,1,0:T(8,128)(2,1)S(1)}, u32[]{:S(2)}, u32[]{:S(2)}) collective-permute-start(bf16[3,128,128]{2,1,0:T(8,128)(2,1)S(1)} %get-tuple-element.20.refs_2_), channel_id=1, source_target_pairs={{0,16},{4,20},{8,24},{12,28},{16,0},{20,4},{24,8},{28,12},{1,17},{... | collective-permute-start | bytes 294920 | tf_op jit(solution)/shard_map/ppermute | solution.py:20
  12.3 0.5 %collective-permute-start.2 = (bf16[3,128,128]{2,1,0:T(8,128)(2,1)S(1)}, bf16[3,128,128]{2,1,0:T(8,128)(2,1)S(1)}, u32[]{:S(2)}, u32[]{:S(2)}) collective-permute-start(bf16[3,128,128]{2,1,0:T(8,128)(2,1)S(1)} %get-tuple-element.20.refs_2_), channel_id=1, source_target_pairs={{0,8},{4,12},{8,0},{12,4},{16,24},{20,28},{24,16},{28,20},{1,9},{5... | collective-permute-start | bytes 294920 | tf_op jit(solution)/shard_map/ppermute | solution.py:20
  12.7 2.0 %collective-permute-done.6.refs_8_ = bf16[3,128,128]{2,1,0:T(8,128)(2,1)S(1)} collective-permute-done((bf16[3,128,128]{2,1,0:T(8,128)(2,1)S(1)}, bf16[3,128,128]{2,1,0:T(8,128)(2,1)S(1)}, u32[]{:S(2)}, u32[]{:S(2)}) %collective-permute-start.6) | collective-permute-done | bytes 98336 | tf_op jit(solution)/shard_map/ppermute | solution.py:20
  14.8 2.6 %collective-permute-start.13 = (bf16[3,128,128]{2,1,0:T(8,128)(2,1)S(1)}, bf16[3,128,128]{2,1,0:T(8,128)(2,1)S(1)}, u32[]{:S(2)}, u32[]{:S(2)}) collective-permute-start(bf16[3,128,128]{2,1,0:T(8,128)(2,1)S(1)} %collective-permute-done.refs_10_), channel_id=1, source_target_pairs={{0,24},{4,28},{8,16},{12,20},{16,8},{20,12},{24,0},{28,4},{1,25},{... | collective-permute-start | bytes 294920 | tf_op jit(solution)/shard_map/ppermute | solution.py:20
  17.4 0.5 collective-permute-start.11
  17.8 0.6 %collective-permute-start.9 = (bf16[3,128,128]{2,1,0:T(8,128)(2,1)S(1)}, bf16[3,128,128]{2,1,0:T(8,128)(2,1)S(1)}, u32[]{:S(2)}, u32[]{:S(2)}) collective-permute-start(bf16[3,128,128]{2,1,0:T(8,128)(2,1)S(1)} %collective-permute-done.refs_10_), channel_id=1, source_target_pairs={{0,8},{4,12},{8,0},{12,4},{16,24},{20,28},{24,16},{28,20},{1,9},{5... | collective-permute-start | bytes 294920 | tf_op jit(solution)/shard_map/ppermute | solution.py:20
  18.4 2.9 %collective-permute-done.13.refs_16_ = bf16[3,128,128]{2,1,0:T(8,128)(2,1)S(1)} collective-permute-done((bf16[3,128,128]{2,1,0:T(8,128)(2,1)S(1)}, bf16[3,128,128]{2,1,0:T(8,128)(2,1)S(1)}, u32[]{:S(2)}, u32[]{:S(2)}) %collective-permute-start.13) | collective-permute-done | bytes 98336 | tf_op jit(solution)/shard_map/ppermute | solution.py:20
  21.3 0.9 %collective-permute-done.11.refs_14_ = bf16[3,128,128]{2,1,0:T(8,128)(2,1)S(1)} collective-permute-done((bf16[3,128,128]{2,1,0:T(8,128)(2,1)S(1)}, bf16[3,128,128]{2,1,0:T(8,128)(2,1)S(1)}, u32[]{:S(2)}, u32[]{:S(2)}) %collective-permute-start.11) | collective-permute-done | bytes 98336 | tf_op jit(solution)/shard_map/ppermute | solution.py:20
  22.7 0.3 collective-permute-start.14
  23.2 0.3 collective-permute-done.5.refs_7_
  23.8 1.6 %collective-permute-start.17 = (bf16[12,128,128]{2,1,0:T(8,128)(2,1)S(1)}, bf16[12,128,128]{2,1,0:T(8,128)(2,1)S(1)}, u32[]{:S(2)}, u32[]{:S(2)}) collective-permute-start(bf16[12,128,128]{2,1,0:T(8,128)(2,1)S(1)} %get-tuple-element.23.refs_19_), channel_id=1, source_target_pairs={{0,1},{1,0},{2,3},{3,2},{4,5},{5,4},{6,7},{7,6},{8,9},{9,8},{10,11... | collective-permute-start | bytes 1179656 | tf_op jit(solution)/shard_map/ppermute | solution.py:20
  25.4 3.2 %shard_map.47 = (f32[3,256,128]{2,1,0:T(8,128)S(1)}, bf16[2,24,128,128]{3,2,1,0:T(8,128)(2,1)S(1)}) custom-call(s32[2]{0:T(128)S(1)} %pad_add_fusion.refs_0_, s32[16,128]{1,0:T(8,128)S(1)} %get-tuple-element.18.refs_1_, bf16[3,128,128]{2,1,0:T(8,128)(2,1)S(1)} %get-tuple-element.20.refs_2_, bf16[3,128,128]{2,1,0:T(8,128)(2,1)S(1)} %collective-permute-done.1.refs_3_, ...), custom_call_target="tpu_custom_call" | custom-call | flops 4000000000 | bytes 4194304 | tf_op jit(solution)/shard_map/pallas_call | solution.py:199
  28.6 2.0 %shard_map.48 = (f32[128,256]{1,0:T(8,128)S(1)}, f32[128,256]{1,0:T(8,128)S(1)}, s32[16,128]{1,0:T(8,128)S(1)}) custom-call(s32[2]{0:T(128)S(1)} %pad_add_fusion.refs_0_, bf16[2,24,128,128]{3,2,1,0:T(8,128)(2,1)S(1)} %get-tuple-element.24.refs_1_.refs_2_, f32[3,256,128]{2,1,0:T(8,128)S(1)} %get-tuple-element.25.refs_2_.refs_3_, ...), custom_call_target="tpu_custom_call" | custom-call | flops 250000000 | bytes 2097152 | tf_op jit(solution)/shard_map/pallas_call | solution.py:215
  30.6 2.2 %collective-permute-start.16 = (f32[128,256]{1,0:T(8,128)S(1)}, f32[128,256]{1,0:T(8,128)S(1)}, u32[]{:S(2)}, u32[]{:S(2)}) collective-permute-start(f32[128,256]{1,0:T(8,128)S(1)} %get-tuple-element.27), channel_id=1, source_target_pairs={{0,2},{1,3},{2,0},{3,1},{4,6},{5,7},{6,4},{7,5},{8,10},{9,11},{10,... | collective-permute-start | bytes 393224 | tf_op jit(solution)/shard_map/ppermute | solution.py:20
  32.8 5.1 %collective-permute-done.17.refs_4_ = bf16[12,128,128]{2,1,0:T(8,128)(2,1)S(1)} collective-permute-done((bf16[12,128,128]{2,1,0:T(8,128)(2,1)S(1)}, bf16[12,128,128]{2,1,0:T(8,128)(2,1)S(1)}, u32[]{:S(2)}, u32[]{:S(2)}) %collective-permute-start.17) | collective-permute-done | bytes 393248 | tf_op jit(solution)/shard_map/ppermute | solution.py:20
  37.9 1.2 %shard_map.49 = (f32[128,128]{1,0:T(8,128)S(1)}, f32[128,128]{1,0:T(8,128)S(1)}) custom-call(s32[2]{0:T(128)S(1)} %pad_add_fusion.refs_0_, s32[16,128]{1,0:T(8,128)S(1)} %get-tuple-element.28.refs_1_, bf16[2,24,128,128]{3,2,1,0:T(8,128)(2,1)S(1)} %get-tuple-element.24.refs_1_.refs_2_, f32[3,256,128]{2,1,0:T(8,128)S(1)} %get-tuple-element.25.refs_2_.refs_3_, ...), custom_call_target="tpu_custom_call" | custom-call | flops 268435456 | bytes 2097152 | tf_op jit(solution)/shard_map/pallas_call | solution.py:224
  39.1 2.4 %collective-permute-start.18 = (f32[128,128]{1,0:T(8,128)S(1)}, f32[128,128]{1,0:T(8,128)S(1)}, u32[]{:S(2)}, u32[]{:S(2)}) collective-permute-start(f32[128,128]{1,0:T(8,128)S(1)} %get-tuple-element.30), channel_id=1, source_target_pairs={{0,2},{1,3},{2,0},{3,1},{4,6},{5,7},{6,4},{7,5},{8,10},{9,11},{10,... | collective-permute-start | bytes 196616 | tf_op jit(solution)/shard_map/ppermute | solution.py:20
  41.6 3.1 %collective-permute-done.18 = f32[128,128]{1,0:T(8,128)S(1)} collective-permute-done((f32[128,128]{1,0:T(8,128)S(1)}, f32[128,128]{1,0:T(8,128)S(1)}, u32[]{:S(2)}, u32[]{:S(2)}) %collective-permute-start.18) | collective-permute-done | bytes 65568 | tf_op jit(solution)/shard_map/ppermute | solution.py:20
  44.7 0.7 %pad_maximum_fusion = f32[128,384]{1,0:T(8,128)} fusion(f32[128,128]{1,0:T(8,128)S(1)} %add.7, f32[128,256]{1,0:T(8,128)S(1)} %add.6), kind=kLoop, calls=%fused_computation | loop fusion | flops 49152 | bytes 393216 | tf_op jit(solution)/shard_map/concatenate | solution.py:235
  (22 shorter events, 1.1 us)
Async XLA Ops:
  0.0 9.3 %collective-permute-start = (bf16[3,128,128]{2,1,0:T(8,128)(2,1)}, bf16[3,128,128]{2,1,0:T(8,128)(2,1)S(1)}, u32[]{:S(2)}, u32[]{:S(2)}) collective-permute-start(bf16[3,128,128]{2,1,0:T(8,128)(2,1)} %amplitudes.1), channel_id=1, source_target_pairs={{0,2},{1,3},{2,0},{3,1},{4,6},{5,7},{6,4},{7,5},{8,10},{9,11},{10,... | collective-permute-start | bytes 294920 | tf_op jit(solution)/shard_map/ppermute | solution.py:20
  5.4 23.2 %collective-permute-start.15 = (bf16[25,128,128]{2,1,0:T(8,128)(2,1)S(1)}, bf16[25,128,128]{2,1,0:T(8,128)(2,1)S(1)}, u32[]{:S(2)}, u32[]{:S(2)}) collective-permute-start(bf16[25,128,128]{2,1,0:T(8,128)(2,1)S(1)} %get-tuple-element.22.refs_18_), channel_id=1, source_target_pairs={{0,1},{1,0},{2,3},{3,2},{4,5},{5,4},{6,7},{7,6},{8,9},{9,8},{10,11... | collective-permute-start | bytes 2457608 | tf_op jit(solution)/shard_map/ppermute | solution.py:20
  9.3 5.5 %collective-permute-start.6 = (bf16[3,128,128]{2,1,0:T(8,128)(2,1)S(1)}, bf16[3,128,128]{2,1,0:T(8,128)(2,1)S(1)}, u32[]{:S(2)}, u32[]{:S(2)}) collective-permute-start(bf16[3,128,128]{2,1,0:T(8,128)(2,1)S(1)} %get-tuple-element.20.refs_2_), channel_id=1, source_target_pairs={{0,24},{4,28},{8,16},{12,20},{16,8},{20,12},{24,0},{28,4},{1,25},{... | collective-permute-start | bytes 294920 | tf_op jit(solution)/shard_map/ppermute | solution.py:20
  11.8 5.6 %collective-permute-start.4 = (bf16[3,128,128]{2,1,0:T(8,128)(2,1)S(1)}, bf16[3,128,128]{2,1,0:T(8,128)(2,1)S(1)}, u32[]{:S(2)}, u32[]{:S(2)}) collective-permute-start(bf16[3,128,128]{2,1,0:T(8,128)(2,1)S(1)} %get-tuple-element.20.refs_2_), channel_id=1, source_target_pairs={{0,16},{4,20},{8,24},{12,28},{16,0},{20,4},{24,8},{28,12},{1,17},{... | collective-permute-start | bytes 294920 | tf_op jit(solution)/shard_map/ppermute | solution.py:20
  12.3 5.6 %collective-permute-start.2 = (bf16[3,128,128]{2,1,0:T(8,128)(2,1)S(1)}, bf16[3,128,128]{2,1,0:T(8,128)(2,1)S(1)}, u32[]{:S(2)}, u32[]{:S(2)}) collective-permute-start(bf16[3,128,128]{2,1,0:T(8,128)(2,1)S(1)} %get-tuple-element.20.refs_2_), channel_id=1, source_target_pairs={{0,8},{4,12},{8,0},{12,4},{16,24},{20,28},{24,16},{28,20},{1,9},{5... | collective-permute-start | bytes 294920 | tf_op jit(solution)/shard_map/ppermute | solution.py:20
  12.7 5.7 %collective-permute-start.1 = (bf16[3,128,128]{2,1,0:T(8,128)(2,1)S(1)}, bf16[3,128,128]{2,1,0:T(8,128)(2,1)S(1)}, u32[]{:S(2)}, u32[]{:S(2)}) collective-permute-start(bf16[3,128,128]{2,1,0:T(8,128)(2,1)S(1)} %get-tuple-element.20.refs_2_), channel_id=1, source_target_pairs={{0,4},{4,0},{8,12},{12,8},{16,20},{20,16},{24,28},{28,24},{1,5},{5... | collective-permute-start | bytes 294920 | tf_op jit(solution)/shard_map/ppermute | solution.py:20
  14.8 6.5 %collective-permute-start.13 = (bf16[3,128,128]{2,1,0:T(8,128)(2,1)S(1)}, bf16[3,128,128]{2,1,0:T(8,128)(2,1)S(1)}, u32[]{:S(2)}, u32[]{:S(2)}) collective-permute-start(bf16[3,128,128]{2,1,0:T(8,128)(2,1)S(1)} %collective-permute-done.refs_10_), channel_id=1, source_target_pairs={{0,24},{4,28},{8,16},{12,20},{16,8},{20,12},{24,0},{28,4},{1,25},{... | collective-permute-start | bytes 294920 | tf_op jit(solution)/shard_map/ppermute | solution.py:20
  17.4 4.8 %collective-permute-start.11 = (bf16[3,128,128]{2,1,0:T(8,128)(2,1)S(1)}, bf16[3,128,128]{2,1,0:T(8,128)(2,1)S(1)}, u32[]{:S(2)}, u32[]{:S(2)}) collective-permute-start(bf16[3,128,128]{2,1,0:T(8,128)(2,1)S(1)} %collective-permute-done.refs_10_), channel_id=1, source_target_pairs={{0,16},{4,20},{8,24},{12,28},{16,0},{20,4},{24,8},{28,12},{1,17},{... | collective-permute-start | bytes 294920 | tf_op jit(solution)/shard_map/ppermute | solution.py:20
  17.8 4.6 %collective-permute-start.9 = (bf16[3,128,128]{2,1,0:T(8,128)(2,1)S(1)}, bf16[3,128,128]{2,1,0:T(8,128)(2,1)S(1)}, u32[]{:S(2)}, u32[]{:S(2)}) collective-permute-start(bf16[3,128,128]{2,1,0:T(8,128)(2,1)S(1)} %collective-permute-done.refs_10_), channel_id=1, source_target_pairs={{0,8},{4,12},{8,0},{12,4},{16,24},{20,28},{24,16},{28,20},{1,9},{5... | collective-permute-start | bytes 294920 | tf_op jit(solution)/shard_map/ppermute | solution.py:20
  18.4 4.3 %collective-permute-start.8 = (bf16[3,128,128]{2,1,0:T(8,128)(2,1)S(1)}, bf16[3,128,128]{2,1,0:T(8,128)(2,1)S(1)}, u32[]{:S(2)}, u32[]{:S(2)}) collective-permute-start(bf16[3,128,128]{2,1,0:T(8,128)(2,1)S(1)} %collective-permute-done.refs_10_), channel_id=1, source_target_pairs={{0,4},{4,0},{8,12},{12,8},{16,20},{20,16},{24,28},{28,24},{1,5},{5... | collective-permute-start | bytes 294920 | tf_op jit(solution)/shard_map/ppermute | solution.py:20
  21.3 1.7 %collective-permute-start.7 = (bf16[3,128,128]{2,1,0:T(8,128)(2,1)S(1)}, bf16[3,128,128]{2,1,0:T(8,128)(2,1)S(1)}, u32[]{:S(2)}, u32[]{:S(2)}) collective-permute-start(bf16[3,128,128]{2,1,0:T(8,128)(2,1)S(1)} %collective-permute-done.6.refs_8_), channel_id=1, source_target_pairs={{0,4},{4,0},{8,12},{12,8},{16,20},{20,16},{24,28},{28,24},{1,5},{5... | collective-permute-start | bytes 294920 | tf_op jit(solution)/shard_map/ppermute | solution.py:20
  22.2 1.3 %collective-permute-start.5 = (bf16[3,128,128]{2,1,0:T(8,128)(2,1)S(1)}, bf16[3,128,128]{2,1,0:T(8,128)(2,1)S(1)}, u32[]{:S(2)}, u32[]{:S(2)}) collective-permute-start(bf16[3,128,128]{2,1,0:T(8,128)(2,1)S(1)} %collective-permute-done.4.refs_6_), channel_id=1, source_target_pairs={{0,4},{4,0},{8,12},{12,8},{16,20},{20,16},{24,28},{28,24},{1,5},{5... | collective-permute-start | bytes 294920 | tf_op jit(solution)/shard_map/ppermute | solution.py:20
  22.4 1.3 %collective-permute-start.3 = (bf16[3,128,128]{2,1,0:T(8,128)(2,1)S(1)}, bf16[3,128,128]{2,1,0:T(8,128)(2,1)S(1)}, u32[]{:S(2)}, u32[]{:S(2)}) collective-permute-start(bf16[3,128,128]{2,1,0:T(8,128)(2,1)S(1)} %collective-permute-done.2.refs_4_), channel_id=1, source_target_pairs={{0,4},{4,0},{8,12},{12,8},{16,20},{20,16},{24,28},{28,24},{1,5},{5... | collective-permute-start | bytes 294920 | tf_op jit(solution)/shard_map/ppermute | solution.py:20
  22.7 2.7 %collective-permute-start.14 = (bf16[3,128,128]{2,1,0:T(8,128)(2,1)S(1)}, bf16[3,128,128]{2,1,0:T(8,128)(2,1)S(1)}, u32[]{:S(2)}, u32[]{:S(2)}) collective-permute-start(bf16[3,128,128]{2,1,0:T(8,128)(2,1)S(1)} %collective-permute-done.13.refs_16_), channel_id=1, source_target_pairs={{0,4},{4,0},{8,12},{12,8},{16,20},{20,16},{24,28},{28,24},{1,5},{5... | collective-permute-start | bytes 294920 | tf_op jit(solution)/shard_map/ppermute | solution.py:20
  23.0 2.4 %collective-permute-start.12 = (bf16[3,128,128]{2,1,0:T(8,128)(2,1)S(1)}, bf16[3,128,128]{2,1,0:T(8,128)(2,1)S(1)}, u32[]{:S(2)}, u32[]{:S(2)}) collective-permute-start(bf16[3,128,128]{2,1,0:T(8,128)(2,1)S(1)} %collective-permute-done.11.refs_14_), channel_id=1, source_target_pairs={{0,4},{4,0},{8,12},{12,8},{16,20},{20,16},{24,28},{28,24},{1,5},{5... | collective-permute-start | bytes 294920 | tf_op jit(solution)/shard_map/ppermute | solution.py:20
  23.5 1.9 %collective-permute-start.10 = (bf16[3,128,128]{2,1,0:T(8,128)(2,1)S(1)}, bf16[3,128,128]{2,1,0:T(8,128)(2,1)S(1)}, u32[]{:S(2)}, u32[]{:S(2)}) collective-permute-start(bf16[3,128,128]{2,1,0:T(8,128)(2,1)S(1)} %collective-permute-done.9.refs_12_), channel_id=1, source_target_pairs={{0,4},{4,0},{8,12},{12,8},{16,20},{20,16},{24,28},{28,24},{1,5},{5... | collective-permute-start | bytes 294920 | tf_op jit(solution)/shard_map/ppermute | solution.py:20
  23.8 14.1 %collective-permute-start.17 = (bf16[12,128,128]{2,1,0:T(8,128)(2,1)S(1)}, bf16[12,128,128]{2,1,0:T(8,128)(2,1)S(1)}, u32[]{:S(2)}, u32[]{:S(2)}) collective-permute-start(bf16[12,128,128]{2,1,0:T(8,128)(2,1)S(1)} %get-tuple-element.23.refs_19_), channel_id=1, source_target_pairs={{0,1},{1,0},{2,3},{3,2},{4,5},{5,4},{6,7},{7,6},{8,9},{9,8},{10,11... | collective-permute-start | bytes 1179656 | tf_op jit(solution)/shard_map/ppermute | solution.py:20
  30.6 14.1 %collective-permute-start.16 = (f32[128,256]{1,0:T(8,128)S(1)}, f32[128,256]{1,0:T(8,128)S(1)}, u32[]{:S(2)}, u32[]{:S(2)}) collective-permute-start(f32[128,256]{1,0:T(8,128)S(1)} %get-tuple-element.27), channel_id=1, source_target_pairs={{0,2},{1,3},{2,0},{3,1},{4,6},{5,7},{6,4},{7,5},{8,10},{9,11},{10,... | collective-permute-start | bytes 393224 | tf_op jit(solution)/shard_map/ppermute | solution.py:20
  39.1 5.5 %collective-permute-start.18 = (f32[128,128]{1,0:T(8,128)S(1)}, f32[128,128]{1,0:T(8,128)S(1)}, u32[]{:S(2)}, u32[]{:S(2)}) collective-permute-start(f32[128,128]{1,0:T(8,128)S(1)} %get-tuple-element.30), channel_id=1, source_target_pairs={{0,2},{1,3},{2,0},{3,1},{4,6},{5,7},{6,4},{7,5},{8,10},{9,11},{10,... | collective-permute-start | bytes 196616 | tf_op jit(solution)/shard_map/ppermute | solution.py:20

commit v4 on v3

v4 whole, which is shorter than its diff:
```python
import jax
import jax.numpy as jnp
from jax import lax
from jax.experimental import pallas as pl
from jax.experimental.pallas import tpu as pltpu
from jax.sharding import PartitionSpec as P

VMEM_BYTES = 48 * 1024 * 1024
UNROLL = 4
OWN_FLOPS = 3750000000
HEAD_FLOPS = 250000000
TABLE_ROWS = 16
PARTS = 2
SMEM = pl.BlockSpec(memory_space=pltpu.SMEM)
VMEM = pl.BlockSpec(memory_space=pltpu.VMEM)
ANY = pl.BlockSpec(memory_space=pl.ANY)
HBM = pl.BlockSpec(memory_space=pltpu.HBM)


def shift(value, axis, size, mask):
    return lax.ppermute(value, axis, [(j, j ^ mask) for j in range(size)])


def contract(total, lists_ref, a, live, slots, stage, blocks_of, flip=False):
    blocks, _, rows, depth = stage.shape
    dims = (((1,), (1,)), ((), ()))

    def pair(s):
        sides, weights = [], []
        for slot in (s, s + 1):
            safe = jnp.minimum(slot, slots - 1)
            block = blocks_of(safe)
            sides.append(stage[:, lists_ref[a, safe]].reshape(blocks * rows, depth))
            weights.append(jnp.where(slot < live, block, jnp.zeros_like(block)))
        sides, weights = jnp.concatenate(sides, axis=1), jnp.concatenate(weights, axis=1)
        left, right = (weights, sides) if flip else (sides, weights)
        return lax.dot_general(left, right, dims, preferred_element_type=jnp.float32)

    def step(group, total):
        for offset in range(0, UNROLL, 2):
            total = total + pair(UNROLL * group + offset)
        return total

    return lax.fori_loop(0, (live + UNROLL - 1) // UNROLL, step, total)


def plain_kernel(lists_ref, live_ref, place_ref, piece, integrals_ref, out_ref, stage, sems):
    copy = pltpu.make_async_copy(piece, stage, sems.at[0])
    copy.start()
    copy.wait()
    tile_dev, _, width, _ = integrals_ref.shape
    blocks, _, rows, _ = stage.shape
    for a in range(tile_dev):
        zero = jnp.zeros((blocks * rows, width), jnp.float32)
        total = contract(zero, lists_ref, a, live_ref[a], lists_ref.shape[1], stage, lambda s, a=a: integrals_ref[a, s])
        for k in range(blocks):
            out_ref[k, :, a * width:(a + 1) * width] = total[k * rows:(k + 1) * rows]


def plain_partials(lists, live, everything, integrals):
    blocks, tiles, rows, depth = everything.shape
    tile_dev, _, width, _ = integrals.shape
    return pl.pallas_call(
        plain_kernel,
        out_shape=jax.ShapeDtypeStruct((blocks, rows, tile_dev * width), jnp.float32),
        in_specs=[SMEM] * 3 + [ANY, VMEM],
        out_specs=VMEM,
        scratch_shapes=[pltpu.VMEM((blocks, tiles, rows, depth), everything.dtype), pltpu.SemaphoreType.DMA((1,))],
        compiler_params=pltpu.CompilerParams(vmem_limit_bytes=VMEM_BYTES),
    )(lists, live, jnp.zeros((1,), jnp.int32), everything, integrals)


def split(tile_dev, slots, width):
    size = width // PARTS
    places = [[(0, a * slots * width, width)] for a in range(tile_dev - 1)]
    places.append([(1 + n, 0, size) for n in range(PARTS)])
    return places, [(tile_dev - 1) * slots * width] + [slots * size] * PARTS


def cut_kernel(whole, amplitudes, lists, counts, *refs):
    arrays, (amplitudes_out, table, lists_v, counts_s, sems) = refs[:1 + PARTS], refs[1 + PARTS:]
    head = arrays[0]
    tile_dev, slots, width, _ = whole.shape
    places, sizes = split(tile_dev, slots, width)
    small = [(lists, lists_v), (counts, counts_s)]
    large = [(amplitudes, amplitudes_out)]
    for a, parts in enumerate(places):
        done = 0
        for array, first, size in parts:
            target = arrays[array]
            if size == width:
                large.append((whole.at[a], target.at[pl.ds(first, slots * size)].reshape(slots, size, whole.shape[3])))
                continue
            for s in range(slots):
                large.append((whole.at[a, s, pl.ds(done, size)], target.at[pl.ds(first + s * size, size)]))
            done += size
    copies = [pltpu.make_async_copy(x, y, sems.at[n]) for n, (x, y) in enumerate(small + large)]
    for copy in copies:
        copy.start()
    for copy in copies[:2]:
        copy.wait()
    lane = lax.broadcasted_iota(jnp.int32, table.shape, 1)
    values = jnp.zeros(table.shape, jnp.int32)
    for a in range(tile_dev):
        values = jnp.where(lane == a, counts_s[a], values)
    table[...] = values
    table[:tile_dev, :slots] = lists_v[...]
    head[sizes[0]:] = table[...].astype(jnp.float32).astype(head.dtype)
    for copy in copies[2:]:
        copy.wait()


def cut(whole, amplitudes, lists, counts):
    tile_dev, slots, width, depth = whole.shape
    sizes = split(tile_dev, slots, width)[1]
    placed = [pltpu.with_memory_space_constraint(x, pltpu.HBM) for x in (whole, amplitudes, lists, counts)]
    return pl.pallas_call(
        cut_kernel,
        out_shape=(
            jax.ShapeDtypeStruct((sizes[0] + TABLE_ROWS, depth), whole.dtype),
            *(jax.ShapeDtypeStruct((size, depth), whole.dtype) for size in sizes[1:]),
            jax.ShapeDtypeStruct(amplitudes.shape, amplitudes.dtype),
            jax.ShapeDtypeStruct((TABLE_ROWS, depth), jnp.int32),
        ),
        in_specs=[HBM] * 4,
        out_specs=(VMEM,) * (3 + PARTS),
        scratch_shapes=[
            pltpu.VMEM(lists.shape, lists.dtype),
            pltpu.SMEM(counts.shape, counts.dtype),
            pltpu.SemaphoreType.DMA((3 + (tile_dev - 1) + PARTS * slots,)),
        ],
        compiler_params=pltpu.CompilerParams(vmem_limit_bytes=VMEM_BYTES),
    )(*placed)


def stack_kernel(first, second, out):
    out[0] = first[...]
    out[1] = second[...]


def live_slots(table_ref, a, group, slots):
    return jnp.clip(table_ref[TABLE_ROWS - 1, a] - group * slots, 0, slots)


def blocks_at(arrays, parts):
    def block(s):
        rows = [arrays[array][pl.ds(pl.multiple_of(first + s * size, 16), size)] for array, first, size in parts]
        return rows[0] if len(rows) == 1 else jnp.concatenate(rows, axis=0)

    return block


def own_kernel(masks, slots, place_ref, table_v, *refs):
    count = len(masks)
    pieces, arrays, (sums_ref, last_ref, stage, table, sem) = refs[:count], refs[count:-5], refs[-5:]
    blocks, _, rows, _ = stage.shape
    before, _, width = sums_ref.shape
    copy = pltpu.make_async_copy(table_v, table, sem)
    copy.start()
    for piece, mask in zip(pieces, masks):
        tiles = piece.shape[1]
        stage[:, pl.ds((place_ref[0] ^ mask) * tiles, tiles)] = piece[...]
    copy.wait()
    places = split(before + 1, slots, width)[0]
    for a, parts in enumerate(places):
        flip = a == before
        total = jnp.zeros((width, blocks * rows) if flip else (blocks * rows, width), jnp.float32)
        live = live_slots(table, a, place_ref[1], slots)
        total = contract(total, table, a, live, slots, stage, blocks_at(arrays, parts), flip)
        if flip:
            last_ref[...] = total
        else:
            sums_ref[a] = total


def head_kernel(slots, place_ref, stage, sums_ref, others, own_ref, far_ref, table_v, table, sem):
    before, both, width = sums_ref.shape
    rows = both // 2
    places, sizes = split(before + 1, slots, width)
    table_v[...] = others[sizes[0]:].astype(jnp.float32).astype(jnp.int32)
    copy = pltpu.make_async_copy(table_v, table, sem)
    copy.start()
    copy.wait()
    for a in range(before):
        live = live_slots(table, a, place_ref[1] ^ 1, slots)
        total = contract(sums_ref[a], table, a, live, slots, stage, blocks_at((others,), places[a]))
        own_ref[a * rows:(a + 1) * rows] = total[:rows]
        far_ref[a * rows:(a + 1) * rows] = total[rows:]


def pick_kernel(a, slots, place_ref, table_v, stage, picked, table, sem):
    blocks, _, rows, depth = stage.shape
    copy = pltpu.make_async_copy(table_v, table, sem)
    copy.start()
    copy.wait()
    live = live_slots(table, a, place_ref[1] ^ 1, slots)
    for s in range(slots):
        block = stage[:, table[a, s]].reshape(blocks * rows, depth)
        picked[:, s * depth:(s + 1) * depth] = jnp.where(s < live, block, jnp.zeros_like(block))


def tail_kernel(slots, n, last_ref, picked, others, own_ref, far_ref):
    size, rows = own_ref.shape
    depth = others.shape[1]
    total = last_ref[n * size:(n + 1) * size]
    for s in range(0, slots, 2):
        some = range(s, min(s + 2, slots))
        weights = jnp.concatenate([others[m * size:(m + 1) * size] for m in some], axis=1)
        sides = picked[:, s * depth:(s + len(some)) * depth]
        total = total + lax.dot_general(weights, sides, (((1,), (1,)), ((), ())), preferred_element_type=jnp.float32)
    own_ref[...] = total[:, :rows]
    far_ref[...] = total[:, rows:]


def join_kernel(*refs):
    own, got, out = refs[:1 + PARTS], refs[1 + PARTS:-1], refs[-1]
    rows = out.shape[0]
    before = own[0].shape[0] // rows
    width = out.shape[1] // (before + 1)
    for a in range(before):
        part = pl.ds(a * rows, rows)
        out[:, a * width:(a + 1) * width] = own[0][part] + got[0][part]
    last = jnp.concatenate([own[n][...] + got[n][...] for n in range(1, 1 + PARTS)], axis=0)
    out[:, before * width:] = jnp.transpose(last)


def on_pairs(amplitudes, tile_counts, tile_lists, integrals, n_vv, n_oo):
    tile_dev, slots, width, depth = integrals.shape
    rows = amplitudes.shape[1]
    tiles = n_vv * tile_dev
    before = tile_dev - 1
    place = jnp.stack([lax.axis_index("vv"), lax.axis_index("oo")]).astype(jnp.int32)

    far = shift(amplitudes, "oo", n_oo, 2)
    *arrays, amplitudes, table = cut(integrals, amplitudes, tile_lists, tile_counts)
    others = [shift(array, "oo", n_oo, 1) for array in arrays]
    block = pl.pallas_call(
        stack_kernel,
        out_shape=jax.ShapeDtypeStruct((2,) + amplitudes.shape, amplitudes.dtype),
        in_specs=[VMEM] * 2,
        out_specs=VMEM,
        compiler_params=pltpu.CompilerParams(vmem_limit_bytes=VMEM_BYTES),
        cost_estimate=pl.CostEstimate(flops=2**20, bytes_accessed=2**19, transcendentals=0),
    )(amplitudes, far)
    pieces, masks = [], []
    for mask in (0, 2, 4, 6):
        piece = shift(block, "vv", n_vv, mask) if mask else block
        pieces += [piece, shift(piece, "vv", n_vv, 1)]
        masks += [mask, mask ^ 1]
    scratch = [pltpu.SMEM(table.shape, table.dtype), pltpu.SemaphoreType.DMA]

    def call(kernel, out, n_smem, n_vmem, scratch, flops):
        return pl.pallas_call(
            kernel,
            out_shape=out,
            in_specs=[SMEM] * n_smem + [VMEM] * n_vmem,
            out_specs=jax.tree.map(lambda _: VMEM, out),
            scratch_shapes=scratch,
            compiler_params=pltpu.CompilerParams(vmem_limit_bytes=VMEM_BYTES),
            cost_estimate=pl.CostEstimate(flops=flops, bytes_accessed=2**21, transcendentals=0),
        )

    def f32(*shape):
        return jax.ShapeDtypeStruct(shape, jnp.float32)

    sums, last, stage = call(
        lambda *refs: own_kernel(masks, slots, *refs),
        (f32(before, 2 * rows, width), f32(width, 2 * rows), jax.ShapeDtypeStruct((2, tiles, rows, depth), far.dtype)),
        1, len(pieces) + 2 + PARTS, scratch, OWN_FLOPS,
    )(place, table, *pieces, *arrays)
    part = f32(before * rows, width)
    own, away, table = call(
        lambda *refs: head_kernel(slots, *refs),
        (part, part, jax.ShapeDtypeStruct(table.shape, table.dtype)),
        1, 3, scratch, HEAD_FLOPS,
    )(place, stage, sums, others[0])
    picked = call(
        lambda *refs: pick_kernel(before, slots, *refs),
        jax.ShapeDtypeStruct((2 * rows, slots * depth), far.dtype),
        1, 2, scratch, 2**28,
    )(place, table, stage)
    owns, gots = [own], [shift(away, "oo", n_oo, 2)]
    for n in range(PARTS):
        own, away = call(
            lambda *refs, n=n: tail_kernel(slots, n, *refs), (f32(width // PARTS, rows),) * 2, 0, 3, [], 2**28
        )(last, picked, others[1 + n])
        owns.append(own)
        gots.append(shift(away, "oo", n_oo, 2))
    return call(join_kernel, f32(rows, tile_dev * width), 0, 2 * (1 + PARTS), [], 2**20)(*owns, *gots)


def on_device(amplitudes, tile_counts, tile_lists, integrals, n_vv, n_oo):
    if (n_vv, n_oo) == (8, 4):
        return on_pairs(amplitudes, tile_counts, tile_lists, integrals, n_vv, n_oo)
    slots = tile_lists.shape[1]
    live = jnp.clip(tile_counts - lax.axis_index("oo") * slots, 0, slots)
    rows = lax.all_gather(amplitudes, "oo", axis=0, tiled=False)
    everything = lax.all_gather(rows, "vv", axis=1, tiled=True)
    parts = plain_partials(tile_lists, live, everything, integrals)
    return lax.psum_scatter(parts.reshape(-1, parts.shape[2]), "oo", scatter_dimension=0, tiled=True)


def solution(mesh):
    n_vv, n_oo = mesh.shape["vv"], mesh.shape["oo"]
    placed = (P("vv", "oo", None), P("vv"), P("vv", "oo"), P("vv", "oo", None, None))
    return jax.shard_map(
        lambda *args: on_device(*args, n_vv, n_oo),
        mesh=mesh, in_specs=placed, out_specs=P("oo", "vv"), check_vma=False,
    )
```

time: 46.1 us -> 43.1 us (0.935)
  starting transfers between devices: 19.9 us -> 16.2 us
  Pallas kernels: 7.76 us -> 9.08 us
  other arithmetic: 0.8 us -> 0.07 us
  waiting for transfers between devices: 16.8 us -> 17.4 us
    ppermute x19 -> x14, starting transfers between devices: 19.9 us -> 16.2 us  [shift(): return lax.ppermute(value, axis, [(j, j ^ mask) for j in range(size)])]
    pallas_call x4 -> x8, Pallas kernels: 7.76 us -> 9.08 us  [the longest x1 2.72 us: on_pairs(): call(lambda *refs: own_kernel(masks, slots, *refs), (f32(before, 2 * rows...]
    concatenate x1 -> x0, other arithmetic: 0.69 us -> none  [on_pairs(): return jnp.concatenate([left, right], axis=1)]
    ppermute x19 -> x14, waiting for transfers between devices: 16.8 us -> 17.4 us  [shift(): return lax.ppermute(value, axis, [(j, j ^ mask) for j in range(size)])]
  transfers between devices with their start and end apart: 19 -> 14, of which waited for: 8 -> 8; matrix products, arithmetic and copies ran while one was open for 0% -> 0% of each run, Pallas kernels for 17% -> 19%
where the time goes in v4:
time: 43.1 us; the launch traced here: 42.8 us
  waiting for transfers between devices  17.4 us (40%)
  starting transfers between devices  16.2 us (38%)
  Pallas kernels  9.08 us (21%)
    ppermute x14, waiting for transfers between devices, shift(): return lax.ppermute(value, axis, [(j, j ^ mask) for j in range(size)])  17.4 us
    ppermute x14, starting transfers between devices, shift(): return lax.ppermute(value, axis, [(j, j ^ mask) for j in range(size)])  16.2 us
    pallas_call x1, Pallas kernels, on_pairs(): call(lambda *refs: own_kernel(masks, slots, *refs), (f32(before, 2 * rows...  2.72 us
    pallas_call x1, Pallas kernels, on_pairs(): call(lambda *refs: head_kernel(slots, *refs), (part, part, jax.ShapeDtype...  1.98 us
    pallas_call x1, Pallas kernels, cut(): pl.pallas_call(cut_kernel, out_shape=(jax.ShapeDtypeStruct((sizes[0] + TA...  1.47 us
    pallas_call x1, Pallas kernels, on_pairs(): call(lambda *refs: pick_kernel(before, slots, *refs), jax.ShapeDtypeStruc...  1.39 us
  transfers between devices with their start and end apart: 14, of which 8 were waited for; matrix products, arithmetic and copies ran while one was open for 0% of the time, Pallas kernels for 19%

profile of v4, /device:TPU:0, one launch (start us, length us, event | category | flops | bytes accessed | tf_op | source)
XLA Modules:
  0.0 42.8 jit_solution(3070267035812835157)
XLA Ops:
  0.0 4.0 %collective-permute-start = (bf16[3,128,128]{2,1,0:T(8,128)(2,1)}, bf16[3,128,128]{2,1,0:T(8,128)(2,1)S(1)}, u32[]{:S(2)}, u32[]{:S(2)}) collective-permute-start(bf16[3,128,128]{2,1,0:T(8,128)(2,1)} %amplitudes.1), channel_id=1, source_target_pairs={{0,2},{1,3},{2,0},{3,1},{4,6},{5,7},{6,4},{7,5},{8,10},{9,11},{10,... | collective-permute-start | bytes 294920 | tf_op jit(solution)/shard_map/ppermute | solution.py:21
  4.0 1.5 %shard_map.46 = (bf16[3088,128]{1,0:T(8,128)(2,1)S(1)}, bf16[768,128]{1,0:T(8,128)(2,1)S(1)}, bf16[768,128]{1,0:T(8,128)(2,1)S(1)}, bf16[3,128,128]{2,1,0:T(8,128)(2,1)S(1)}, s32[16,128]{1,0:T(8,128)S(1)}) custom-call(bf16[3,12,128,128]{3,2,1,0:T(8,128)(2,1)} %whole.1, bf16[3,128,128]{2,1,0:T(8,128)(2,1)} %amplitudes.1, s32[3,12]{1,0:T(4,128)} %lists.1, s32[3]{0:T(128)} %counts.1), custom_call_target="tpu_custom_call" | custom-call | tf_op jit(solution)/shard_map/pallas_call | solution.py:117
  5.5 1.6 %collective-permute-start.8 = (bf16[3088,128]{1,0:T(8,128)(2,1)S(1)}, bf16[3088,128]{1,0:T(8,128)(2,1)S(1)}, u32[]{:S(2)}, u32[]{:S(2)}) collective-permute-start(bf16[3088,128]{1,0:T(8,128)(2,1)S(1)} %get-tuple-element.22.refs_10_), channel_id=1, source_target_pairs={{0,1},{1,0},{2,3},{3,2},{4,5},{5,4},{6,7},{7,6},{8,9},{9,8},{10,11... | collective-permute-start | bytes 2371592 | tf_op jit(solution)/shard_map/ppermute | solution.py:21
  7.2 2.1 %collective-permute-done.second = bf16[3,128,128]{2,1,0:T(8,128)(2,1)S(1)} collective-permute-done((bf16[3,128,128]{2,1,0:T(8,128)(2,1)}, bf16[3,128,128]{2,1,0:T(8,128)(2,1)S(1)}, u32[]{:S(2)}, u32[]{:S(2)}) %collective-permute-start) | collective-permute-done | bytes 98336 | tf_op jit(solution)/shard_map/ppermute | solution.py:21
  9.3 1.6 %collective-permute-start.2 = (bf16[2,3,128,128]{3,2,1,0:T(8,128)(2,1)S(1)}, bf16[2,3,128,128]{3,2,1,0:T(8,128)(2,1)S(1)}, u32[]{:S(2)}, u32[]{:S(2)}) collective-permute-start(bf16[2,3,128,128]{3,2,1,0:T(8,128)(2,1)S(1)} %shard_map.47.refs_2_), channel_id=1, source_target_pairs={{0,8},{4,12},{8,0},{12,4},{16,24},{20,28},{24,16},{28,20},{1,9},{5... | collective-permute-start | bytes 589832 | tf_op jit(solution)/shard_map/ppermute | solution.py:21
  10.9 1.5 %collective-permute-start.4 = (bf16[2,3,128,128]{3,2,1,0:T(8,128)(2,1)S(1)}, bf16[2,3,128,128]{3,2,1,0:T(8,128)(2,1)S(1)}, u32[]{:S(2)}, u32[]{:S(2)}) collective-permute-start(bf16[2,3,128,128]{3,2,1,0:T(8,128)(2,1)S(1)} %shard_map.47.refs_2_), channel_id=1, source_target_pairs={{0,16},{4,20},{8,24},{12,28},{16,0},{20,4},{24,8},{28,12},{1,17},{... | collective-permute-start | bytes 589832 | tf_op jit(solution)/shard_map/ppermute | solution.py:21
  12.4 0.4 collective-permute-start.6
  12.8 4.0 %collective-permute-done.2.refs_4_ = bf16[2,3,128,128]{3,2,1,0:T(8,128)(2,1)S(1)} collective-permute-done((bf16[2,3,128,128]{3,2,1,0:T(8,128)(2,1)S(1)}, bf16[2,3,128,128]{3,2,1,0:T(8,128)(2,1)S(1)}, u32[]{:S(2)}, u32[]{:S(2)}) %collective-permute-start.2) | collective-permute-done | bytes 196640 | tf_op jit(solution)/shard_map/ppermute | solution.py:21
  16.8 1.9 %collective-permute-done.4.refs_6_ = bf16[2,3,128,128]{3,2,1,0:T(8,128)(2,1)S(1)} collective-permute-done((bf16[2,3,128,128]{3,2,1,0:T(8,128)(2,1)S(1)}, bf16[2,3,128,128]{3,2,1,0:T(8,128)(2,1)S(1)}, u32[]{:S(2)}, u32[]{:S(2)}) %collective-permute-start.4) | collective-permute-done | bytes 196640 | tf_op jit(solution)/shard_map/ppermute | solution.py:21
  18.7 0.4 collective-permute-done.6.refs_8_
  19.1 0.1 collective-permute-start.7
  19.3 3.7 %collective-permute-start.10 = (bf16[768,128]{1,0:T(8,128)(2,1)S(1)}, bf16[768,128]{1,0:T(8,128)(2,1)S(1)}, u32[]{:S(2)}, u32[]{:S(2)}) collective-permute-start(bf16[768,128]{1,0:T(8,128)(2,1)S(1)} %get-tuple-element.24.refs_12_), channel_id=1, source_target_pairs={{0,1},{1,0},{2,3},{3,2},{4,5},{5,4},{6,7},{7,6},{8,9},{9,8},{10,11... | collective-permute-start | bytes 589832 | tf_op jit(solution)/shard_map/ppermute | solution.py:21
  23.0 2.7 %shard_map.48 = (f32[2,256,128]{2,1,0:T(8,128)S(1)}, f32[128,256]{1,0:T(8,128)S(1)}, bf16[2,24,128,128]{3,2,1,0:T(8,128)(2,1)S(1)}) custom-call(s32[2]{0:T(128)S(1)} %pad_add_fusion.refs_0_, s32[16,128]{1,0:T(8,128)S(1)} %get-tuple-element.20.refs_1_, bf16[2,3,128,128]{3,2,1,0:T(8,128)(2,1)S(1)} %shard_map.47.refs_2_, ...), custom_call_target="tpu_custom_call" | custom-call | flops 3750000128 | bytes 2097152 | tf_op jit(solution)/shard_map/pallas_call | solution.py:266
  25.8 0.5 %collective-permute-done.8.refs_3_ = bf16[3088,128]{1,0:T(8,128)(2,1)S(1)} collective-permute-done((bf16[3088,128]{1,0:T(8,128)(2,1)S(1)}, bf16[3088,128]{1,0:T(8,128)(2,1)S(1)}, u32[]{:S(2)}, u32[]{:S(2)}) %collective-permute-start.8) | collective-permute-done | bytes 790560 | tf_op jit(solution)/shard_map/ppermute | solution.py:21
  26.2 2.0 %shard_map.49 = (f32[256,128]{1,0:T(8,128)S(1)}, f32[256,128]{1,0:T(8,128)S(1)}, s32[16,128]{1,0:T(8,128)S(1)}) custom-call(s32[2]{0:T(128)S(1)} %pad_add_fusion.refs_0_, bf16[2,24,128,128]{3,2,1,0:T(8,128)(2,1)S(1)} %get-tuple-element.25.refs_1_.refs_2_, f32[2,256,128]{2,1,0:T(8,128)S(1)} %get-tuple-element.26.refs_2_, ...), custom_call_target="tpu_custom_call" | custom-call | flops 250000000 | bytes 2097152 | tf_op jit(solution)/shard_map/pallas_call | solution.py:272
  28.2 2.2 %collective-permute-start.11 = (f32[256,128]{1,0:T(8,128)S(1)}, f32[256,128]{1,0:T(8,128)S(1)}, u32[]{:S(2)}, u32[]{:S(2)}) collective-permute-start(f32[256,128]{1,0:T(8,128)S(1)} %get-tuple-element.32), channel_id=1, source_target_pairs={{0,2},{1,3},{2,0},{3,1},{4,6},{5,7},{6,4},{7,5},{8,10},{9,11},{10,... | collective-permute-start | bytes 393224 | tf_op jit(solution)/shard_map/ppermute | solution.py:21
  30.4 1.4 %shard_map.50.refs_1_ = bf16[256,1536]{1,0:T(8,128)(2,1)S(1)} custom-call(s32[2]{0:T(128)S(1)} %pad_add_fusion.refs_0_, s32[16,128]{1,0:T(8,128)S(1)} %get-tuple-element.29.refs_1_, bf16[2,24,128,128]{3,2,1,0:T(8,128)(2,1)S(1)} %get-tuple-element.25.refs_1_.refs_2_), custom_call_target="tpu_custom_call" | custom-call | flops 268435456 | bytes 2097152 | tf_op jit(solution)/shard_map/pallas_call | solution.py:277
  31.8 0.4 shard_map.52
  32.2 0.9 %collective-permute-start.13 = (f32[64,128]{1,0:T(8,128)S(1)}, f32[64,128]{1,0:T(8,128)S(1)}, u32[]{:S(2)}, u32[]{:S(2)}) collective-permute-start(f32[64,128]{1,0:T(8,128)S(1)} %get-tuple-element.34), channel_id=1, source_target_pairs={{0,2},{1,3},{2,0},{3,1},{4,6},{5,7},{6,4},{7,5},{8,10},{9,11},{10,... | collective-permute-start | bytes 98312 | tf_op jit(solution)/shard_map/ppermute | solution.py:21
  33.1 3.8 %collective-permute-done.9.refs_2_ = bf16[768,128]{1,0:T(8,128)(2,1)S(1)} collective-permute-done((bf16[768,128]{1,0:T(8,128)(2,1)S(1)}, bf16[768,128]{1,0:T(8,128)(2,1)S(1)}, u32[]{:S(2)}, u32[]{:S(2)}) %collective-permute-start.9) | collective-permute-done | bytes 196640 | tf_op jit(solution)/shard_map/ppermute | solution.py:21
  36.8 0.4 shard_map.51
  37.3 2.3 %collective-permute-done.13.refs_5_ = f32[64,128]{1,0:T(8,128)S(1)} collective-permute-done((f32[64,128]{1,0:T(8,128)S(1)}, f32[64,128]{1,0:T(8,128)S(1)}, u32[]{:S(2)}, u32[]{:S(2)}) %collective-permute-start.13) | collective-permute-done | bytes 32800 | tf_op jit(solution)/shard_map/ppermute | solution.py:21
  39.5 2.5 %collective-permute-done.12.refs_4_ = f32[64,128]{1,0:T(8,128)S(1)} collective-permute-done((f32[64,128]{1,0:T(8,128)S(1)}, f32[64,128]{1,0:T(8,128)S(1)}, u32[]{:S(2)}, u32[]{:S(2)}) %collective-permute-start.12) | collective-permute-done | bytes 32800 | tf_op jit(solution)/shard_map/ppermute | solution.py:21
  42.1 0.8 %shard_map.53 = f32[128,384]{1,0:T(8,128)} custom-call(f32[256,128]{1,0:T(8,128)S(1)} %get-tuple-element.27.refs_0_, f32[64,128]{1,0:T(8,128)S(1)} %get-tuple-element.30.refs_1_, f32[64,128]{1,0:T(8,128)S(1)} %get-tuple-element.31.refs_2_, f32[256,128]{1,0:T(8,128)S(1)} %collective-permute-done.11.refs_3_, f32[64,128]{1,0:T(8,128)S(1)} %collective-permute-done.12.refs_4_, ...), custom_call_target="tpu_custom_call" | custom-call | flops 1048576 | bytes 2097152 | tf_op jit(solution)/shard_map/pallas_call | solution.py:289
  (13 shorter events, 0.3 us)
Async XLA Ops:
  0.0 9.2 %collective-permute-start = (bf16[3,128,128]{2,1,0:T(8,128)(2,1)}, bf16[3,128,128]{2,1,0:T(8,128)(2,1)S(1)}, u32[]{:S(2)}, u32[]{:S(2)}) collective-permute-start(bf16[3,128,128]{2,1,0:T(8,128)(2,1)} %amplitudes.1), channel_id=1, source_target_pairs={{0,2},{1,3},{2,0},{3,1},{4,6},{5,7},{6,4},{7,5},{8,10},{9,11},{10,... | collective-permute-start | bytes 294920 | tf_op jit(solution)/shard_map/ppermute | solution.py:21
  5.5 20.7 %collective-permute-start.8 = (bf16[3088,128]{1,0:T(8,128)(2,1)S(1)}, bf16[3088,128]{1,0:T(8,128)(2,1)S(1)}, u32[]{:S(2)}, u32[]{:S(2)}) collective-permute-start(bf16[3088,128]{1,0:T(8,128)(2,1)S(1)} %get-tuple-element.22.refs_10_), channel_id=1, source_target_pairs={{0,1},{1,0},{2,3},{3,2},{4,5},{5,4},{6,7},{7,6},{8,9},{9,8},{10,11... | collective-permute-start | bytes 2371592 | tf_op jit(solution)/shard_map/ppermute | solution.py:21
  9.3 7.5 %collective-permute-start.2 = (bf16[2,3,128,128]{3,2,1,0:T(8,128)(2,1)S(1)}, bf16[2,3,128,128]{3,2,1,0:T(8,128)(2,1)S(1)}, u32[]{:S(2)}, u32[]{:S(2)}) collective-permute-start(bf16[2,3,128,128]{3,2,1,0:T(8,128)(2,1)S(1)} %shard_map.47.refs_2_), channel_id=1, source_target_pairs={{0,8},{4,12},{8,0},{12,4},{16,24},{20,28},{24,16},{28,20},{1,9},{5... | collective-permute-start | bytes 589832 | tf_op jit(solution)/shard_map/ppermute | solution.py:21
  10.9 7.8 %collective-permute-start.4 = (bf16[2,3,128,128]{3,2,1,0:T(8,128)(2,1)S(1)}, bf16[2,3,128,128]{3,2,1,0:T(8,128)(2,1)S(1)}, u32[]{:S(2)}, u32[]{:S(2)}) collective-permute-start(bf16[2,3,128,128]{3,2,1,0:T(8,128)(2,1)S(1)} %shard_map.47.refs_2_), channel_id=1, source_target_pairs={{0,16},{4,20},{8,24},{12,28},{16,0},{20,4},{24,8},{28,12},{1,17},{... | collective-permute-start | bytes 589832 | tf_op jit(solution)/shard_map/ppermute | solution.py:21
  12.4 6.7 %collective-permute-start.6 = (bf16[2,3,128,128]{3,2,1,0:T(8,128)(2,1)S(1)}, bf16[2,3,128,128]{3,2,1,0:T(8,128)(2,1)S(1)}, u32[]{:S(2)}, u32[]{:S(2)}) collective-permute-start(bf16[2,3,128,128]{3,2,1,0:T(8,128)(2,1)S(1)} %shard_map.47.refs_2_), channel_id=1, source_target_pairs={{0,24},{4,28},{8,16},{12,20},{16,8},{20,12},{24,0},{28,4},{1,25},{... | collective-permute-start | bytes 589832 | tf_op jit(solution)/shard_map/ppermute | solution.py:21
  12.8 6.4 %collective-permute-start.1 = (bf16[2,3,128,128]{3,2,1,0:T(8,128)(2,1)S(1)}, bf16[2,3,128,128]{3,2,1,0:T(8,128)(2,1)S(1)}, u32[]{:S(2)}, u32[]{:S(2)}) collective-permute-start(bf16[2,3,128,128]{3,2,1,0:T(8,128)(2,1)S(1)} %shard_map.47.refs_2_), channel_id=1, source_target_pairs={{0,4},{4,0},{8,12},{12,8},{16,20},{20,16},{24,28},{28,24},{1,5},{5... | collective-permute-start | bytes 589832 | tf_op jit(solution)/shard_map/ppermute | solution.py:21
  16.8 6.1 %collective-permute-start.3 = (bf16[2,3,128,128]{3,2,1,0:T(8,128)(2,1)S(1)}, bf16[2,3,128,128]{3,2,1,0:T(8,128)(2,1)S(1)}, u32[]{:S(2)}, u32[]{:S(2)}) collective-permute-start(bf16[2,3,128,128]{3,2,1,0:T(8,128)(2,1)S(1)} %collective-permute-done.2.refs_4_), channel_id=1, source_target_pairs={{0,4},{4,0},{8,12},{12,8},{16,20},{20,16},{24,28},{28,24},{1,5},{5... | collective-permute-start | bytes 589832 | tf_op jit(solution)/shard_map/ppermute | solution.py:21
  18.7 4.4 %collective-permute-start.5 = (bf16[2,3,128,128]{3,2,1,0:T(8,128)(2,1)S(1)}, bf16[2,3,128,128]{3,2,1,0:T(8,128)(2,1)S(1)}, u32[]{:S(2)}, u32[]{:S(2)}) collective-permute-start(bf16[2,3,128,128]{3,2,1,0:T(8,128)(2,1)S(1)} %collective-permute-done.4.refs_6_), channel_id=1, source_target_pairs={{0,4},{4,0},{8,12},{12,8},{16,20},{20,16},{24,28},{28,24},{1,5},{5... | collective-permute-start | bytes 589832 | tf_op jit(solution)/shard_map/ppermute | solution.py:21
  19.1 4.0 %collective-permute-start.7 = (bf16[2,3,128,128]{3,2,1,0:T(8,128)(2,1)S(1)}, bf16[2,3,128,128]{3,2,1,0:T(8,128)(2,1)S(1)}, u32[]{:S(2)}, u32[]{:S(2)}) collective-permute-start(bf16[2,3,128,128]{3,2,1,0:T(8,128)(2,1)S(1)} %collective-permute-done.6.refs_8_), channel_id=1, source_target_pairs={{0,4},{4,0},{8,12},{12,8},{16,20},{20,16},{24,28},{28,24},{1,5},{5... | collective-permute-start | bytes 589832 | tf_op jit(solution)/shard_map/ppermute | solution.py:21
  19.3 12.5 %collective-permute-start.10 = (bf16[768,128]{1,0:T(8,128)(2,1)S(1)}, bf16[768,128]{1,0:T(8,128)(2,1)S(1)}, u32[]{:S(2)}, u32[]{:S(2)}) collective-permute-start(bf16[768,128]{1,0:T(8,128)(2,1)S(1)} %get-tuple-element.24.refs_12_), channel_id=1, source_target_pairs={{0,1},{1,0},{2,3},{3,2},{4,5},{5,4},{6,7},{7,6},{8,9},{9,8},{10,11... | collective-permute-start | bytes 589832 | tf_op jit(solution)/shard_map/ppermute | solution.py:21
  23.0 13.9 %collective-permute-start.9 = (bf16[768,128]{1,0:T(8,128)(2,1)S(1)}, bf16[768,128]{1,0:T(8,128)(2,1)S(1)}, u32[]{:S(2)}, u32[]{:S(2)}) collective-permute-start(bf16[768,128]{1,0:T(8,128)(2,1)S(1)} %get-tuple-element.23.refs_11_), channel_id=1, source_target_pairs={{0,1},{1,0},{2,3},{3,2},{4,5},{5,4},{6,7},{7,6},{8,9},{9,8},{10,11... | collective-permute-start | bytes 589832 | tf_op jit(solution)/shard_map/ppermute | solution.py:21
  28.2 13.8 %collective-permute-start.11 = (f32[256,128]{1,0:T(8,128)S(1)}, f32[256,128]{1,0:T(8,128)S(1)}, u32[]{:S(2)}, u32[]{:S(2)}) collective-permute-start(f32[256,128]{1,0:T(8,128)S(1)} %get-tuple-element.32), channel_id=1, source_target_pairs={{0,2},{1,3},{2,0},{3,1},{4,6},{5,7},{6,4},{7,5},{8,10},{9,11},{10,... | collective-permute-start | bytes 393224 | tf_op jit(solution)/shard_map/ppermute | solution.py:21
  32.2 7.3 %collective-permute-start.13 = (f32[64,128]{1,0:T(8,128)S(1)}, f32[64,128]{1,0:T(8,128)S(1)}, u32[]{:S(2)}, u32[]{:S(2)}) collective-permute-start(f32[64,128]{1,0:T(8,128)S(1)} %get-tuple-element.34), channel_id=1, source_target_pairs={{0,2},{1,3},{2,0},{3,1},{4,6},{5,7},{6,4},{7,5},{8,10},{9,11},{10,... | collective-permute-start | bytes 98312 | tf_op jit(solution)/shard_map/ppermute | solution.py:21
  37.2 4.9 %collective-permute-start.12 = (f32[64,128]{1,0:T(8,128)S(1)}, f32[64,128]{1,0:T(8,128)S(1)}, u32[]{:S(2)}, u32[]{:S(2)}) collective-permute-start(f32[64,128]{1,0:T(8,128)S(1)} %get-tuple-element.33), channel_id=1, source_target_pairs={{0,2},{1,3},{2,0},{3,1},{4,6},{5,7},{6,4},{7,5},{8,10},{9,11},{10,... | collective-permute-start | bytes 98312 | tf_op jit(solution)/shard_map/ppermute | solution.py:21

commit v5 on v4

--- a/solution.py
+++ b/solution.py
@@ -77,24 +77,13 @@
     return places, [(tile_dev - 1) * slots * width] + [slots * size] * PARTS
 
 
-def cut_kernel(whole, amplitudes, lists, counts, *refs):
-    arrays, (amplitudes_out, table, lists_v, counts_s, sems) = refs[:1 + PARTS], refs[1 + PARTS:]
-    head = arrays[0]
-    tile_dev, slots, width, _ = whole.shape
-    places, sizes = split(tile_dev, slots, width)
-    small = [(lists, lists_v), (counts, counts_s)]
-    large = [(amplitudes, amplitudes_out)]
-    for a, parts in enumerate(places):
-        done = 0
-        for array, first, size in parts:
-            target = arrays[array]
-            if size == width:
-                large.append((whole.at[a], target.at[pl.ds(first, slots * size)].reshape(slots, size, whole.shape[3])))
-                continue
-            for s in range(slots):
-                large.append((whole.at[a, s, pl.ds(done, size)], target.at[pl.ds(first + s * size, size)]))
-            done += size
-    copies = [pltpu.make_async_copy(x, y, sems.at[n]) for n, (x, y) in enumerate(small + large)]
+def head_cut_kernel(whole, lists, counts, head, table, lists_v, counts_s, sems):
+    tile_dev, slots, width, depth = whole.shape
+    pairs = [(lists, lists_v), (counts, counts_s)]
+    for a in range(tile_dev - 1):
+        rows = slots * width
+        pairs.append((whole.at[a], head.at[pl.ds(a * rows, rows)].reshape(slots, width, depth)))
+    copies = [pltpu.make_async_copy(x, y, sems.at[n]) for n, (x, y) in enumerate(pairs)]
     for copy in copies:
         copy.start()
     for copy in copies[:2]:
@@ -105,32 +94,59 @@
         values = jnp.where(lane == a, counts_s[a], values)
     table[...] = values
     table[:tile_dev, :slots] = lists_v[...]
-    head[sizes[0]:] = table[...].astype(jnp.float32).astype(head.dtype)
+    head[(tile_dev - 1) * slots * width:] = table[...].astype(jnp.float32).astype(head.dtype)
     for copy in copies[2:]:
+        copy.wait()
+
+
+def rest_cut_kernel(whole, amplitudes, *refs):
+    parts, (amplitudes_out, sems) = refs[:PARTS], refs[PARTS:]
+    tile_dev, slots, width, _ = whole.shape
+    size = width // PARTS
+    pairs = [(amplitudes, amplitudes_out)]
+    for n, part in enumerate(parts):
+        for s in range(slots):
+            pairs.append((whole.at[tile_dev - 1, s, pl.ds(n * size, size)], part.at[pl.ds(s * size, size)]))
+    copies = [pltpu.make_async_copy(x, y, sems.at[n]) for n, (x, y) in enumerate(pairs)]
+    for copy in copies:
+        copy.start()
+    for copy in copies:
         copy.wait()
 
 
 def cut(whole, amplitudes, lists, counts):
     tile_dev, slots, width, depth = whole.shape
     sizes = split(tile_dev, slots, width)[1]
-    placed = [pltpu.with_memory_space_constraint(x, pltpu.HBM) for x in (whole, amplitudes, lists, counts)]
-    return pl.pallas_call(
-        cut_kernel,
+    whole, amplitudes, lists, counts = (
+        pltpu.with_memory_space_constraint(x, pltpu.HBM) for x in (whole, amplitudes, lists, counts)
+    )
+    params = pltpu.CompilerParams(vmem_limit_bytes=VMEM_BYTES)
+    head, table = pl.pallas_call(
+        head_cut_kernel,
         out_shape=(
             jax.ShapeDtypeStruct((sizes[0] + TABLE_ROWS, depth), whole.dtype),
-            *(jax.ShapeDtypeStruct((size, depth), whole.dtype) for size in sizes[1:]),
-            jax.ShapeDtypeStruct(amplitudes.shape, amplitudes.dtype),
             jax.ShapeDtypeStruct((TABLE_ROWS, depth), jnp.int32),
         ),
-        in_specs=[HBM] * 4,
-        out_specs=(VMEM,) * (3 + PARTS),
+        in_specs=[HBM] * 3,
+        out_specs=(VMEM,) * 2,
         scratch_shapes=[
             pltpu.VMEM(lists.shape, lists.dtype),
             pltpu.SMEM(counts.shape, counts.dtype),
-            pltpu.SemaphoreType.DMA((3 + (tile_dev - 1) + PARTS * slots,)),
+            pltpu.SemaphoreType.DMA((1 + tile_dev,)),
         ],
-        compiler_params=pltpu.CompilerParams(vmem_limit_bytes=VMEM_BYTES),
-    )(*placed)
+        compiler_params=params,
+    )(whole, lists, counts)
+    *parts, amplitudes = pl.pallas_call(
+        rest_cut_kernel,
+        out_shape=(jax.ShapeDtypeStruct((sizes[1], depth), whole.dtype),) * PARTS
+        + (jax.ShapeDtypeStruct(amplitudes.shape, amplitudes.dtype),),
+        in_specs=[HBM] * 2,
+        out_specs=(VMEM,) * (1 + PARTS),
+        scratch_shapes=[pltpu.SemaphoreType.DMA((1 + PARTS * slots,))],
+        compiler_params=params,
+        cost_estimate=pl.CostEstimate(flops=2**20, bytes_accessed=2**19, transcendentals=0),
+    )(whole, amplitudes)
+    return [head, *parts, amplitudes, table]
 
 
 def stack_kernel(first, second, out):

time: 43.1 us -> 43 us (level)
  Pallas kernels: 9.08 us -> 10.7 us
  starting transfers between devices: 16.2 us -> 15.3 us
  waiting for transfers between devices: 17.4 us -> 16.6 us
    ppermute x14, starting transfers between devices: 16.2 us -> 15.3 us  [shift(): return lax.ppermute(value, axis, [(j, j ^ mask) for j in range(size)])]
    pallas_call x1 -> x2, Pallas kernels: 1.47 us -> 2.36 us  [the longest x1 1.2 us: cut(): pl.pallas_call(rest_cut_kernel, out_shape=(jax.ShapeDtypeStruct((sizes[1]...]
    ppermute x14, waiting for transfers between devices: 17.4 us -> 16.6 us  [shift(): return lax.ppermute(value, axis, [(j, j ^ mask) for j in range(size)])]
    pallas_call x1, Pallas kernels: 2.72 us -> 3.19 us  [on_pairs(): call(lambda *refs: own_kernel(masks, slots, *refs), (f32(before, 2 * rows...]
  transfers between devices with their start and end apart: 14 -> 14, of which waited for: 8 -> 6; matrix products, arithmetic and copies ran while one was open for 0% -> 0% of each run, Pallas kernels for 19% -> 23%
where the time goes in v5:
time: 43 us; the launch traced here: 42.8 us
  waiting for transfers between devices  16.6 us (39%)
  starting transfers between devices  15.3 us (36%)
  Pallas kernels  10.7 us (25%)
    ppermute x14, waiting for transfers between devices, shift(): return lax.ppermute(value, axis, [(j, j ^ mask) for j in range(size)])  16.6 us
    ppermute x14, starting transfers between devices, shift(): return lax.ppermute(value, axis, [(j, j ^ mask) for j in range(size)])  15.3 us
    pallas_call x1, Pallas kernels, on_pairs(): call(lambda *refs: own_kernel(masks, slots, *refs), (f32(before, 2 * rows...  3.19 us
    pallas_call x1, Pallas kernels, on_pairs(): call(lambda *refs: head_kernel(slots, *refs), (part, part, jax.ShapeDtype...  2.22 us
    pallas_call x1, Pallas kernels, on_pairs(): call(lambda *refs: pick_kernel(before, slots, *refs), jax.ShapeDtypeStruc...  1.39 us
    pallas_call x1, Pallas kernels, cut(): pl.pallas_call(rest_cut_kernel, out_shape=(jax.ShapeDtypeStruct((sizes[1]...  1.2 us
    pallas_call x1, Pallas kernels, cut(): pl.pallas_call(head_cut_kernel, out_shape=(jax.ShapeDtypeStruct((sizes[0]...  1.16 us
  transfers between devices with their start and end apart: 14, of which 6 were waited for; matrix products, arithmetic and copies ran while one was open for 0% of the time, Pallas kernels for 23%

profile of v5, /device:TPU:0, one launch (start us, length us, event | category | flops | bytes accessed | tf_op | source)
XLA Modules:
  0.0 42.8 jit_solution(15393057206172346358)
XLA Ops:
  0.0 4.0 %collective-permute-start = (bf16[3,128,128]{2,1,0:T(8,128)(2,1)}, bf16[3,128,128]{2,1,0:T(8,128)(2,1)S(1)}, u32[]{:S(2)}, u32[]{:S(2)}) collective-permute-start(bf16[3,128,128]{2,1,0:T(8,128)(2,1)} %amplitudes.1), channel_id=1, source_target_pairs={{0,2},{1,3},{2,0},{3,1},{4,6},{5,7},{6,4},{7,5},{8,10},{9,11},{10,... | collective-permute-start | bytes 294920 | tf_op jit(solution)/shard_map/ppermute | solution.py:21
  4.0 1.2 %shard_map.46 = (bf16[3088,128]{1,0:T(8,128)(2,1)S(1)}, s32[16,128]{1,0:T(8,128)S(1)}) custom-call(bf16[3,12,128,128]{3,2,1,0:T(8,128)(2,1)} %whole.3, s32[3,12]{1,0:T(4,128)} %lists.1, s32[3]{0:T(128)} %counts.1), custom_call_target="tpu_custom_call" | custom-call | tf_op jit(solution)/shard_map/pallas_call | solution.py:124
  5.2 1.6 %collective-permute-start.8 = (bf16[3088,128]{1,0:T(8,128)(2,1)S(1)}, bf16[3088,128]{1,0:T(8,128)(2,1)S(1)}, u32[]{:S(2)}, u32[]{:S(2)}) collective-permute-start(bf16[3088,128]{1,0:T(8,128)(2,1)S(1)} %get-tuple-element.22.refs_10_), channel_id=1, source_target_pairs={{0,1},{1,0},{2,3},{3,2},{4,5},{5,4},{6,7},{7,6},{8,9},{9,8},{10,11... | collective-permute-start | bytes 2371592 | tf_op jit(solution)/shard_map/ppermute | solution.py:21
  6.9 1.2 %shard_map.47 = (bf16[768,128]{1,0:T(8,128)(2,1)S(1)}, bf16[768,128]{1,0:T(8,128)(2,1)S(1)}, bf16[3,128,128]{2,1,0:T(8,128)(2,1)S(1)}) custom-call(bf16[3,12,128,128]{3,2,1,0:T(8,128)(2,1)} %whole.3, bf16[3,128,128]{2,1,0:T(8,128)(2,1)} %amplitudes.1), custom_call_target="tpu_custom_call" | custom-call | flops 1048576 | bytes 524288 | tf_op jit(solution)/shard_map/pallas_call | solution.py:139
  8.1 1.0 %collective-permute-done.second = bf16[3,128,128]{2,1,0:T(8,128)(2,1)S(1)} collective-permute-done((bf16[3,128,128]{2,1,0:T(8,128)(2,1)}, bf16[3,128,128]{2,1,0:T(8,128)(2,1)S(1)}, u32[]{:S(2)}, u32[]{:S(2)}) %collective-permute-start) | collective-permute-done | bytes 98336 | tf_op jit(solution)/shard_map/ppermute | solution.py:21
  9.1 1.8 %collective-permute-start.2 = (bf16[2,3,128,128]{3,2,1,0:T(8,128)(2,1)S(1)}, bf16[2,3,128,128]{3,2,1,0:T(8,128)(2,1)S(1)}, u32[]{:S(2)}, u32[]{:S(2)}) collective-permute-start(bf16[2,3,128,128]{3,2,1,0:T(8,128)(2,1)S(1)} %shard_map.48.refs_2_), channel_id=1, source_target_pairs={{0,8},{4,12},{8,0},{12,4},{16,24},{20,28},{24,16},{28,20},{1,9},{5... | collective-permute-start | bytes 589832 | tf_op jit(solution)/shard_map/ppermute | solution.py:21
  10.9 1.5 %collective-permute-start.4 = (bf16[2,3,128,128]{3,2,1,0:T(8,128)(2,1)S(1)}, bf16[2,3,128,128]{3,2,1,0:T(8,128)(2,1)S(1)}, u32[]{:S(2)}, u32[]{:S(2)}) collective-permute-start(bf16[2,3,128,128]{3,2,1,0:T(8,128)(2,1)S(1)} %shard_map.48.refs_2_), channel_id=1, source_target_pairs={{0,16},{4,20},{8,24},{12,28},{16,0},{20,4},{24,8},{28,12},{1,17},{... | collective-permute-start | bytes 589832 | tf_op jit(solution)/shard_map/ppermute | solution.py:21
  12.4 0.2 collective-permute-start.6
  12.6 4.0 %collective-permute-done.2.refs_4_ = bf16[2,3,128,128]{3,2,1,0:T(8,128)(2,1)S(1)} collective-permute-done((bf16[2,3,128,128]{3,2,1,0:T(8,128)(2,1)S(1)}, bf16[2,3,128,128]{3,2,1,0:T(8,128)(2,1)S(1)}, u32[]{:S(2)}, u32[]{:S(2)}) %collective-permute-start.2) | collective-permute-done | bytes 196640 | tf_op jit(solution)/shard_map/ppermute | solution.py:21
  16.6 3.4 %collective-permute-done.4.refs_6_ = bf16[2,3,128,128]{3,2,1,0:T(8,128)(2,1)S(1)} collective-permute-done((bf16[2,3,128,128]{3,2,1,0:T(8,128)(2,1)S(1)}, bf16[2,3,128,128]{3,2,1,0:T(8,128)(2,1)S(1)}, u32[]{:S(2)}, u32[]{:S(2)}) %collective-permute-start.4) | collective-permute-done | bytes 196640 | tf_op jit(solution)/shard_map/ppermute | solution.py:21
  20.0 0.5 %collective-permute-start.7 = (bf16[2,3,128,128]{3,2,1,0:T(8,128)(2,1)S(1)}, bf16[2,3,128,128]{3,2,1,0:T(8,128)(2,1)S(1)}, u32[]{:S(2)}, u32[]{:S(2)}) collective-permute-start(bf16[2,3,128,128]{3,2,1,0:T(8,128)(2,1)S(1)} %collective-permute-done.6.refs_8_), channel_id=1, source_target_pairs={{0,4},{4,0},{8,12},{12,8},{16,20},{20,16},{24,28},{28,24},{1,5},{5... | collective-permute-start | bytes 589832 | tf_op jit(solution)/shard_map/ppermute | solution.py:21
  20.6 2.4 %collective-permute-start.10 = (bf16[768,128]{1,0:T(8,128)(2,1)S(1)}, bf16[768,128]{1,0:T(8,128)(2,1)S(1)}, u32[]{:S(2)}, u32[]{:S(2)}) collective-permute-start(bf16[768,128]{1,0:T(8,128)(2,1)S(1)} %get-tuple-element.24.refs_12_), channel_id=1, source_target_pairs={{0,1},{1,0},{2,3},{3,2},{4,5},{5,4},{6,7},{7,6},{8,9},{9,8},{10,11... | collective-permute-start | bytes 589832 | tf_op jit(solution)/shard_map/ppermute | solution.py:21
  22.9 0.1 collective-permute-start.9
  23.0 3.2 %shard_map.49 = (f32[2,256,128]{2,1,0:T(8,128)S(1)}, f32[128,256]{1,0:T(8,128)S(1)}, bf16[2,24,128,128]{3,2,1,0:T(8,128)(2,1)S(1)}) custom-call(s32[2]{0:T(128)S(1)} %pad_add_fusion.refs_0_, s32[16,128]{1,0:T(8,128)S(1)} %get-tuple-element.20.refs_1_, bf16[2,3,128,128]{3,2,1,0:T(8,128)(2,1)S(1)} %shard_map.48.refs_2_, ...), custom_call_target="tpu_custom_call" | custom-call | flops 3750000128 | bytes 2097152 | tf_op jit(solution)/shard_map/pallas_call | solution.py:282
  26.3 2.2 %shard_map.50 = (f32[256,128]{1,0:T(8,128)S(1)}, f32[256,128]{1,0:T(8,128)S(1)}, s32[16,128]{1,0:T(8,128)S(1)}) custom-call(s32[2]{0:T(128)S(1)} %pad_add_fusion.refs_0_, bf16[2,24,128,128]{3,2,1,0:T(8,128)(2,1)S(1)} %get-tuple-element.25.refs_1_.refs_2_, f32[2,256,128]{2,1,0:T(8,128)S(1)} %get-tuple-element.26.refs_2_, ...), custom_call_target="tpu_custom_call" | custom-call | flops 250000000 | bytes 2097152 | tf_op jit(solution)/shard_map/pallas_call | solution.py:288
  28.5 1.9 %collective-permute-start.11 = (f32[256,128]{1,0:T(8,128)S(1)}, f32[256,128]{1,0:T(8,128)S(1)}, u32[]{:S(2)}, u32[]{:S(2)}) collective-permute-start(f32[256,128]{1,0:T(8,128)S(1)} %get-tuple-element.32), channel_id=1, source_target_pairs={{0,2},{1,3},{2,0},{3,1},{4,6},{5,7},{6,4},{7,5},{8,10},{9,11},{10,... | collective-permute-start | bytes 393224 | tf_op jit(solution)/shard_map/ppermute | solution.py:21
  30.4 1.4 %shard_map.51.refs_1_ = bf16[256,1536]{1,0:T(8,128)(2,1)S(1)} custom-call(s32[2]{0:T(128)S(1)} %pad_add_fusion.refs_0_, s32[16,128]{1,0:T(8,128)S(1)} %get-tuple-element.29.refs_1_, bf16[2,24,128,128]{3,2,1,0:T(8,128)(2,1)S(1)} %get-tuple-element.25.refs_1_.refs_2_), custom_call_target="tpu_custom_call" | custom-call | flops 268435456 | bytes 2097152 | tf_op jit(solution)/shard_map/pallas_call | solution.py:293
  31.8 0.4 shard_map.53
  32.2 1.1 %collective-permute-start.13 = (f32[64,128]{1,0:T(8,128)S(1)}, f32[64,128]{1,0:T(8,128)S(1)}, u32[]{:S(2)}, u32[]{:S(2)}) collective-permute-start(f32[64,128]{1,0:T(8,128)S(1)} %get-tuple-element.34), channel_id=1, source_target_pairs={{0,2},{1,3},{2,0},{3,1},{4,6},{5,7},{6,4},{7,5},{8,10},{9,11},{10,... | collective-permute-start | bytes 98312 | tf_op jit(solution)/shard_map/ppermute | solution.py:21
  33.3 3.5 %collective-permute-done.9.refs_2_ = bf16[768,128]{1,0:T(8,128)(2,1)S(1)} collective-permute-done((bf16[768,128]{1,0:T(8,128)(2,1)S(1)}, bf16[768,128]{1,0:T(8,128)(2,1)S(1)}, u32[]{:S(2)}, u32[]{:S(2)}) %collective-permute-start.9) | collective-permute-done | bytes 196640 | tf_op jit(solution)/shard_map/ppermute | solution.py:21
  36.8 0.4 shard_map.52
  37.2 1.6 %collective-permute-done.13.refs_5_ = f32[64,128]{1,0:T(8,128)S(1)} collective-permute-done((f32[64,128]{1,0:T(8,128)S(1)}, f32[64,128]{1,0:T(8,128)S(1)}, u32[]{:S(2)}, u32[]{:S(2)}) %collective-permute-start.13) | collective-permute-done | bytes 32800 | tf_op jit(solution)/shard_map/ppermute | solution.py:21
  38.8 3.2 %collective-permute-done.12.refs_4_ = f32[64,128]{1,0:T(8,128)S(1)} collective-permute-done((f32[64,128]{1,0:T(8,128)S(1)}, f32[64,128]{1,0:T(8,128)S(1)}, u32[]{:S(2)}, u32[]{:S(2)}) %collective-permute-start.12) | collective-permute-done | bytes 32800 | tf_op jit(solution)/shard_map/ppermute | solution.py:21
  42.0 0.8 %shard_map.54 = f32[128,384]{1,0:T(8,128)} custom-call(f32[256,128]{1,0:T(8,128)S(1)} %get-tuple-element.27.refs_0_, f32[64,128]{1,0:T(8,128)S(1)} %get-tuple-element.30.refs_1_, f32[64,128]{1,0:T(8,128)S(1)} %get-tuple-element.31.refs_2_, f32[256,128]{1,0:T(8,128)S(1)} %collective-permute-done.11.refs_3_, f32[64,128]{1,0:T(8,128)S(1)} %collective-permute-done.12.refs_4_, ...), custom_call_target="tpu_custom_call" | custom-call | flops 1048576 | bytes 2097152 | tf_op jit(solution)/shard_map/pallas_call | solution.py:305
  (14 shorter events, 0.2 us)
Async XLA Ops:
  0.0 9.1 %collective-permute-start = (bf16[3,128,128]{2,1,0:T(8,128)(2,1)}, bf16[3,128,128]{2,1,0:T(8,128)(2,1)S(1)}, u32[]{:S(2)}, u32[]{:S(2)}) collective-permute-start(bf16[3,128,128]{2,1,0:T(8,128)(2,1)} %amplitudes.1), channel_id=1, source_target_pairs={{0,2},{1,3},{2,0},{3,1},{4,6},{5,7},{6,4},{7,5},{8,10},{9,11},{10,... | collective-permute-start | bytes 294920 | tf_op jit(solution)/shard_map/ppermute | solution.py:21
  5.2 21.0 %collective-permute-start.8 = (bf16[3088,128]{1,0:T(8,128)(2,1)S(1)}, bf16[3088,128]{1,0:T(8,128)(2,1)S(1)}, u32[]{:S(2)}, u32[]{:S(2)}) collective-permute-start(bf16[3088,128]{1,0:T(8,128)(2,1)S(1)} %get-tuple-element.22.refs_10_), channel_id=1, source_target_pairs={{0,1},{1,0},{2,3},{3,2},{4,5},{5,4},{6,7},{7,6},{8,9},{9,8},{10,11... | collective-permute-start | bytes 2371592 | tf_op jit(solution)/shard_map/ppermute | solution.py:21
  9.1 7.6 %collective-permute-start.2 = (bf16[2,3,128,128]{3,2,1,0:T(8,128)(2,1)S(1)}, bf16[2,3,128,128]{3,2,1,0:T(8,128)(2,1)S(1)}, u32[]{:S(2)}, u32[]{:S(2)}) collective-permute-start(bf16[2,3,128,128]{3,2,1,0:T(8,128)(2,1)S(1)} %shard_map.48.refs_2_), channel_id=1, source_target_pairs={{0,8},{4,12},{8,0},{12,4},{16,24},{20,28},{24,16},{28,20},{1,9},{5... | collective-permute-start | bytes 589832 | tf_op jit(solution)/shard_map/ppermute | solution.py:21
  10.9 9.1 %collective-permute-start.4 = (bf16[2,3,128,128]{3,2,1,0:T(8,128)(2,1)S(1)}, bf16[2,3,128,128]{3,2,1,0:T(8,128)(2,1)S(1)}, u32[]{:S(2)}, u32[]{:S(2)}) collective-permute-start(bf16[2,3,128,128]{3,2,1,0:T(8,128)(2,1)S(1)} %shard_map.48.refs_2_), channel_id=1, source_target_pairs={{0,16},{4,20},{8,24},{12,28},{16,0},{20,4},{24,8},{28,12},{1,17},{... | collective-permute-start | bytes 589832 | tf_op jit(solution)/shard_map/ppermute | solution.py:21
  12.4 7.6 %collective-permute-start.6 = (bf16[2,3,128,128]{3,2,1,0:T(8,128)(2,1)S(1)}, bf16[2,3,128,128]{3,2,1,0:T(8,128)(2,1)S(1)}, u32[]{:S(2)}, u32[]{:S(2)}) collective-permute-start(bf16[2,3,128,128]{3,2,1,0:T(8,128)(2,1)S(1)} %shard_map.48.refs_2_), channel_id=1, source_target_pairs={{0,24},{4,28},{8,16},{12,20},{16,8},{20,12},{24,0},{28,4},{1,25},{... | collective-permute-start | bytes 589832 | tf_op jit(solution)/shard_map/ppermute | solution.py:21
  12.6 8.0 %collective-permute-start.1 = (bf16[2,3,128,128]{3,2,1,0:T(8,128)(2,1)S(1)}, bf16[2,3,128,128]{3,2,1,0:T(8,128)(2,1)S(1)}, u32[]{:S(2)}, u32[]{:S(2)}) collective-permute-start(bf16[2,3,128,128]{3,2,1,0:T(8,128)(2,1)S(1)} %shard_map.48.refs_2_), channel_id=1, source_target_pairs={{0,4},{4,0},{8,12},{12,8},{16,20},{20,16},{24,28},{28,24},{1,5},{5... | collective-permute-start | bytes 589832 | tf_op jit(solution)/shard_map/ppermute | solution.py:21
  16.6 6.3 %collective-permute-start.3 = (bf16[2,3,128,128]{3,2,1,0:T(8,128)(2,1)S(1)}, bf16[2,3,128,128]{3,2,1,0:T(8,128)(2,1)S(1)}, u32[]{:S(2)}, u32[]{:S(2)}) collective-permute-start(bf16[2,3,128,128]{3,2,1,0:T(8,128)(2,1)S(1)} %collective-permute-done.2.refs_4_), channel_id=1, source_target_pairs={{0,4},{4,0},{8,12},{12,8},{16,20},{20,16},{24,28},{28,24},{1,5},{5... | collective-permute-start | bytes 589832 | tf_op jit(solution)/shard_map/ppermute | solution.py:21
  20.0 3.0 %collective-permute-start.5 = (bf16[2,3,128,128]{3,2,1,0:T(8,128)(2,1)S(1)}, bf16[2,3,128,128]{3,2,1,0:T(8,128)(2,1)S(1)}, u32[]{:S(2)}, u32[]{:S(2)}) collective-permute-start(bf16[2,3,128,128]{3,2,1,0:T(8,128)(2,1)S(1)} %collective-permute-done.4.refs_6_), channel_id=1, source_target_pairs={{0,4},{4,0},{8,12},{12,8},{16,20},{20,16},{24,28},{28,24},{1,5},{5... | collective-permute-start | bytes 589832 | tf_op jit(solution)/shard_map/ppermute | solution.py:21
  20.0 3.0 %collective-permute-start.7 = (bf16[2,3,128,128]{3,2,1,0:T(8,128)(2,1)S(1)}, bf16[2,3,128,128]{3,2,1,0:T(8,128)(2,1)S(1)}, u32[]{:S(2)}, u32[]{:S(2)}) collective-permute-start(bf16[2,3,128,128]{3,2,1,0:T(8,128)(2,1)S(1)} %collective-permute-done.6.refs_8_), channel_id=1, source_target_pairs={{0,4},{4,0},{8,12},{12,8},{16,20},{20,16},{24,28},{28,24},{1,5},{5... | collective-permute-start | bytes 589832 | tf_op jit(solution)/shard_map/ppermute | solution.py:21
  20.6 11.2 %collective-permute-start.10 = (bf16[768,128]{1,0:T(8,128)(2,1)S(1)}, bf16[768,128]{1,0:T(8,128)(2,1)S(1)}, u32[]{:S(2)}, u32[]{:S(2)}) collective-permute-start(bf16[768,128]{1,0:T(8,128)(2,1)S(1)} %get-tuple-element.24.refs_12_), channel_id=1, source_target_pairs={{0,1},{1,0},{2,3},{3,2},{4,5},{5,4},{6,7},{7,6},{8,9},{9,8},{10,11... | collective-permute-start | bytes 589832 | tf_op jit(solution)/shard_map/ppermute | solution.py:21
  22.9 13.8 %collective-permute-start.9 = (bf16[768,128]{1,0:T(8,128)(2,1)S(1)}, bf16[768,128]{1,0:T(8,128)(2,1)S(1)}, u32[]{:S(2)}, u32[]{:S(2)}) collective-permute-start(bf16[768,128]{1,0:T(8,128)(2,1)S(1)} %get-tuple-element.23.refs_11_), channel_id=1, source_target_pairs={{0,1},{1,0},{2,3},{3,2},{4,5},{5,4},{6,7},{7,6},{8,9},{9,8},{10,11... | collective-permute-start | bytes 589832 | tf_op jit(solution)/shard_map/ppermute | solution.py:21
  28.5 13.5 %collective-permute-start.11 = (f32[256,128]{1,0:T(8,128)S(1)}, f32[256,128]{1,0:T(8,128)S(1)}, u32[]{:S(2)}, u32[]{:S(2)}) collective-permute-start(f32[256,128]{1,0:T(8,128)S(1)} %get-tuple-element.32), channel_id=1, source_target_pairs={{0,2},{1,3},{2,0},{3,1},{4,6},{5,7},{6,4},{7,5},{8,10},{9,11},{10,... | collective-permute-start | bytes 393224 | tf_op jit(solution)/shard_map/ppermute | solution.py:21
  32.2 6.6 %collective-permute-start.13 = (f32[64,128]{1,0:T(8,128)S(1)}, f32[64,128]{1,0:T(8,128)S(1)}, u32[]{:S(2)}, u32[]{:S(2)}) collective-permute-start(f32[64,128]{1,0:T(8,128)S(1)} %get-tuple-element.34), channel_id=1, source_target_pairs={{0,2},{1,3},{2,0},{3,1},{4,6},{5,7},{6,4},{7,5},{8,10},{9,11},{10,... | collective-permute-start | bytes 98312 | tf_op jit(solution)/shard_map/ppermute | solution.py:21
  37.1 4.9 %collective-permute-start.12 = (f32[64,128]{1,0:T(8,128)S(1)}, f32[64,128]{1,0:T(8,128)S(1)}, u32[]{:S(2)}, u32[]{:S(2)}) collective-permute-start(f32[64,128]{1,0:T(8,128)S(1)} %get-tuple-element.33), channel_id=1, source_target_pairs={{0,2},{1,3},{2,0},{3,1},{4,6},{5,7},{6,4},{7,5},{8,10},{9,11},{10,... | collective-permute-start | bytes 98312 | tf_op jit(solution)/shard_map/ppermute | solution.py:21

commit v6 on v5

--- a/solution.py
+++ b/solution.py
@@ -9,6 +9,7 @@
 UNROLL = 4
 OWN_FLOPS = 3750000000
 HEAD_FLOPS = 250000000
+SOON = 4
 TABLE_ROWS = 16
 PARTS = 2
 SMEM = pl.BlockSpec(memory_space=pltpu.SMEM)
@@ -189,9 +190,9 @@
             sums_ref[a] = total
 
 
-def head_kernel(slots, place_ref, stage, sums_ref, others, own_ref, far_ref, table_v, table, sem):
+def head_kernel(slots, place_ref, stage, sums_ref, others, own_ref, soon_ref, late_ref, table_v, table, sem):
     before, both, width = sums_ref.shape
-    rows = both // 2
+    rows, soon = both // 2, soon_ref.shape[0]
     places, sizes = split(before + 1, slots, width)
     table_v[...] = others[sizes[0]:].astype(jnp.float32).astype(jnp.int32)
     copy = pltpu.make_async_copy(table_v, table, sem)
@@ -201,7 +202,12 @@
         live = live_slots(table, a, place_ref[1] ^ 1, slots)
         total = contract(sums_ref[a], table, a, live, slots, stage, blocks_at((others,), places[a]))
         own_ref[a * rows:(a + 1) * rows] = total[:rows]
-        far_ref[a * rows:(a + 1) * rows] = total[rows:]
+        cut_at = min(max(soon - a * rows, 0), rows)
+        if cut_at > 0:
+            soon_ref[a * rows:a * rows + cut_at] = total[rows:rows + cut_at]
+        if cut_at < rows:
+            first = a * rows + cut_at - soon
+            late_ref[first:first + rows - cut_at] = total[rows + cut_at:]
 
 
 def pick_kernel(a, slots, place_ref, table_v, stage, picked, table, sem):
@@ -229,14 +235,21 @@
 
 
 def join_kernel(*refs):
-    own, got, out = refs[:1 + PARTS], refs[1 + PARTS:-1], refs[-1]
-    rows = out.shape[0]
+    own, soon_ref, late_ref, got, out = refs[:1 + PARTS], refs[1 + PARTS], refs[2 + PARTS], refs[3 + PARTS:-1], refs[-1]
+    rows, soon = out.shape[0], soon_ref.shape[0]
     before = own[0].shape[0] // rows
     width = out.shape[1] // (before + 1)
     for a in range(before):
-        part = pl.ds(a * rows, rows)
-        out[:, a * width:(a + 1) * width] = own[0][part] + got[0][part]
-    last = jnp.concatenate([own[n][...] + got[n][...] for n in range(1, 1 + PARTS)], axis=0)
+        columns = slice(a * width, (a + 1) * width)
+        cut_at = min(max(soon - a * rows, 0), rows)
+        if cut_at > 0:
+            part = slice(a * rows, a * rows + cut_at)
+            out[:cut_at, columns] = own[0][part] + soon_ref[part]
+        if cut_at < rows:
+            first = a * rows + cut_at - soon
+            came = late_ref[first:first + rows - cut_at]
+            out[cut_at:, columns] = own[0][a * rows + cut_at:(a + 1) * rows] + came
+    last = jnp.concatenate([own[1 + n][...] + got[n][...] for n in range(PARTS)], axis=0)
     out[:, before * width:] = jnp.transpose(last)
 
 
@@ -284,10 +297,13 @@
         (f32(before, 2 * rows, width), f32(width, 2 * rows), jax.ShapeDtypeStruct((2, tiles, rows, depth), far.dtype)),
         1, len(pieces) + 2 + PARTS, scratch, OWN_FLOPS,
     )(place, table, *pieces, *arrays)
-    part = f32(before * rows, width)
-    own, away, table = call(
+    soon = before * rows * SOON // 8
+    own, *away, table = call(
         lambda *refs: head_kernel(slots, *refs),
-        (part, part, jax.ShapeDtypeStruct(table.shape, table.dtype)),
+        (
+            f32(before * rows, width), f32(soon, width), f32(before * rows - soon, width),
+            jax.ShapeDtypeStruct(table.shape, table.dtype),
+        ),
         1, 3, scratch, HEAD_FLOPS,
     )(place, stage, sums, others[0])
     picked = call(
@@ -295,14 +311,14 @@
         jax.ShapeDtypeStruct((2 * rows, slots * depth), far.dtype),
         1, 2, scratch, 2**28,
     )(place, table, stage)
-    owns, gots = [own], [shift(away, "oo", n_oo, 2)]
+    owns, gots = [own], [shift(x, "oo", n_oo, 2) for x in away]
     for n in range(PARTS):
         own, away = call(
             lambda *refs, n=n: tail_kernel(slots, n, *refs), (f32(width // PARTS, rows),) * 2, 0, 3, [], 2**28
         )(last, picked, others[1 + n])
         owns.append(own)
         gots.append(shift(away, "oo", n_oo, 2))
-    return call(join_kernel, f32(rows, tile_dev * width), 0, 2 * (1 + PARTS), [], 2**20)(*owns, *gots)
+    return call(join_kernel, f32(rows, tile_dev * width), 0, 3 + 2 * PARTS, [], 2**20)(*owns, *gots)
 
 
 def on_device(amplitudes, tile_counts, tile_lists, integrals, n_vv, n_oo):

time: 43 us -> 42.5 us (0.988)
  waiting for transfers between devices: 16.6 us -> 12.8 us
  starting transfers between devices: 15.3 us -> 18.2 us
  Pallas kernels: 10.7 us -> 11.4 us
    ppermute x14 -> x15, waiting for transfers between devices: 16.6 us -> 12.8 us  [shift(): return lax.ppermute(value, axis, [(j, j ^ mask) for j in range(size)])]
    ppermute x14 -> x15, starting transfers between devices: 15.3 us -> 18.2 us  [shift(): return lax.ppermute(value, axis, [(j, j ^ mask) for j in range(size)])]
    pallas_call x2, Pallas kernels: 3.01 us -> 3.48 us  [the longest x1 2.7 us: on_pairs(): call(lambda *refs: head_kernel(slots, *refs), (f32(before * rows, width),...]
  transfers between devices with their start and end apart: 14 -> 15, of which waited for: 6 -> 5; matrix products, arithmetic and copies ran while one was open for 0% -> 0% of each run, Pallas kernels for 23% -> 25%
where the time goes in v6:
time: 42.5 us; the launch traced here: 42.6 us
  starting transfers between devices  18.2 us (43%)
  waiting for transfers between devices  12.8 us (30%)
  Pallas kernels  11.4 us (27%)
    ppermute x15, starting transfers between devices, shift(): return lax.ppermute(value, axis, [(j, j ^ mask) for j in range(size)])  18.2 us
    ppermute x15, waiting for transfers between devices, shift(): return lax.ppermute(value, axis, [(j, j ^ mask) for j in range(size)])  12.8 us
    pallas_call x1, Pallas kernels, on_pairs(): call(lambda *refs: own_kernel(masks, slots, *refs), (f32(before, 2 * rows...  3.43 us
    pallas_call x1, Pallas kernels, on_pairs(): call(lambda *refs: head_kernel(slots, *refs), (f32(before * rows, width),...  2.7 us
    pallas_call x1, Pallas kernels, on_pairs(): call(lambda *refs: pick_kernel(before, slots, *refs), jax.ShapeDtypeStruc...  1.39 us
    pallas_call x1, Pallas kernels, cut(): pl.pallas_call(rest_cut_kernel, out_shape=(jax.ShapeDtypeStruct((sizes[1]...  1.2 us
    pallas_call x1, Pallas kernels, cut(): pl.pallas_call(head_cut_kernel, out_shape=(jax.ShapeDtypeStruct((sizes[0]...  1.16 us
  transfers between devices with their start and end apart: 15, of which 5 were waited for; matrix products, arithmetic and copies ran while one was open for 0% of the time, Pallas kernels for 25%

profile of v6, /device:TPU:0, one launch (start us, length us, event | category | flops | bytes accessed | tf_op | source)
XLA Modules:
  0.0 42.6 jit_solution(11067802002258806744)
XLA Ops:
  0.0 4.0 %collective-permute-start = (bf16[3,128,128]{2,1,0:T(8,128)(2,1)}, bf16[3,128,128]{2,1,0:T(8,128)(2,1)S(1)}, u32[]{:S(2)}, u32[]{:S(2)}) collective-permute-start(bf16[3,128,128]{2,1,0:T(8,128)(2,1)} %amplitudes.1), channel_id=1, source_target_pairs={{0,2},{1,3},{2,0},{3,1},{4,6},{5,7},{6,4},{7,5},{8,10},{9,11},{10,... | collective-permute-start | bytes 294920 | tf_op jit(solution)/shard_map/ppermute | solution.py:22
  4.0 1.2 %shard_map.46 = (bf16[3088,128]{1,0:T(8,128)(2,1)S(1)}, s32[16,128]{1,0:T(8,128)S(1)}) custom-call(bf16[3,12,128,128]{3,2,1,0:T(8,128)(2,1)} %whole.3, s32[3,12]{1,0:T(4,128)} %lists.1, s32[3]{0:T(128)} %counts.1), custom_call_target="tpu_custom_call" | custom-call | tf_op jit(solution)/shard_map/pallas_call | solution.py:125
  5.2 1.6 %collective-permute-start.8 = (bf16[3088,128]{1,0:T(8,128)(2,1)S(1)}, bf16[3088,128]{1,0:T(8,128)(2,1)S(1)}, u32[]{:S(2)}, u32[]{:S(2)}) collective-permute-start(bf16[3088,128]{1,0:T(8,128)(2,1)S(1)} %get-tuple-element.23.refs_10_), channel_id=1, source_target_pairs={{0,1},{1,0},{2,3},{3,2},{4,5},{5,4},{6,7},{7,6},{8,9},{9,8},{10,11... | collective-permute-start | bytes 2371592 | tf_op jit(solution)/shard_map/ppermute | solution.py:22
  6.9 1.2 %shard_map.47 = (bf16[768,128]{1,0:T(8,128)(2,1)S(1)}, bf16[768,128]{1,0:T(8,128)(2,1)S(1)}, bf16[3,128,128]{2,1,0:T(8,128)(2,1)S(1)}) custom-call(bf16[3,12,128,128]{3,2,1,0:T(8,128)(2,1)} %whole.3, bf16[3,128,128]{2,1,0:T(8,128)(2,1)} %amplitudes.1), custom_call_target="tpu_custom_call" | custom-call | flops 1048576 | bytes 524288 | tf_op jit(solution)/shard_map/pallas_call | solution.py:140
  8.1 1.0 %collective-permute-done.second = bf16[3,128,128]{2,1,0:T(8,128)(2,1)S(1)} collective-permute-done((bf16[3,128,128]{2,1,0:T(8,128)(2,1)}, bf16[3,128,128]{2,1,0:T(8,128)(2,1)S(1)}, u32[]{:S(2)}, u32[]{:S(2)}) %collective-permute-start) | collective-permute-done | bytes 98336 | tf_op jit(solution)/shard_map/ppermute | solution.py:22
  9.1 1.8 %collective-permute-start.2 = (bf16[2,3,128,128]{3,2,1,0:T(8,128)(2,1)S(1)}, bf16[2,3,128,128]{3,2,1,0:T(8,128)(2,1)S(1)}, u32[]{:S(2)}, u32[]{:S(2)}) collective-permute-start(bf16[2,3,128,128]{3,2,1,0:T(8,128)(2,1)S(1)} %shard_map.48.refs_2_), channel_id=1, source_target_pairs={{0,8},{4,12},{8,0},{12,4},{16,24},{20,28},{24,16},{28,20},{1,9},{5... | collective-permute-start | bytes 589832 | tf_op jit(solution)/shard_map/ppermute | solution.py:22
  10.9 1.5 %collective-permute-start.4 = (bf16[2,3,128,128]{3,2,1,0:T(8,128)(2,1)S(1)}, bf16[2,3,128,128]{3,2,1,0:T(8,128)(2,1)S(1)}, u32[]{:S(2)}, u32[]{:S(2)}) collective-permute-start(bf16[2,3,128,128]{3,2,1,0:T(8,128)(2,1)S(1)} %shard_map.48.refs_2_), channel_id=1, source_target_pairs={{0,16},{4,20},{8,24},{12,28},{16,0},{20,4},{24,8},{28,12},{1,17},{... | collective-permute-start | bytes 589832 | tf_op jit(solution)/shard_map/ppermute | solution.py:22
  12.4 0.2 collective-permute-start.6
  12.6 4.0 %collective-permute-done.2.refs_4_ = bf16[2,3,128,128]{3,2,1,0:T(8,128)(2,1)S(1)} collective-permute-done((bf16[2,3,128,128]{3,2,1,0:T(8,128)(2,1)S(1)}, bf16[2,3,128,128]{3,2,1,0:T(8,128)(2,1)S(1)}, u32[]{:S(2)}, u32[]{:S(2)}) %collective-permute-start.2) | collective-permute-done | bytes 196640 | tf_op jit(solution)/shard_map/ppermute | solution.py:22
  16.6 3.4 %collective-permute-done.4.refs_6_ = bf16[2,3,128,128]{3,2,1,0:T(8,128)(2,1)S(1)} collective-permute-done((bf16[2,3,128,128]{3,2,1,0:T(8,128)(2,1)S(1)}, bf16[2,3,128,128]{3,2,1,0:T(8,128)(2,1)S(1)}, u32[]{:S(2)}, u32[]{:S(2)}) %collective-permute-start.4) | collective-permute-done | bytes 196640 | tf_op jit(solution)/shard_map/ppermute | solution.py:22
  20.0 0.5 %collective-permute-start.7 = (bf16[2,3,128,128]{3,2,1,0:T(8,128)(2,1)S(1)}, bf16[2,3,128,128]{3,2,1,0:T(8,128)(2,1)S(1)}, u32[]{:S(2)}, u32[]{:S(2)}) collective-permute-start(bf16[2,3,128,128]{3,2,1,0:T(8,128)(2,1)S(1)} %collective-permute-done.6.refs_8_), channel_id=1, source_target_pairs={{0,4},{4,0},{8,12},{12,8},{16,20},{20,16},{24,28},{28,24},{1,5},{5... | collective-permute-start | bytes 589832 | tf_op jit(solution)/shard_map/ppermute | solution.py:22
  20.6 2.4 %collective-permute-start.10 = (bf16[768,128]{1,0:T(8,128)(2,1)S(1)}, bf16[768,128]{1,0:T(8,128)(2,1)S(1)}, u32[]{:S(2)}, u32[]{:S(2)}) collective-permute-start(bf16[768,128]{1,0:T(8,128)(2,1)S(1)} %get-tuple-element.25.refs_12_), channel_id=1, source_target_pairs={{0,1},{1,0},{2,3},{3,2},{4,5},{5,4},{6,7},{7,6},{8,9},{9,8},{10,11... | collective-permute-start | bytes 589832 | tf_op jit(solution)/shard_map/ppermute | solution.py:22
  23.0 3.4 %shard_map.49 = (f32[2,256,128]{2,1,0:T(8,128)S(1)}, f32[128,256]{1,0:T(8,128)S(1)}, bf16[2,24,128,128]{3,2,1,0:T(8,128)(2,1)S(1)}) custom-call(s32[2]{0:T(128)S(1)} %pad_add_fusion.refs_0_, s32[16,128]{1,0:T(8,128)S(1)} %get-tuple-element.21.refs_1_, bf16[2,3,128,128]{3,2,1,0:T(8,128)(2,1)S(1)} %shard_map.48.refs_2_, ...), custom_call_target="tpu_custom_call" | custom-call | flops 3750000128 | bytes 2097152 | tf_op jit(solution)/shard_map/pallas_call | solution.py:295
  26.5 2.7 %shard_map.50 = (f32[256,128]{1,0:T(8,128)S(1)}, f32[128,128]{1,0:T(8,128)S(1)}, f32[128,128]{1,0:T(8,128)S(1)}, s32[16,128]{1,0:T(8,128)S(1)}) custom-call(s32[2]{0:T(128)S(1)} %pad_add_fusion.refs_0_, bf16[2,24,128,128]{3,2,1,0:T(8,128)(2,1)S(1)} %get-tuple-element.26.refs_1_.refs_2_, f32[2,256,128]{2,1,0:T(8,128)S(1)} %get-tuple-element.27.refs_2_, ...), custom_call_target="tpu_custom_call" | custom-call | flops 250000000 | bytes 2097152 | tf_op jit(solution)/shard_map/pallas_call | solution.py:301
  29.2 2.6 %collective-permute-start.11 = (f32[128,128]{1,0:T(8,128)S(1)}, f32[128,128]{1,0:T(8,128)S(1)}, u32[]{:S(2)}, u32[]{:S(2)}) collective-permute-start(f32[128,128]{1,0:T(8,128)S(1)} %get-tuple-element.33), channel_id=1, source_target_pairs={{0,2},{1,3},{2,0},{3,1},{4,6},{5,7},{6,4},{7,5},{8,10},{9,11},{10,... | collective-permute-start | bytes 196616 | tf_op jit(solution)/shard_map/ppermute | solution.py:22
  31.8 0.4 collective-permute-start.12
  32.2 1.4 %shard_map.51.refs_1_ = bf16[256,1536]{1,0:T(8,128)(2,1)S(1)} custom-call(s32[2]{0:T(128)S(1)} %pad_add_fusion.refs_0_, s32[16,128]{1,0:T(8,128)S(1)} %get-tuple-element.30.refs_1_, bf16[2,24,128,128]{3,2,1,0:T(8,128)(2,1)S(1)} %get-tuple-element.26.refs_1_.refs_2_), custom_call_target="tpu_custom_call" | custom-call | flops 268435456 | bytes 2097152 | tf_op jit(solution)/shard_map/pallas_call | solution.py:309
  33.6 0.4 shard_map.53
  34.0 2.6 %collective-permute-start.14 = (f32[64,128]{1,0:T(8,128)S(1)}, f32[64,128]{1,0:T(8,128)S(1)}, u32[]{:S(2)}, u32[]{:S(2)}) collective-permute-start(f32[64,128]{1,0:T(8,128)S(1)} %get-tuple-element.36), channel_id=1, source_target_pairs={{0,2},{1,3},{2,0},{3,1},{4,6},{5,7},{6,4},{7,5},{8,10},{9,11},{10,... | collective-permute-start | bytes 98312 | tf_op jit(solution)/shard_map/ppermute | solution.py:22
  36.6 0.4 shard_map.52
  37.0 0.4 collective-permute-start.13
  37.4 3.0 %collective-permute-done.14.refs_6_ = f32[64,128]{1,0:T(8,128)S(1)} collective-permute-done((f32[64,128]{1,0:T(8,128)S(1)}, f32[64,128]{1,0:T(8,128)S(1)}, u32[]{:S(2)}, u32[]{:S(2)}) %collective-permute-start.14) | collective-permute-done | bytes 32800 | tf_op jit(solution)/shard_map/ppermute | solution.py:22
  40.4 1.4 %collective-permute-done.13.refs_5_ = f32[64,128]{1,0:T(8,128)S(1)} collective-permute-done((f32[64,128]{1,0:T(8,128)S(1)}, f32[64,128]{1,0:T(8,128)S(1)}, u32[]{:S(2)}, u32[]{:S(2)}) %collective-permute-start.13) | collective-permute-done | bytes 32800 | tf_op jit(solution)/shard_map/ppermute | solution.py:22
  41.8 0.8 %shard_map.54 = f32[128,384]{1,0:T(8,128)} custom-call(f32[256,128]{1,0:T(8,128)S(1)} %get-tuple-element.28.refs_0_, f32[64,128]{1,0:T(8,128)S(1)} %get-tuple-element.31.refs_1_, f32[64,128]{1,0:T(8,128)S(1)} %get-tuple-element.32.refs_2_, f32[128,128]{1,0:T(8,128)S(1)} %collective-permute-done.11.refs_3_, f32[128,128]{1,0:T(8,128)S(1)} %collective-permute-done.12.refs_4_, ...), custom_call_target="tpu_custom_call" | custom-call | flops 1048576 | bytes 2097152 | tf_op jit(solution)/shard_map/pallas_call | solution.py:321
  (16 shorter events, 0.2 us)
Async XLA Ops:
  0.0 9.1 %collective-permute-start = (bf16[3,128,128]{2,1,0:T(8,128)(2,1)}, bf16[3,128,128]{2,1,0:T(8,128)(2,1)S(1)}, u32[]{:S(2)}, u32[]{:S(2)}) collective-permute-start(bf16[3,128,128]{2,1,0:T(8,128)(2,1)} %amplitudes.1), channel_id=1, source_target_pairs={{0,2},{1,3},{2,0},{3,1},{4,6},{5,7},{6,4},{7,5},{8,10},{9,11},{10,... | collective-permute-start | bytes 294920 | tf_op jit(solution)/shard_map/ppermute | solution.py:22
  5.2 21.3 %collective-permute-start.8 = (bf16[3088,128]{1,0:T(8,128)(2,1)S(1)}, bf16[3088,128]{1,0:T(8,128)(2,1)S(1)}, u32[]{:S(2)}, u32[]{:S(2)}) collective-permute-start(bf16[3088,128]{1,0:T(8,128)(2,1)S(1)} %get-tuple-element.23.refs_10_), channel_id=1, source_target_pairs={{0,1},{1,0},{2,3},{3,2},{4,5},{5,4},{6,7},{7,6},{8,9},{9,8},{10,11... | collective-permute-start | bytes 2371592 | tf_op jit(solution)/shard_map/ppermute | solution.py:22
  9.1 7.6 %collective-permute-start.2 = (bf16[2,3,128,128]{3,2,1,0:T(8,128)(2,1)S(1)}, bf16[2,3,128,128]{3,2,1,0:T(8,128)(2,1)S(1)}, u32[]{:S(2)}, u32[]{:S(2)}) collective-permute-start(bf16[2,3,128,128]{3,2,1,0:T(8,128)(2,1)S(1)} %shard_map.48.refs_2_), channel_id=1, source_target_pairs={{0,8},{4,12},{8,0},{12,4},{16,24},{20,28},{24,16},{28,20},{1,9},{5... | collective-permute-start | bytes 589832 | tf_op jit(solution)/shard_map/ppermute | solution.py:22
  10.9 9.1 %collective-permute-start.4 = (bf16[2,3,128,128]{3,2,1,0:T(8,128)(2,1)S(1)}, bf16[2,3,128,128]{3,2,1,0:T(8,128)(2,1)S(1)}, u32[]{:S(2)}, u32[]{:S(2)}) collective-permute-start(bf16[2,3,128,128]{3,2,1,0:T(8,128)(2,1)S(1)} %shard_map.48.refs_2_), channel_id=1, source_target_pairs={{0,16},{4,20},{8,24},{12,28},{16,0},{20,4},{24,8},{28,12},{1,17},{... | collective-permute-start | bytes 589832 | tf_op jit(solution)/shard_map/ppermute | solution.py:22
  12.4 7.6 %collective-permute-start.6 = (bf16[2,3,128,128]{3,2,1,0:T(8,128)(2,1)S(1)}, bf16[2,3,128,128]{3,2,1,0:T(8,128)(2,1)S(1)}, u32[]{:S(2)}, u32[]{:S(2)}) collective-permute-start(bf16[2,3,128,128]{3,2,1,0:T(8,128)(2,1)S(1)} %shard_map.48.refs_2_), channel_id=1, source_target_pairs={{0,24},{4,28},{8,16},{12,20},{16,8},{20,12},{24,0},{28,4},{1,25},{... | collective-permute-start | bytes 589832 | tf_op jit(solution)/shard_map/ppermute | solution.py:22
  12.6 8.0 %collective-permute-start.1 = (bf16[2,3,128,128]{3,2,1,0:T(8,128)(2,1)S(1)}, bf16[2,3,128,128]{3,2,1,0:T(8,128)(2,1)S(1)}, u32[]{:S(2)}, u32[]{:S(2)}) collective-permute-start(bf16[2,3,128,128]{3,2,1,0:T(8,128)(2,1)S(1)} %shard_map.48.refs_2_), channel_id=1, source_target_pairs={{0,4},{4,0},{8,12},{12,8},{16,20},{20,16},{24,28},{28,24},{1,5},{5... | collective-permute-start | bytes 589832 | tf_op jit(solution)/shard_map/ppermute | solution.py:22
  16.6 6.3 %collective-permute-start.3 = (bf16[2,3,128,128]{3,2,1,0:T(8,128)(2,1)S(1)}, bf16[2,3,128,128]{3,2,1,0:T(8,128)(2,1)S(1)}, u32[]{:S(2)}, u32[]{:S(2)}) collective-permute-start(bf16[2,3,128,128]{3,2,1,0:T(8,128)(2,1)S(1)} %collective-permute-done.2.refs_4_), channel_id=1, source_target_pairs={{0,4},{4,0},{8,12},{12,8},{16,20},{20,16},{24,28},{28,24},{1,5},{5... | collective-permute-start | bytes 589832 | tf_op jit(solution)/shard_map/ppermute | solution.py:22
  20.0 3.0 %collective-permute-start.5 = (bf16[2,3,128,128]{3,2,1,0:T(8,128)(2,1)S(1)}, bf16[2,3,128,128]{3,2,1,0:T(8,128)(2,1)S(1)}, u32[]{:S(2)}, u32[]{:S(2)}) collective-permute-start(bf16[2,3,128,128]{3,2,1,0:T(8,128)(2,1)S(1)} %collective-permute-done.4.refs_6_), channel_id=1, source_target_pairs={{0,4},{4,0},{8,12},{12,8},{16,20},{20,16},{24,28},{28,24},{1,5},{5... | collective-permute-start | bytes 589832 | tf_op jit(solution)/shard_map/ppermute | solution.py:22
  20.0 3.0 %collective-permute-start.7 = (bf16[2,3,128,128]{3,2,1,0:T(8,128)(2,1)S(1)}, bf16[2,3,128,128]{3,2,1,0:T(8,128)(2,1)S(1)}, u32[]{:S(2)}, u32[]{:S(2)}) collective-permute-start(bf16[2,3,128,128]{3,2,1,0:T(8,128)(2,1)S(1)} %collective-permute-done.6.refs_8_), channel_id=1, source_target_pairs={{0,4},{4,0},{8,12},{12,8},{16,20},{20,16},{24,28},{28,24},{1,5},{5... | collective-permute-start | bytes 589832 | tf_op jit(solution)/shard_map/ppermute | solution.py:22
  20.6 13.0 %collective-permute-start.10 = (bf16[768,128]{1,0:T(8,128)(2,1)S(1)}, bf16[768,128]{1,0:T(8,128)(2,1)S(1)}, u32[]{:S(2)}, u32[]{:S(2)}) collective-permute-start(bf16[768,128]{1,0:T(8,128)(2,1)S(1)} %get-tuple-element.25.refs_12_), channel_id=1, source_target_pairs={{0,1},{1,0},{2,3},{3,2},{4,5},{5,4},{6,7},{7,6},{8,9},{9,8},{10,11... | collective-permute-start | bytes 589832 | tf_op jit(solution)/shard_map/ppermute | solution.py:22
  22.9 13.6 %collective-permute-start.9 = (bf16[768,128]{1,0:T(8,128)(2,1)S(1)}, bf16[768,128]{1,0:T(8,128)(2,1)S(1)}, u32[]{:S(2)}, u32[]{:S(2)}) collective-permute-start(bf16[768,128]{1,0:T(8,128)(2,1)S(1)} %get-tuple-element.24.refs_11_), channel_id=1, source_target_pairs={{0,1},{1,0},{2,3},{3,2},{4,5},{5,4},{6,7},{7,6},{8,9},{9,8},{10,11... | collective-permute-start | bytes 589832 | tf_op jit(solution)/shard_map/ppermute | solution.py:22
  29.2 12.6 %collective-permute-start.11 = (f32[128,128]{1,0:T(8,128)S(1)}, f32[128,128]{1,0:T(8,128)S(1)}, u32[]{:S(2)}, u32[]{:S(2)}) collective-permute-start(f32[128,128]{1,0:T(8,128)S(1)} %get-tuple-element.33), channel_id=1, source_target_pairs={{0,2},{1,3},{2,0},{3,1},{4,6},{5,7},{6,4},{7,5},{8,10},{9,11},{10,... | collective-permute-start | bytes 196616 | tf_op jit(solution)/shard_map/ppermute | solution.py:22
  31.8 10.0 %collective-permute-start.12 = (f32[128,128]{1,0:T(8,128)S(1)}, f32[128,128]{1,0:T(8,128)S(1)}, u32[]{:S(2)}, u32[]{:S(2)}) collective-permute-start(f32[128,128]{1,0:T(8,128)S(1)} %get-tuple-element.34), channel_id=1, source_target_pairs={{0,2},{1,3},{2,0},{3,1},{4,6},{5,7},{6,4},{7,5},{8,10},{9,11},{10,... | collective-permute-start | bytes 196616 | tf_op jit(solution)/shard_map/ppermute | solution.py:22
  34.0 6.4 %collective-permute-start.14 = (f32[64,128]{1,0:T(8,128)S(1)}, f32[64,128]{1,0:T(8,128)S(1)}, u32[]{:S(2)}, u32[]{:S(2)}) collective-permute-start(f32[64,128]{1,0:T(8,128)S(1)} %get-tuple-element.36), channel_id=1, source_target_pairs={{0,2},{1,3},{2,0},{3,1},{4,6},{5,7},{6,4},{7,5},{8,10},{9,11},{10,... | collective-permute-start | bytes 98312 | tf_op jit(solution)/shard_map/ppermute | solution.py:22
  37.0 4.9 %collective-permute-start.13 = (f32[64,128]{1,0:T(8,128)S(1)}, f32[64,128]{1,0:T(8,128)S(1)}, u32[]{:S(2)}, u32[]{:S(2)}) collective-permute-start(f32[64,128]{1,0:T(8,128)S(1)} %get-tuple-element.35), channel_id=1, source_target_pairs={{0,2},{1,3},{2,0},{3,1},{4,6},{5,7},{6,4},{7,5},{8,10},{9,11},{10,... | collective-permute-start | bytes 98312 | tf_op jit(solution)/shard_map/ppermute | solution.py:22

commit v7 on v6

--- a/solution.py
+++ b/solution.py
@@ -6,7 +6,7 @@
 from jax.sharding import PartitionSpec as P
 
 VMEM_BYTES = 48 * 1024 * 1024
-UNROLL = 4
+UNROLL = 12
 OWN_FLOPS = 3750000000
 HEAD_FLOPS = 250000000
 SOON = 4

time: 42.5 us -> 42.6 us (level)
  waiting for transfers between devices: 12.8 us -> 15.4 us
  Pallas kernels: 11.4 us -> 9.39 us
  starting transfers between devices: 18.2 us -> 17.7 us
    ppermute x15, waiting for transfers between devices: 12.8 us -> 15.4 us  [shift(): return lax.ppermute(value, axis, [(j, j ^ mask) for j in range(size)])]
    pallas_call x1, Pallas kernels: 2.7 us -> 1.65 us  [on_pairs(): call(lambda *refs: head_kernel(slots, *refs), (f32(before * rows, width),...]
    pallas_call x1, Pallas kernels: 3.43 us -> 2.48 us  [on_pairs(): call(lambda *refs: own_kernel(masks, slots, *refs), (f32(before, 2 * rows...]
    ppermute x15, starting transfers between devices: 18.2 us -> 17.7 us  [shift(): return lax.ppermute(value, axis, [(j, j ^ mask) for j in range(size)])]
  transfers between devices with their start and end apart: 15 -> 15, of which waited for: 5 -> 7; matrix products, arithmetic and copies ran while one was open for 0% -> 0% of each run, Pallas kernels for 25% -> 20%
where the time goes in v7:
time: 42.6 us
  starting transfers between devices  17.7 us (42%)
  waiting for transfers between devices  15.4 us (36%)
  Pallas kernels  9.39 us (22%)
    ppermute x15, starting transfers between devices, shift(): return lax.ppermute(value, axis, [(j, j ^ mask) for j in range(size)])  17.7 us
    ppermute x15, waiting for transfers between devices, shift(): return lax.ppermute(value, axis, [(j, j ^ mask) for j in range(size)])  15.4 us
    pallas_call x1, Pallas kernels, on_pairs(): call(lambda *refs: own_kernel(masks, slots, *refs), (f32(before, 2 * rows...  2.48 us
    pallas_call x1, Pallas kernels, on_pairs(): call(lambda *refs: head_kernel(slots, *refs), (f32(before * rows, width),...  1.65 us
    pallas_call x1, Pallas kernels, on_pairs(): call(lambda *refs: pick_kernel(before, slots, *refs), jax.ShapeDtypeStruc...  1.39 us
    pallas_call x1, Pallas kernels, cut(): pl.pallas_call(rest_cut_kernel, out_shape=(jax.ShapeDtypeStruct((sizes[1]...  1.2 us
    pallas_call x1, Pallas kernels, cut(): pl.pallas_call(head_cut_kernel, out_shape=(jax.ShapeDtypeStruct((sizes[0]...  1.16 us
  transfers between devices with their start and end apart: 15, of which 7 were waited for; matrix products, arithmetic and copies ran while one was open for 0% of the time, Pallas kernels for 20%

profile of v7, /device:TPU:0, one launch (start us, length us, event | category | flops | bytes accessed | tf_op | source)
XLA Modules:
  0.0 42.6 jit_solution(8851056280995552495)
XLA Ops:
  0.0 4.0 %collective-permute-start = (bf16[3,128,128]{2,1,0:T(8,128)(2,1)}, bf16[3,128,128]{2,1,0:T(8,128)(2,1)S(1)}, u32[]{:S(2)}, u32[]{:S(2)}) collective-permute-start(bf16[3,128,128]{2,1,0:T(8,128)(2,1)} %amplitudes.1), channel_id=1, source_target_pairs={{0,2},{1,3},{2,0},{3,1},{4,6},{5,7},{6,4},{7,5},{8,10},{9,11},{10,... | collective-permute-start | bytes 294920 | tf_op jit(solution)/shard_map/ppermute | solution.py:22
  4.0 1.2 %shard_map.46 = (bf16[3088,128]{1,0:T(8,128)(2,1)S(1)}, s32[16,128]{1,0:T(8,128)S(1)}) custom-call(bf16[3,12,128,128]{3,2,1,0:T(8,128)(2,1)} %whole.3, s32[3,12]{1,0:T(4,128)} %lists.1, s32[3]{0:T(128)} %counts.1), custom_call_target="tpu_custom_call" | custom-call | tf_op jit(solution)/shard_map/pallas_call | solution.py:125
  5.2 1.6 %collective-permute-start.8 = (bf16[3088,128]{1,0:T(8,128)(2,1)S(1)}, bf16[3088,128]{1,0:T(8,128)(2,1)S(1)}, u32[]{:S(2)}, u32[]{:S(2)}) collective-permute-start(bf16[3088,128]{1,0:T(8,128)(2,1)S(1)} %get-tuple-element.23.refs_10_), channel_id=1, source_target_pairs={{0,1},{1,0},{2,3},{3,2},{4,5},{5,4},{6,7},{7,6},{8,9},{9,8},{10,11... | collective-permute-start | bytes 2371592 | tf_op jit(solution)/shard_map/ppermute | solution.py:22
  6.9 1.2 %shard_map.47 = (bf16[768,128]{1,0:T(8,128)(2,1)S(1)}, bf16[768,128]{1,0:T(8,128)(2,1)S(1)}, bf16[3,128,128]{2,1,0:T(8,128)(2,1)S(1)}) custom-call(bf16[3,12,128,128]{3,2,1,0:T(8,128)(2,1)} %whole.3, bf16[3,128,128]{2,1,0:T(8,128)(2,1)} %amplitudes.1), custom_call_target="tpu_custom_call" | custom-call | flops 1048576 | bytes 524288 | tf_op jit(solution)/shard_map/pallas_call | solution.py:140
  8.1 1.0 %collective-permute-done.second = bf16[3,128,128]{2,1,0:T(8,128)(2,1)S(1)} collective-permute-done((bf16[3,128,128]{2,1,0:T(8,128)(2,1)}, bf16[3,128,128]{2,1,0:T(8,128)(2,1)S(1)}, u32[]{:S(2)}, u32[]{:S(2)}) %collective-permute-start) | collective-permute-done | bytes 98336 | tf_op jit(solution)/shard_map/ppermute | solution.py:22
  9.1 1.8 %collective-permute-start.2 = (bf16[2,3,128,128]{3,2,1,0:T(8,128)(2,1)S(1)}, bf16[2,3,128,128]{3,2,1,0:T(8,128)(2,1)S(1)}, u32[]{:S(2)}, u32[]{:S(2)}) collective-permute-start(bf16[2,3,128,128]{3,2,1,0:T(8,128)(2,1)S(1)} %shard_map.48.refs_2_), channel_id=1, source_target_pairs={{0,8},{4,12},{8,0},{12,4},{16,24},{20,28},{24,16},{28,20},{1,9},{5... | collective-permute-start | bytes 589832 | tf_op jit(solution)/shard_map/ppermute | solution.py:22
  10.9 1.5 %collective-permute-start.4 = (bf16[2,3,128,128]{3,2,1,0:T(8,128)(2,1)S(1)}, bf16[2,3,128,128]{3,2,1,0:T(8,128)(2,1)S(1)}, u32[]{:S(2)}, u32[]{:S(2)}) collective-permute-start(bf16[2,3,128,128]{3,2,1,0:T(8,128)(2,1)S(1)} %shard_map.48.refs_2_), channel_id=1, source_target_pairs={{0,16},{4,20},{8,24},{12,28},{16,0},{20,4},{24,8},{28,12},{1,17},{... | collective-permute-start | bytes 589832 | tf_op jit(solution)/shard_map/ppermute | solution.py:22
  12.6 4.0 %collective-permute-done.2.refs_4_ = bf16[2,3,128,128]{3,2,1,0:T(8,128)(2,1)S(1)} collective-permute-done((bf16[2,3,128,128]{3,2,1,0:T(8,128)(2,1)S(1)}, bf16[2,3,128,128]{3,2,1,0:T(8,128)(2,1)S(1)}, u32[]{:S(2)}, u32[]{:S(2)}) %collective-permute-start.2) | collective-permute-done | bytes 196640 | tf_op jit(solution)/shard_map/ppermute | solution.py:22
  16.6 3.4 %collective-permute-done.4.refs_6_ = bf16[2,3,128,128]{3,2,1,0:T(8,128)(2,1)S(1)} collective-permute-done((bf16[2,3,128,128]{3,2,1,0:T(8,128)(2,1)S(1)}, bf16[2,3,128,128]{3,2,1,0:T(8,128)(2,1)S(1)}, u32[]{:S(2)}, u32[]{:S(2)}) %collective-permute-start.4) | collective-permute-done | bytes 196640 | tf_op jit(solution)/shard_map/ppermute | solution.py:22
  20.0 0.5 %collective-permute-start.7 = (bf16[2,3,128,128]{3,2,1,0:T(8,128)(2,1)S(1)}, bf16[2,3,128,128]{3,2,1,0:T(8,128)(2,1)S(1)}, u32[]{:S(2)}, u32[]{:S(2)}) collective-permute-start(bf16[2,3,128,128]{3,2,1,0:T(8,128)(2,1)S(1)} %collective-permute-done.6.refs_8_), channel_id=1, source_target_pairs={{0,4},{4,0},{8,12},{12,8},{16,20},{20,16},{24,28},{28,24},{1,5},{5... | collective-permute-start | bytes 589832 | tf_op jit(solution)/shard_map/ppermute | solution.py:22
  20.6 2.4 %collective-permute-start.10 = (bf16[768,128]{1,0:T(8,128)(2,1)S(1)}, bf16[768,128]{1,0:T(8,128)(2,1)S(1)}, u32[]{:S(2)}, u32[]{:S(2)}) collective-permute-start(bf16[768,128]{1,0:T(8,128)(2,1)S(1)} %get-tuple-element.25.refs_12_), channel_id=1, source_target_pairs={{0,1},{1,0},{2,3},{3,2},{4,5},{5,4},{6,7},{7,6},{8,9},{9,8},{10,11... | collective-permute-start | bytes 589832 | tf_op jit(solution)/shard_map/ppermute | solution.py:22
  23.0 2.5 %shard_map.49 = (f32[2,256,128]{2,1,0:T(8,128)S(1)}, f32[128,256]{1,0:T(8,128)S(1)}, bf16[2,24,128,128]{3,2,1,0:T(8,128)(2,1)S(1)}) custom-call(s32[2]{0:T(128)S(1)} %pad_add_fusion.refs_0_, s32[16,128]{1,0:T(8,128)S(1)} %get-tuple-element.21.refs_1_, bf16[2,3,128,128]{3,2,1,0:T(8,128)(2,1)S(1)} %shard_map.48.refs_2_, ...), custom_call_target="tpu_custom_call" | custom-call | flops 3750000128 | bytes 2097152 | tf_op jit(solution)/shard_map/pallas_call | solution.py:295
  25.5 0.4 collective-permute-done.8.refs_3_
  25.9 1.7 %shard_map.50 = (f32[256,128]{1,0:T(8,128)S(1)}, f32[128,128]{1,0:T(8,128)S(1)}, f32[128,128]{1,0:T(8,128)S(1)}, s32[16,128]{1,0:T(8,128)S(1)}) custom-call(s32[2]{0:T(128)S(1)} %pad_add_fusion.refs_0_, bf16[2,24,128,128]{3,2,1,0:T(8,128)(2,1)S(1)} %get-tuple-element.26.refs_1_.refs_2_, f32[2,256,128]{2,1,0:T(8,128)S(1)} %get-tuple-element.27.refs_2_, ...), custom_call_target="tpu_custom_call" | custom-call | flops 250000000 | bytes 2097152 | tf_op jit(solution)/shard_map/pallas_call | solution.py:301
  27.6 2.1 %collective-permute-start.11 = (f32[128,128]{1,0:T(8,128)S(1)}, f32[128,128]{1,0:T(8,128)S(1)}, u32[]{:S(2)}, u32[]{:S(2)}) collective-permute-start(f32[128,128]{1,0:T(8,128)S(1)} %get-tuple-element.33), channel_id=1, source_target_pairs={{0,2},{1,3},{2,0},{3,1},{4,6},{5,7},{6,4},{7,5},{8,10},{9,11},{10,... | collective-permute-start | bytes 196616 | tf_op jit(solution)/shard_map/ppermute | solution.py:22
  29.7 0.8 %collective-permute-start.12 = (f32[128,128]{1,0:T(8,128)S(1)}, f32[128,128]{1,0:T(8,128)S(1)}, u32[]{:S(2)}, u32[]{:S(2)}) collective-permute-start(f32[128,128]{1,0:T(8,128)S(1)} %get-tuple-element.34), channel_id=1, source_target_pairs={{0,2},{1,3},{2,0},{3,1},{4,6},{5,7},{6,4},{7,5},{8,10},{9,11},{10,... | collective-permute-start | bytes 196616 | tf_op jit(solution)/shard_map/ppermute | solution.py:22
  30.6 1.4 %shard_map.51.refs_1_ = bf16[256,1536]{1,0:T(8,128)(2,1)S(1)} custom-call(s32[2]{0:T(128)S(1)} %pad_add_fusion.refs_0_, s32[16,128]{1,0:T(8,128)S(1)} %get-tuple-element.30.refs_1_, bf16[2,24,128,128]{3,2,1,0:T(8,128)(2,1)S(1)} %get-tuple-element.26.refs_1_.refs_2_), custom_call_target="tpu_custom_call" | custom-call | flops 268435456 | bytes 2097152 | tf_op jit(solution)/shard_map/pallas_call | solution.py:309
  32.0 0.4 shard_map.53
  32.4 2.1 %collective-permute-start.14 = (f32[64,128]{1,0:T(8,128)S(1)}, f32[64,128]{1,0:T(8,128)S(1)}, u32[]{:S(2)}, u32[]{:S(2)}) collective-permute-start(f32[64,128]{1,0:T(8,128)S(1)} %get-tuple-element.36), channel_id=1, source_target_pairs={{0,2},{1,3},{2,0},{3,1},{4,6},{5,7},{6,4},{7,5},{8,10},{9,11},{10,... | collective-permute-start | bytes 98312 | tf_op jit(solution)/shard_map/ppermute | solution.py:22
  34.5 2.1 %collective-permute-done.9.refs_2_ = bf16[768,128]{1,0:T(8,128)(2,1)S(1)} collective-permute-done((bf16[768,128]{1,0:T(8,128)(2,1)S(1)}, bf16[768,128]{1,0:T(8,128)(2,1)S(1)}, u32[]{:S(2)}, u32[]{:S(2)}) %collective-permute-start.9) | collective-permute-done | bytes 196640 | tf_op jit(solution)/shard_map/ppermute | solution.py:22
  36.9 0.4 collective-permute-start.13
  37.3 1.8 %collective-permute-done.14.refs_6_ = f32[64,128]{1,0:T(8,128)S(1)} collective-permute-done((f32[64,128]{1,0:T(8,128)S(1)}, f32[64,128]{1,0:T(8,128)S(1)}, u32[]{:S(2)}, u32[]{:S(2)}) %collective-permute-start.14) | collective-permute-done | bytes 32800 | tf_op jit(solution)/shard_map/ppermute | solution.py:22
  39.1 2.7 %collective-permute-done.13.refs_5_ = f32[64,128]{1,0:T(8,128)S(1)} collective-permute-done((f32[64,128]{1,0:T(8,128)S(1)}, f32[64,128]{1,0:T(8,128)S(1)}, u32[]{:S(2)}, u32[]{:S(2)}) %collective-permute-start.13) | collective-permute-done | bytes 32800 | tf_op jit(solution)/shard_map/ppermute | solution.py:22
  41.8 0.8 %shard_map.54 = f32[128,384]{1,0:T(8,128)} custom-call(f32[256,128]{1,0:T(8,128)S(1)} %get-tuple-element.28.refs_0_, f32[64,128]{1,0:T(8,128)S(1)} %get-tuple-element.31.refs_1_, f32[64,128]{1,0:T(8,128)S(1)} %get-tuple-element.32.refs_2_, f32[128,128]{1,0:T(8,128)S(1)} %collective-permute-done.11.refs_3_, f32[128,128]{1,0:T(8,128)S(1)} %collective-permute-done.12.refs_4_, ...), custom_call_target="tpu_custom_call" | custom-call | flops 1048576 | bytes 2097152 | tf_op jit(solution)/shard_map/pallas_call | solution.py:321
  (16 shorter events, 0.8 us)
Async XLA Ops:
  0.0 9.1 %collective-permute-start = (bf16[3,128,128]{2,1,0:T(8,128)(2,1)}, bf16[3,128,128]{2,1,0:T(8,128)(2,1)S(1)}, u32[]{:S(2)}, u32[]{:S(2)}) collective-permute-start(bf16[3,128,128]{2,1,0:T(8,128)(2,1)} %amplitudes.1), channel_id=1, source_target_pairs={{0,2},{1,3},{2,0},{3,1},{4,6},{5,7},{6,4},{7,5},{8,10},{9,11},{10,... | collective-permute-start | bytes 294920 | tf_op jit(solution)/shard_map/ppermute | solution.py:22
  5.2 20.7 %collective-permute-start.8 = (bf16[3088,128]{1,0:T(8,128)(2,1)S(1)}, bf16[3088,128]{1,0:T(8,128)(2,1)S(1)}, u32[]{:S(2)}, u32[]{:S(2)}) collective-permute-start(bf16[3088,128]{1,0:T(8,128)(2,1)S(1)} %get-tuple-element.23.refs_10_), channel_id=1, source_target_pairs={{0,1},{1,0},{2,3},{3,2},{4,5},{5,4},{6,7},{7,6},{8,9},{9,8},{10,11... | collective-permute-start | bytes 2371592 | tf_op jit(solution)/shard_map/ppermute | solution.py:22
  9.1 7.6 %collective-permute-start.2 = (bf16[2,3,128,128]{3,2,1,0:T(8,128)(2,1)S(1)}, bf16[2,3,128,128]{3,2,1,0:T(8,128)(2,1)S(1)}, u32[]{:S(2)}, u32[]{:S(2)}) collective-permute-start(bf16[2,3,128,128]{3,2,1,0:T(8,128)(2,1)S(1)} %shard_map.48.refs_2_), channel_id=1, source_target_pairs={{0,8},{4,12},{8,0},{12,4},{16,24},{20,28},{24,16},{28,20},{1,9},{5... | collective-permute-start | bytes 589832 | tf_op jit(solution)/shard_map/ppermute | solution.py:22
  10.9 9.1 %collective-permute-start.4 = (bf16[2,3,128,128]{3,2,1,0:T(8,128)(2,1)S(1)}, bf16[2,3,128,128]{3,2,1,0:T(8,128)(2,1)S(1)}, u32[]{:S(2)}, u32[]{:S(2)}) collective-permute-start(bf16[2,3,128,128]{3,2,1,0:T(8,128)(2,1)S(1)} %shard_map.48.refs_2_), channel_id=1, source_target_pairs={{0,16},{4,20},{8,24},{12,28},{16,0},{20,4},{24,8},{28,12},{1,17},{... | collective-permute-start | bytes 589832 | tf_op jit(solution)/shard_map/ppermute | solution.py:22
  12.4 7.6 %collective-permute-start.6 = (bf16[2,3,128,128]{3,2,1,0:T(8,128)(2,1)S(1)}, bf16[2,3,128,128]{3,2,1,0:T(8,128)(2,1)S(1)}, u32[]{:S(2)}, u32[]{:S(2)}) collective-permute-start(bf16[2,3,128,128]{3,2,1,0:T(8,128)(2,1)S(1)} %shard_map.48.refs_2_), channel_id=1, source_target_pairs={{0,24},{4,28},{8,16},{12,20},{16,8},{20,12},{24,0},{28,4},{1,25},{... | collective-permute-start | bytes 589832 | tf_op jit(solution)/shard_map/ppermute | solution.py:22
  12.6 8.0 %collective-permute-start.1 = (bf16[2,3,128,128]{3,2,1,0:T(8,128)(2,1)S(1)}, bf16[2,3,128,128]{3,2,1,0:T(8,128)(2,1)S(1)}, u32[]{:S(2)}, u32[]{:S(2)}) collective-permute-start(bf16[2,3,128,128]{3,2,1,0:T(8,128)(2,1)S(1)} %shard_map.48.refs_2_), channel_id=1, source_target_pairs={{0,4},{4,0},{8,12},{12,8},{16,20},{20,16},{24,28},{28,24},{1,5},{5... | collective-permute-start | bytes 589832 | tf_op jit(solution)/shard_map/ppermute | solution.py:22
  16.6 6.3 %collective-permute-start.3 = (bf16[2,3,128,128]{3,2,1,0:T(8,128)(2,1)S(1)}, bf16[2,3,128,128]{3,2,1,0:T(8,128)(2,1)S(1)}, u32[]{:S(2)}, u32[]{:S(2)}) collective-permute-start(bf16[2,3,128,128]{3,2,1,0:T(8,128)(2,1)S(1)} %collective-permute-done.2.refs_4_), channel_id=1, source_target_pairs={{0,4},{4,0},{8,12},{12,8},{16,20},{20,16},{24,28},{28,24},{1,5},{5... | collective-permute-start | bytes 589832 | tf_op jit(solution)/shard_map/ppermute | solution.py:22
  20.0 3.0 %collective-permute-start.5 = (bf16[2,3,128,128]{3,2,1,0:T(8,128)(2,1)S(1)}, bf16[2,3,128,128]{3,2,1,0:T(8,128)(2,1)S(1)}, u32[]{:S(2)}, u32[]{:S(2)}) collective-permute-start(bf16[2,3,128,128]{3,2,1,0:T(8,128)(2,1)S(1)} %collective-permute-done.4.refs_6_), channel_id=1, source_target_pairs={{0,4},{4,0},{8,12},{12,8},{16,20},{20,16},{24,28},{28,24},{1,5},{5... | collective-permute-start | bytes 589832 | tf_op jit(solution)/shard_map/ppermute | solution.py:22
  20.0 3.0 %collective-permute-start.7 = (bf16[2,3,128,128]{3,2,1,0:T(8,128)(2,1)S(1)}, bf16[2,3,128,128]{3,2,1,0:T(8,128)(2,1)S(1)}, u32[]{:S(2)}, u32[]{:S(2)}) collective-permute-start(bf16[2,3,128,128]{3,2,1,0:T(8,128)(2,1)S(1)} %collective-permute-done.6.refs_8_), channel_id=1, source_target_pairs={{0,4},{4,0},{8,12},{12,8},{16,20},{20,16},{24,28},{28,24},{1,5},{5... | collective-permute-start | bytes 589832 | tf_op jit(solution)/shard_map/ppermute | solution.py:22
  20.6 11.4 %collective-permute-start.10 = (bf16[768,128]{1,0:T(8,128)(2,1)S(1)}, bf16[768,128]{1,0:T(8,128)(2,1)S(1)}, u32[]{:S(2)}, u32[]{:S(2)}) collective-permute-start(bf16[768,128]{1,0:T(8,128)(2,1)S(1)} %get-tuple-element.25.refs_12_), channel_id=1, source_target_pairs={{0,1},{1,0},{2,3},{3,2},{4,5},{5,4},{6,7},{7,6},{8,9},{9,8},{10,11... | collective-permute-start | bytes 589832 | tf_op jit(solution)/shard_map/ppermute | solution.py:22
  22.9 13.6 %collective-permute-start.9 = (bf16[768,128]{1,0:T(8,128)(2,1)S(1)}, bf16[768,128]{1,0:T(8,128)(2,1)S(1)}, u32[]{:S(2)}, u32[]{:S(2)}) collective-permute-start(bf16[768,128]{1,0:T(8,128)(2,1)S(1)} %get-tuple-element.24.refs_11_), channel_id=1, source_target_pairs={{0,1},{1,0},{2,3},{3,2},{4,5},{5,4},{6,7},{7,6},{8,9},{9,8},{10,11... | collective-permute-start | bytes 589832 | tf_op jit(solution)/shard_map/ppermute | solution.py:22
  27.6 14.2 %collective-permute-start.11 = (f32[128,128]{1,0:T(8,128)S(1)}, f32[128,128]{1,0:T(8,128)S(1)}, u32[]{:S(2)}, u32[]{:S(2)}) collective-permute-start(f32[128,128]{1,0:T(8,128)S(1)} %get-tuple-element.33), channel_id=1, source_target_pairs={{0,2},{1,3},{2,0},{3,1},{4,6},{5,7},{6,4},{7,5},{8,10},{9,11},{10,... | collective-permute-start | bytes 196616 | tf_op jit(solution)/shard_map/ppermute | solution.py:22
  29.7 12.1 %collective-permute-start.12 = (f32[128,128]{1,0:T(8,128)S(1)}, f32[128,128]{1,0:T(8,128)S(1)}, u32[]{:S(2)}, u32[]{:S(2)}) collective-permute-start(f32[128,128]{1,0:T(8,128)S(1)} %get-tuple-element.34), channel_id=1, source_target_pairs={{0,2},{1,3},{2,0},{3,1},{4,6},{5,7},{6,4},{7,5},{8,10},{9,11},{10,... | collective-permute-start | bytes 196616 | tf_op jit(solution)/shard_map/ppermute | solution.py:22
  32.4 6.8 %collective-permute-start.14 = (f32[64,128]{1,0:T(8,128)S(1)}, f32[64,128]{1,0:T(8,128)S(1)}, u32[]{:S(2)}, u32[]{:S(2)}) collective-permute-start(f32[64,128]{1,0:T(8,128)S(1)} %get-tuple-element.36), channel_id=1, source_target_pairs={{0,2},{1,3},{2,0},{3,1},{4,6},{5,7},{6,4},{7,5},{8,10},{9,11},{10,... | collective-permute-start | bytes 98312 | tf_op jit(solution)/shard_map/ppermute | solution.py:22
  36.9 4.9 %collective-permute-start.13 = (f32[64,128]{1,0:T(8,128)S(1)}, f32[64,128]{1,0:T(8,128)S(1)}, u32[]{:S(2)}, u32[]{:S(2)}) collective-permute-start(f32[64,128]{1,0:T(8,128)S(1)} %get-tuple-element.35), channel_id=1, source_target_pairs={{0,2},{1,3},{2,0},{3,1},{4,6},{5,7},{6,4},{7,5},{8,10},{9,11},{10,... | collective-permute-start | bytes 98312 | tf_op jit(solution)/shard_map/ppermute | solution.py:22

commit v8 on v7

--- a/solution.py
+++ b/solution.py
@@ -311,7 +311,9 @@
         jax.ShapeDtypeStruct((2 * rows, slots * depth), far.dtype),
         1, 2, scratch, 2**28,
     )(place, table, stage)
-    owns, gots = [own], [shift(x, "oo", n_oo, 2) for x in away]
+    soon, late = away
+    late, picked = lax.optimization_barrier((late, picked))
+    owns, gots = [own], [shift(x, "oo", n_oo, 2) for x in (soon, late)]
     for n in range(PARTS):
         own, away = call(
             lambda *refs, n=n: tail_kernel(slots, n, *refs), (f32(width // PARTS, rows),) * 2, 0, 3, [], 2**28

time: 42.6 us -> 42.1 us (0.988)
  waiting for transfers between devices: 15.4 us -> 14.2 us
    ppermute x15, waiting for transfers between devices: 15.4 us -> 14.2 us  [shift(): return lax.ppermute(value, axis, [(j, j ^ mask) for j in range(size)])]
  transfers between devices with their start and end apart: 15 -> 15, of which waited for: 7 -> 7; matrix products, arithmetic and copies ran while one was open for 0% -> 0% of each run, Pallas kernels for 20% -> 21%
where the time goes in v8:
time: 42.1 us; the launch traced here: 41.9 us
  starting transfers between devices  18.1 us (43%)
  waiting for transfers between devices  14.2 us (34%)
  Pallas kernels  9.39 us (22%)
    ppermute x15, starting transfers between devices, shift(): return lax.ppermute(value, axis, [(j, j ^ mask) for j in range(size)])  18.1 us
    ppermute x15, waiting for transfers between devices, shift(): return lax.ppermute(value, axis, [(j, j ^ mask) for j in range(size)])  14.2 us
    pallas_call x1, Pallas kernels, on_pairs(): call(lambda *refs: own_kernel(masks, slots, *refs), (f32(before, 2 * rows...  2.48 us
    pallas_call x1, Pallas kernels, on_pairs(): call(lambda *refs: head_kernel(slots, *refs), (f32(before * rows, width),...  1.65 us
    pallas_call x1, Pallas kernels, on_pairs(): call(lambda *refs: pick_kernel(before, slots, *refs), jax.ShapeDtypeStruc...  1.4 us
    pallas_call x1, Pallas kernels, cut(): pl.pallas_call(rest_cut_kernel, out_shape=(jax.ShapeDtypeStruct((sizes[1]...  1.2 us
    pallas_call x1, Pallas kernels, cut(): pl.pallas_call(head_cut_kernel, out_shape=(jax.ShapeDtypeStruct((sizes[0]...  1.16 us
  transfers between devices with their start and end apart: 15, of which 7 were waited for; matrix products, arithmetic and copies ran while one was open for 0% of the time, Pallas kernels for 21%

profile of v8, /device:TPU:0, one launch (start us, length us, event | category | flops | bytes accessed | tf_op | source)
XLA Modules:
  0.0 41.9 jit_solution(5541643690091989138)
XLA Ops:
  0.0 4.0 %collective-permute-start = (bf16[3,128,128]{2,1,0:T(8,128)(2,1)}, bf16[3,128,128]{2,1,0:T(8,128)(2,1)S(1)}, u32[]{:S(2)}, u32[]{:S(2)}) collective-permute-start(bf16[3,128,128]{2,1,0:T(8,128)(2,1)} %amplitudes.1), channel_id=1, source_target_pairs={{0,2},{1,3},{2,0},{3,1},{4,6},{5,7},{6,4},{7,5},{8,10},{9,11},{10,... | collective-permute-start | bytes 294920 | tf_op jit(solution)/shard_map/ppermute | solution.py:22
  4.0 1.2 %shard_map.46 = (bf16[3088,128]{1,0:T(8,128)(2,1)S(1)}, s32[16,128]{1,0:T(8,128)S(1)}) custom-call(bf16[3,12,128,128]{3,2,1,0:T(8,128)(2,1)} %whole.3, s32[3,12]{1,0:T(4,128)} %lists.1, s32[3]{0:T(128)} %counts.1), custom_call_target="tpu_custom_call" | custom-call | tf_op jit(solution)/shard_map/pallas_call | solution.py:125
  5.2 1.6 %collective-permute-start.8 = (bf16[3088,128]{1,0:T(8,128)(2,1)S(1)}, bf16[3088,128]{1,0:T(8,128)(2,1)S(1)}, u32[]{:S(2)}, u32[]{:S(2)}) collective-permute-start(bf16[3088,128]{1,0:T(8,128)(2,1)S(1)} %get-tuple-element.25.refs_10_), channel_id=1, source_target_pairs={{0,1},{1,0},{2,3},{3,2},{4,5},{5,4},{6,7},{7,6},{8,9},{9,8},{10,11... | collective-permute-start | bytes 2371592 | tf_op jit(solution)/shard_map/ppermute | solution.py:22
  6.9 1.2 %shard_map.47 = (bf16[768,128]{1,0:T(8,128)(2,1)S(1)}, bf16[768,128]{1,0:T(8,128)(2,1)S(1)}, bf16[3,128,128]{2,1,0:T(8,128)(2,1)S(1)}) custom-call(bf16[3,12,128,128]{3,2,1,0:T(8,128)(2,1)} %whole.3, bf16[3,128,128]{2,1,0:T(8,128)(2,1)} %amplitudes.1), custom_call_target="tpu_custom_call" | custom-call | flops 1048576 | bytes 524288 | tf_op jit(solution)/shard_map/pallas_call | solution.py:140
  8.1 1.0 %collective-permute-done.second = bf16[3,128,128]{2,1,0:T(8,128)(2,1)S(1)} collective-permute-done((bf16[3,128,128]{2,1,0:T(8,128)(2,1)}, bf16[3,128,128]{2,1,0:T(8,128)(2,1)S(1)}, u32[]{:S(2)}, u32[]{:S(2)}) %collective-permute-start) | collective-permute-done | bytes 98336 | tf_op jit(solution)/shard_map/ppermute | solution.py:22
  9.1 1.8 %collective-permute-start.2 = (bf16[2,3,128,128]{3,2,1,0:T(8,128)(2,1)S(1)}, bf16[2,3,128,128]{3,2,1,0:T(8,128)(2,1)S(1)}, u32[]{:S(2)}, u32[]{:S(2)}) collective-permute-start(bf16[2,3,128,128]{3,2,1,0:T(8,128)(2,1)S(1)} %shard_map.48.refs_2_), channel_id=1, source_target_pairs={{0,8},{4,12},{8,0},{12,4},{16,24},{20,28},{24,16},{28,20},{1,9},{5... | collective-permute-start | bytes 589832 | tf_op jit(solution)/shard_map/ppermute | solution.py:22
  10.9 1.5 %collective-permute-start.4 = (bf16[2,3,128,128]{3,2,1,0:T(8,128)(2,1)S(1)}, bf16[2,3,128,128]{3,2,1,0:T(8,128)(2,1)S(1)}, u32[]{:S(2)}, u32[]{:S(2)}) collective-permute-start(bf16[2,3,128,128]{3,2,1,0:T(8,128)(2,1)S(1)} %shard_map.48.refs_2_), channel_id=1, source_target_pairs={{0,16},{4,20},{8,24},{12,28},{16,0},{20,4},{24,8},{28,12},{1,17},{... | collective-permute-start | bytes 589832 | tf_op jit(solution)/shard_map/ppermute | solution.py:22
  12.6 4.0 %collective-permute-done.2.refs_4_ = bf16[2,3,128,128]{3,2,1,0:T(8,128)(2,1)S(1)} collective-permute-done((bf16[2,3,128,128]{3,2,1,0:T(8,128)(2,1)S(1)}, bf16[2,3,128,128]{3,2,1,0:T(8,128)(2,1)S(1)}, u32[]{:S(2)}, u32[]{:S(2)}) %collective-permute-start.2) | collective-permute-done | bytes 196640 | tf_op jit(solution)/shard_map/ppermute | solution.py:22
  16.6 3.4 %collective-permute-done.4.refs_6_ = bf16[2,3,128,128]{3,2,1,0:T(8,128)(2,1)S(1)} collective-permute-done((bf16[2,3,128,128]{3,2,1,0:T(8,128)(2,1)S(1)}, bf16[2,3,128,128]{3,2,1,0:T(8,128)(2,1)S(1)}, u32[]{:S(2)}, u32[]{:S(2)}) %collective-permute-start.4) | collective-permute-done | bytes 196640 | tf_op jit(solution)/shard_map/ppermute | solution.py:22
  20.0 0.5 %collective-permute-start.7 = (bf16[2,3,128,128]{3,2,1,0:T(8,128)(2,1)S(1)}, bf16[2,3,128,128]{3,2,1,0:T(8,128)(2,1)S(1)}, u32[]{:S(2)}, u32[]{:S(2)}) collective-permute-start(bf16[2,3,128,128]{3,2,1,0:T(8,128)(2,1)S(1)} %collective-permute-done.6.refs_8_), channel_id=1, source_target_pairs={{0,4},{4,0},{8,12},{12,8},{16,20},{20,16},{24,28},{28,24},{1,5},{5... | collective-permute-start | bytes 589832 | tf_op jit(solution)/shard_map/ppermute | solution.py:22
  20.6 2.4 %collective-permute-start.10 = (bf16[768,128]{1,0:T(8,128)(2,1)S(1)}, bf16[768,128]{1,0:T(8,128)(2,1)S(1)}, u32[]{:S(2)}, u32[]{:S(2)}) collective-permute-start(bf16[768,128]{1,0:T(8,128)(2,1)S(1)} %get-tuple-element.27.refs_12_), channel_id=1, source_target_pairs={{0,1},{1,0},{2,3},{3,2},{4,5},{5,4},{6,7},{7,6},{8,9},{9,8},{10,11... | collective-permute-start | bytes 589832 | tf_op jit(solution)/shard_map/ppermute | solution.py:22
  23.0 2.5 %shard_map.49 = (f32[2,256,128]{2,1,0:T(8,128)S(1)}, f32[128,256]{1,0:T(8,128)S(1)}, bf16[2,24,128,128]{3,2,1,0:T(8,128)(2,1)S(1)}) custom-call(s32[2]{0:T(128)S(1)} %pad_add_fusion.refs_0_, s32[16,128]{1,0:T(8,128)S(1)} %get-tuple-element.23.refs_1_, bf16[2,3,128,128]{3,2,1,0:T(8,128)(2,1)S(1)} %shard_map.48.refs_2_, ...), custom_call_target="tpu_custom_call" | custom-call | flops 3750000128 | bytes 2097152 | tf_op jit(solution)/shard_map/pallas_call | solution.py:295
  25.5 0.4 collective-permute-done.8.refs_3_
  25.9 1.7 %shard_map.50 = (f32[256,128]{1,0:T(8,128)S(1)}, f32[128,128]{1,0:T(8,128)S(1)}, f32[128,128]{1,0:T(8,128)S(1)}, s32[16,128]{1,0:T(8,128)S(1)}) custom-call(s32[2]{0:T(128)S(1)} %pad_add_fusion.refs_0_, bf16[2,24,128,128]{3,2,1,0:T(8,128)(2,1)S(1)} %get-tuple-element.28.refs_1_.refs_2_, f32[2,256,128]{2,1,0:T(8,128)S(1)} %get-tuple-element.29.refs_2_, ...), custom_call_target="tpu_custom_call" | custom-call | flops 250000000 | bytes 2097152 | tf_op jit(solution)/shard_map/pallas_call | solution.py:301
  27.6 1.4 %shard_map.51.refs_1_ = bf16[256,1536]{1,0:T(8,128)(2,1)S(1)} custom-call(s32[2]{0:T(128)S(1)} %pad_add_fusion.refs_0_, s32[16,128]{1,0:T(8,128)S(1)} %get-tuple-element.33.refs_1_, bf16[2,24,128,128]{3,2,1,0:T(8,128)(2,1)S(1)} %get-tuple-element.28.refs_1_.refs_2_), custom_call_target="tpu_custom_call" | custom-call | flops 268435456 | bytes 2097152 | tf_op jit(solution)/shard_map/pallas_call | solution.py:309
  29.0 2.6 %collective-permute-start.12 = (f32[128,128]{1,0:T(8,128)S(1)}, f32[128,128]{1,0:T(8,128)S(1)}, u32[]{:S(2)}, u32[]{:S(2)}) collective-permute-start(f32[128,128]{1,0:T(8,128)S(1)} %get-tuple-element.38), channel_id=1, source_target_pairs={{0,2},{1,3},{2,0},{3,1},{4,6},{5,7},{6,4},{7,5},{8,10},{9,11},{10,... | collective-permute-start | bytes 196616 | tf_op jit(solution)/shard_map/ppermute | solution.py:22
  31.6 0.4 %collective-permute-start.11 = (f32[128,128]{1,0:T(8,128)S(1)}, f32[128,128]{1,0:T(8,128)S(1)}, u32[]{:S(2)}, u32[]{:S(2)}) collective-permute-start(f32[128,128]{1,0:T(8,128)S(1)} %get-tuple-element.37), channel_id=1, source_target_pairs={{0,2},{1,3},{2,0},{3,1},{4,6},{5,7},{6,4},{7,5},{8,10},{9,11},{10,... | collective-permute-start | bytes 196616 | tf_op jit(solution)/shard_map/ppermute | solution.py:22
  32.0 0.4 shard_map.53
  32.4 2.6 %collective-permute-start.14 = (f32[64,128]{1,0:T(8,128)S(1)}, f32[64,128]{1,0:T(8,128)S(1)}, u32[]{:S(2)}, u32[]{:S(2)}) collective-permute-start(f32[64,128]{1,0:T(8,128)S(1)} %get-tuple-element.40), channel_id=1, source_target_pairs={{0,2},{1,3},{2,0},{3,1},{4,6},{5,7},{6,4},{7,5},{8,10},{9,11},{10,... | collective-permute-start | bytes 98312 | tf_op jit(solution)/shard_map/ppermute | solution.py:22
  34.9 0.9 %collective-permute-done.9.refs_2_ = bf16[768,128]{1,0:T(8,128)(2,1)S(1)} collective-permute-done((bf16[768,128]{1,0:T(8,128)(2,1)S(1)}, bf16[768,128]{1,0:T(8,128)(2,1)S(1)}, u32[]{:S(2)}, u32[]{:S(2)}) %collective-permute-start.9) | collective-permute-done | bytes 196640 | tf_op jit(solution)/shard_map/ppermute | solution.py:22
  36.2 0.4 collective-permute-start.13
  36.6 4.0 %collective-permute-done.14.refs_6_ = f32[64,128]{1,0:T(8,128)S(1)} collective-permute-done((f32[64,128]{1,0:T(8,128)S(1)}, f32[64,128]{1,0:T(8,128)S(1)}, u32[]{:S(2)}, u32[]{:S(2)}) %collective-permute-start.14) | collective-permute-done | bytes 32800 | tf_op jit(solution)/shard_map/ppermute | solution.py:22
  40.6 0.5 %collective-permute-done.13.refs_5_ = f32[64,128]{1,0:T(8,128)S(1)} collective-permute-done((f32[64,128]{1,0:T(8,128)S(1)}, f32[64,128]{1,0:T(8,128)S(1)}, u32[]{:S(2)}, u32[]{:S(2)}) %collective-permute-start.13) | collective-permute-done | bytes 32800 | tf_op jit(solution)/shard_map/ppermute | solution.py:22
  41.1 0.8 %shard_map.54 = f32[128,384]{1,0:T(8,128)} custom-call(f32[256,128]{1,0:T(8,128)S(1)} %get-tuple-element.30.refs_0_, f32[64,128]{1,0:T(8,128)S(1)} %get-tuple-element.35.refs_1_, f32[64,128]{1,0:T(8,128)S(1)} %get-tuple-element.36.refs_2_, f32[128,128]{1,0:T(8,128)S(1)} %collective-permute-done.11.refs_3_, f32[128,128]{1,0:T(8,128)S(1)} %collective-permute-done.12.refs_4_, ...), custom_call_target="tpu_custom_call" | custom-call | flops 1048576 | bytes 2097152 | tf_op jit(solution)/shard_map/pallas_call | solution.py:323
  (16 shorter events, 0.8 us)
Async XLA Ops:
  0.0 9.1 %collective-permute-start = (bf16[3,128,128]{2,1,0:T(8,128)(2,1)}, bf16[3,128,128]{2,1,0:T(8,128)(2,1)S(1)}, u32[]{:S(2)}, u32[]{:S(2)}) collective-permute-start(bf16[3,128,128]{2,1,0:T(8,128)(2,1)} %amplitudes.1), channel_id=1, source_target_pairs={{0,2},{1,3},{2,0},{3,1},{4,6},{5,7},{6,4},{7,5},{8,10},{9,11},{10,... | collective-permute-start | bytes 294920 | tf_op jit(solution)/shard_map/ppermute | solution.py:22
  5.2 20.7 %collective-permute-start.8 = (bf16[3088,128]{1,0:T(8,128)(2,1)S(1)}, bf16[3088,128]{1,0:T(8,128)(2,1)S(1)}, u32[]{:S(2)}, u32[]{:S(2)}) collective-permute-start(bf16[3088,128]{1,0:T(8,128)(2,1)S(1)} %get-tuple-element.25.refs_10_), channel_id=1, source_target_pairs={{0,1},{1,0},{2,3},{3,2},{4,5},{5,4},{6,7},{7,6},{8,9},{9,8},{10,11... | collective-permute-start | bytes 2371592 | tf_op jit(solution)/shard_map/ppermute | solution.py:22
  9.1 7.6 %collective-permute-start.2 = (bf16[2,3,128,128]{3,2,1,0:T(8,128)(2,1)S(1)}, bf16[2,3,128,128]{3,2,1,0:T(8,128)(2,1)S(1)}, u32[]{:S(2)}, u32[]{:S(2)}) collective-permute-start(bf16[2,3,128,128]{3,2,1,0:T(8,128)(2,1)S(1)} %shard_map.48.refs_2_), channel_id=1, source_target_pairs={{0,8},{4,12},{8,0},{12,4},{16,24},{20,28},{24,16},{28,20},{1,9},{5... | collective-permute-start | bytes 589832 | tf_op jit(solution)/shard_map/ppermute | solution.py:22
  10.9 9.1 %collective-permute-start.4 = (bf16[2,3,128,128]{3,2,1,0:T(8,128)(2,1)S(1)}, bf16[2,3,128,128]{3,2,1,0:T(8,128)(2,1)S(1)}, u32[]{:S(2)}, u32[]{:S(2)}) collective-permute-start(bf16[2,3,128,128]{3,2,1,0:T(8,128)(2,1)S(1)} %shard_map.48.refs_2_), channel_id=1, source_target_pairs={{0,16},{4,20},{8,24},{12,28},{16,0},{20,4},{24,8},{28,12},{1,17},{... | collective-permute-start | bytes 589832 | tf_op jit(solution)/shard_map/ppermute | solution.py:22
  12.4 7.6 %collective-permute-start.6 = (bf16[2,3,128,128]{3,2,1,0:T(8,128)(2,1)S(1)}, bf16[2,3,128,128]{3,2,1,0:T(8,128)(2,1)S(1)}, u32[]{:S(2)}, u32[]{:S(2)}) collective-permute-start(bf16[2,3,128,128]{3,2,1,0:T(8,128)(2,1)S(1)} %shard_map.48.refs_2_), channel_id=1, source_target_pairs={{0,24},{4,28},{8,16},{12,20},{16,8},{20,12},{24,0},{28,4},{1,25},{... | collective-permute-start | bytes 589832 | tf_op jit(solution)/shard_map/ppermute | solution.py:22
  12.6 8.0 %collective-permute-start.1 = (bf16[2,3,128,128]{3,2,1,0:T(8,128)(2,1)S(1)}, bf16[2,3,128,128]{3,2,1,0:T(8,128)(2,1)S(1)}, u32[]{:S(2)}, u32[]{:S(2)}) collective-permute-start(bf16[2,3,128,128]{3,2,1,0:T(8,128)(2,1)S(1)} %shard_map.48.refs_2_), channel_id=1, source_target_pairs={{0,4},{4,0},{8,12},{12,8},{16,20},{20,16},{24,28},{28,24},{1,5},{5... | collective-permute-start | bytes 589832 | tf_op jit(solution)/shard_map/ppermute | solution.py:22
  16.6 6.3 %collective-permute-start.3 = (bf16[2,3,128,128]{3,2,1,0:T(8,128)(2,1)S(1)}, bf16[2,3,128,128]{3,2,1,0:T(8,128)(2,1)S(1)}, u32[]{:S(2)}, u32[]{:S(2)}) collective-permute-start(bf16[2,3,128,128]{3,2,1,0:T(8,128)(2,1)S(1)} %collective-permute-done.2.refs_4_), channel_id=1, source_target_pairs={{0,4},{4,0},{8,12},{12,8},{16,20},{20,16},{24,28},{28,24},{1,5},{5... | collective-permute-start | bytes 589832 | tf_op jit(solution)/shard_map/ppermute | solution.py:22
  20.0 3.0 %collective-permute-start.5 = (bf16[2,3,128,128]{3,2,1,0:T(8,128)(2,1)S(1)}, bf16[2,3,128,128]{3,2,1,0:T(8,128)(2,1)S(1)}, u32[]{:S(2)}, u32[]{:S(2)}) collective-permute-start(bf16[2,3,128,128]{3,2,1,0:T(8,128)(2,1)S(1)} %collective-permute-done.4.refs_6_), channel_id=1, source_target_pairs={{0,4},{4,0},{8,12},{12,8},{16,20},{20,16},{24,28},{28,24},{1,5},{5... | collective-permute-start | bytes 589832 | tf_op jit(solution)/shard_map/ppermute | solution.py:22
  20.0 3.0 %collective-permute-start.7 = (bf16[2,3,128,128]{3,2,1,0:T(8,128)(2,1)S(1)}, bf16[2,3,128,128]{3,2,1,0:T(8,128)(2,1)S(1)}, u32[]{:S(2)}, u32[]{:S(2)}) collective-permute-start(bf16[2,3,128,128]{3,2,1,0:T(8,128)(2,1)S(1)} %collective-permute-done.6.refs_8_), channel_id=1, source_target_pairs={{0,4},{4,0},{8,12},{12,8},{16,20},{20,16},{24,28},{28,24},{1,5},{5... | collective-permute-start | bytes 589832 | tf_op jit(solution)/shard_map/ppermute | solution.py:22
  20.6 11.4 %collective-permute-start.10 = (bf16[768,128]{1,0:T(8,128)(2,1)S(1)}, bf16[768,128]{1,0:T(8,128)(2,1)S(1)}, u32[]{:S(2)}, u32[]{:S(2)}) collective-permute-start(bf16[768,128]{1,0:T(8,128)(2,1)S(1)} %get-tuple-element.27.refs_12_), channel_id=1, source_target_pairs={{0,1},{1,0},{2,3},{3,2},{4,5},{5,4},{6,7},{7,6},{8,9},{9,8},{10,11... | collective-permute-start | bytes 589832 | tf_op jit(solution)/shard_map/ppermute | solution.py:22
  22.9 12.9 %collective-permute-start.9 = (bf16[768,128]{1,0:T(8,128)(2,1)S(1)}, bf16[768,128]{1,0:T(8,128)(2,1)S(1)}, u32[]{:S(2)}, u32[]{:S(2)}) collective-permute-start(bf16[768,128]{1,0:T(8,128)(2,1)S(1)} %get-tuple-element.26.refs_11_), channel_id=1, source_target_pairs={{0,1},{1,0},{2,3},{3,2},{4,5},{5,4},{6,7},{7,6},{8,9},{9,8},{10,11... | collective-permute-start | bytes 589832 | tf_op jit(solution)/shard_map/ppermute | solution.py:22
  29.0 12.1 %collective-permute-start.12 = (f32[128,128]{1,0:T(8,128)S(1)}, f32[128,128]{1,0:T(8,128)S(1)}, u32[]{:S(2)}, u32[]{:S(2)}) collective-permute-start(f32[128,128]{1,0:T(8,128)S(1)} %get-tuple-element.38), channel_id=1, source_target_pairs={{0,2},{1,3},{2,0},{3,1},{4,6},{5,7},{6,4},{7,5},{8,10},{9,11},{10,... | collective-permute-start | bytes 196616 | tf_op jit(solution)/shard_map/ppermute | solution.py:22
  31.6 9.5 %collective-permute-start.11 = (f32[128,128]{1,0:T(8,128)S(1)}, f32[128,128]{1,0:T(8,128)S(1)}, u32[]{:S(2)}, u32[]{:S(2)}) collective-permute-start(f32[128,128]{1,0:T(8,128)S(1)} %get-tuple-element.37), channel_id=1, source_target_pairs={{0,2},{1,3},{2,0},{3,1},{4,6},{5,7},{6,4},{7,5},{8,10},{9,11},{10,... | collective-permute-start | bytes 196616 | tf_op jit(solution)/shard_map/ppermute | solution.py:22
  32.4 8.2 %collective-permute-start.14 = (f32[64,128]{1,0:T(8,128)S(1)}, f32[64,128]{1,0:T(8,128)S(1)}, u32[]{:S(2)}, u32[]{:S(2)}) collective-permute-start(f32[64,128]{1,0:T(8,128)S(1)} %get-tuple-element.40), channel_id=1, source_target_pairs={{0,2},{1,3},{2,0},{3,1},{4,6},{5,7},{6,4},{7,5},{8,10},{9,11},{10,... | collective-permute-start | bytes 98312 | tf_op jit(solution)/shard_map/ppermute | solution.py:22
  36.2 4.9 %collective-permute-start.13 = (f32[64,128]{1,0:T(8,128)S(1)}, f32[64,128]{1,0:T(8,128)S(1)}, u32[]{:S(2)}, u32[]{:S(2)}) collective-permute-start(f32[64,128]{1,0:T(8,128)S(1)} %get-tuple-element.39), channel_id=1, source_target_pairs={{0,2},{1,3},{2,0},{3,1},{4,6},{5,7},{6,4},{7,5},{8,10},{9,11},{10,... | collective-permute-start | bytes 98312 | tf_op jit(solution)/shard_map/ppermute | solution.py:22

commit v9 on v8

--- a/solution.py
+++ b/solution.py
@@ -9,7 +9,7 @@
 UNROLL = 12
 OWN_FLOPS = 3750000000
 HEAD_FLOPS = 250000000
-SOON = 4
+SOON = 5
 TABLE_ROWS = 16
 PARTS = 2
 SMEM = pl.BlockSpec(memory_space=pltpu.SMEM)

time: 42.1 us -> 42.4 us (level)
  waiting for transfers between devices: 14.2 us -> 15.2 us
  starting transfers between devices: 18.1 us -> 17.5 us
    ppermute x15, waiting for transfers between devices: 14.2 us -> 15.2 us  [shift(): return lax.ppermute(value, axis, [(j, j ^ mask) for j in range(size)])]
    ppermute x15, starting transfers between devices: 18.1 us -> 17.5 us  [shift(): return lax.ppermute(value, axis, [(j, j ^ mask) for j in range(size)])]
  transfers between devices with their start and end apart: 15 -> 15, of which waited for: 7 -> 7; matrix products, arithmetic and copies ran while one was open for 0% -> 0% of each run, Pallas kernels for 21% -> 20%
where the time goes in v9:
time: 42.4 us; the launch traced here: 42.3 us
  starting transfers between devices  17.5 us (41%)
  waiting for transfers between devices  15.2 us (36%)
  Pallas kernels  9.39 us (22%)
    ppermute x15, starting transfers between devices, shift(): return lax.ppermute(value, axis, [(j, j ^ mask) for j in range(size)])  17.5 us
    ppermute x15, waiting for transfers between devices, shift(): return lax.ppermute(value, axis, [(j, j ^ mask) for j in range(size)])  15.2 us
    pallas_call x1, Pallas kernels, on_pairs(): call(lambda *refs: own_kernel(masks, slots, *refs), (f32(before, 2 * rows...  2.48 us
    pallas_call x1, Pallas kernels, on_pairs(): call(lambda *refs: head_kernel(slots, *refs), (f32(before * rows, width),...  1.65 us
    pallas_call x1, Pallas kernels, on_pairs(): call(lambda *refs: pick_kernel(before, slots, *refs), jax.ShapeDtypeStruc...  1.4 us
    pallas_call x1, Pallas kernels, cut(): pl.pallas_call(rest_cut_kernel, out_shape=(jax.ShapeDtypeStruct((sizes[1]...  1.2 us
    pallas_call x1, Pallas kernels, cut(): pl.pallas_call(head_cut_kernel, out_shape=(jax.ShapeDtypeStruct((sizes[0]...  1.16 us
  transfers between devices with their start and end apart: 15, of which 7 were waited for; matrix products, arithmetic and copies ran while one was open for 0% of the time, Pallas kernels for 20%

profile of v9, /device:TPU:0, one launch (start us, length us, event | category | flops | bytes accessed | tf_op | source)
XLA Modules:
  0.0 42.3 jit_solution(15302600655336734137)
XLA Ops:
  0.0 4.0 %collective-permute-start = (bf16[3,128,128]{2,1,0:T(8,128)(2,1)}, bf16[3,128,128]{2,1,0:T(8,128)(2,1)S(1)}, u32[]{:S(2)}, u32[]{:S(2)}) collective-permute-start(bf16[3,128,128]{2,1,0:T(8,128)(2,1)} %amplitudes.1), channel_id=1, source_target_pairs={{0,2},{1,3},{2,0},{3,1},{4,6},{5,7},{6,4},{7,5},{8,10},{9,11},{10,... | collective-permute-start | bytes 294920 | tf_op jit(solution)/shard_map/ppermute | solution.py:22
  4.0 1.2 %shard_map.46 = (bf16[3088,128]{1,0:T(8,128)(2,1)S(1)}, s32[16,128]{1,0:T(8,128)S(1)}) custom-call(bf16[3,12,128,128]{3,2,1,0:T(8,128)(2,1)} %whole.3, s32[3,12]{1,0:T(4,128)} %lists.1, s32[3]{0:T(128)} %counts.1), custom_call_target="tpu_custom_call" | custom-call | tf_op jit(solution)/shard_map/pallas_call | solution.py:125
  5.2 1.6 %collective-permute-start.8 = (bf16[3088,128]{1,0:T(8,128)(2,1)S(1)}, bf16[3088,128]{1,0:T(8,128)(2,1)S(1)}, u32[]{:S(2)}, u32[]{:S(2)}) collective-permute-start(bf16[3088,128]{1,0:T(8,128)(2,1)S(1)} %get-tuple-element.25.refs_10_), channel_id=1, source_target_pairs={{0,1},{1,0},{2,3},{3,2},{4,5},{5,4},{6,7},{7,6},{8,9},{9,8},{10,11... | collective-permute-start | bytes 2371592 | tf_op jit(solution)/shard_map/ppermute | solution.py:22
  6.9 1.2 %shard_map.47 = (bf16[768,128]{1,0:T(8,128)(2,1)S(1)}, bf16[768,128]{1,0:T(8,128)(2,1)S(1)}, bf16[3,128,128]{2,1,0:T(8,128)(2,1)S(1)}) custom-call(bf16[3,12,128,128]{3,2,1,0:T(8,128)(2,1)} %whole.3, bf16[3,128,128]{2,1,0:T(8,128)(2,1)} %amplitudes.1), custom_call_target="tpu_custom_call" | custom-call | flops 1048576 | bytes 524288 | tf_op jit(solution)/shard_map/pallas_call | solution.py:140
  8.1 1.0 %collective-permute-done.second = bf16[3,128,128]{2,1,0:T(8,128)(2,1)S(1)} collective-permute-done((bf16[3,128,128]{2,1,0:T(8,128)(2,1)}, bf16[3,128,128]{2,1,0:T(8,128)(2,1)S(1)}, u32[]{:S(2)}, u32[]{:S(2)}) %collective-permute-start) | collective-permute-done | bytes 98336 | tf_op jit(solution)/shard_map/ppermute | solution.py:22
  9.1 1.8 %collective-permute-start.2 = (bf16[2,3,128,128]{3,2,1,0:T(8,128)(2,1)S(1)}, bf16[2,3,128,128]{3,2,1,0:T(8,128)(2,1)S(1)}, u32[]{:S(2)}, u32[]{:S(2)}) collective-permute-start(bf16[2,3,128,128]{3,2,1,0:T(8,128)(2,1)S(1)} %shard_map.48.refs_2_), channel_id=1, source_target_pairs={{0,8},{4,12},{8,0},{12,4},{16,24},{20,28},{24,16},{28,20},{1,9},{5... | collective-permute-start | bytes 589832 | tf_op jit(solution)/shard_map/ppermute | solution.py:22
  10.9 1.5 %collective-permute-start.4 = (bf16[2,3,128,128]{3,2,1,0:T(8,128)(2,1)S(1)}, bf16[2,3,128,128]{3,2,1,0:T(8,128)(2,1)S(1)}, u32[]{:S(2)}, u32[]{:S(2)}) collective-permute-start(bf16[2,3,128,128]{3,2,1,0:T(8,128)(2,1)S(1)} %shard_map.48.refs_2_), channel_id=1, source_target_pairs={{0,16},{4,20},{8,24},{12,28},{16,0},{20,4},{24,8},{28,12},{1,17},{... | collective-permute-start | bytes 589832 | tf_op jit(solution)/shard_map/ppermute | solution.py:22
  12.6 4.0 %collective-permute-done.2.refs_4_ = bf16[2,3,128,128]{3,2,1,0:T(8,128)(2,1)S(1)} collective-permute-done((bf16[2,3,128,128]{3,2,1,0:T(8,128)(2,1)S(1)}, bf16[2,3,128,128]{3,2,1,0:T(8,128)(2,1)S(1)}, u32[]{:S(2)}, u32[]{:S(2)}) %collective-permute-start.2) | collective-permute-done | bytes 196640 | tf_op jit(solution)/shard_map/ppermute | solution.py:22
  16.6 3.4 %collective-permute-done.4.refs_6_ = bf16[2,3,128,128]{3,2,1,0:T(8,128)(2,1)S(1)} collective-permute-done((bf16[2,3,128,128]{3,2,1,0:T(8,128)(2,1)S(1)}, bf16[2,3,128,128]{3,2,1,0:T(8,128)(2,1)S(1)}, u32[]{:S(2)}, u32[]{:S(2)}) %collective-permute-start.4) | collective-permute-done | bytes 196640 | tf_op jit(solution)/shard_map/ppermute | solution.py:22
  20.0 0.5 %collective-permute-start.7 = (bf16[2,3,128,128]{3,2,1,0:T(8,128)(2,1)S(1)}, bf16[2,3,128,128]{3,2,1,0:T(8,128)(2,1)S(1)}, u32[]{:S(2)}, u32[]{:S(2)}) collective-permute-start(bf16[2,3,128,128]{3,2,1,0:T(8,128)(2,1)S(1)} %collective-permute-done.6.refs_8_), channel_id=1, source_target_pairs={{0,4},{4,0},{8,12},{12,8},{16,20},{20,16},{24,28},{28,24},{1,5},{5... | collective-permute-start | bytes 589832 | tf_op jit(solution)/shard_map/ppermute | solution.py:22
  20.6 2.4 %collective-permute-start.10 = (bf16[768,128]{1,0:T(8,128)(2,1)S(1)}, bf16[768,128]{1,0:T(8,128)(2,1)S(1)}, u32[]{:S(2)}, u32[]{:S(2)}) collective-permute-start(bf16[768,128]{1,0:T(8,128)(2,1)S(1)} %get-tuple-element.27.refs_12_), channel_id=1, source_target_pairs={{0,1},{1,0},{2,3},{3,2},{4,5},{5,4},{6,7},{7,6},{8,9},{9,8},{10,11... | collective-permute-start | bytes 589832 | tf_op jit(solution)/shard_map/ppermute | solution.py:22
  23.0 2.5 %shard_map.49 = (f32[2,256,128]{2,1,0:T(8,128)S(1)}, f32[128,256]{1,0:T(8,128)S(1)}, bf16[2,24,128,128]{3,2,1,0:T(8,128)(2,1)S(1)}) custom-call(s32[2]{0:T(128)S(1)} %pad_add_fusion.refs_0_, s32[16,128]{1,0:T(8,128)S(1)} %get-tuple-element.23.refs_1_, bf16[2,3,128,128]{3,2,1,0:T(8,128)(2,1)S(1)} %shard_map.48.refs_2_, ...), custom_call_target="tpu_custom_call" | custom-call | flops 3750000128 | bytes 2097152 | tf_op jit(solution)/shard_map/pallas_call | solution.py:295
  25.5 0.4 collective-permute-done.8.refs_3_
  25.9 1.7 %shard_map.50 = (f32[256,128]{1,0:T(8,128)S(1)}, f32[160,128]{1,0:T(8,128)S(1)}, f32[96,128]{1,0:T(8,128)S(1)}, s32[16,128]{1,0:T(8,128)S(1)}) custom-call(s32[2]{0:T(128)S(1)} %pad_add_fusion.refs_0_, bf16[2,24,128,128]{3,2,1,0:T(8,128)(2,1)S(1)} %get-tuple-element.28.refs_1_.refs_2_, f32[2,256,128]{2,1,0:T(8,128)S(1)} %get-tuple-element.29.refs_2_, ...), custom_call_target="tpu_custom_call" | custom-call | flops 250000000 | bytes 2097152 | tf_op jit(solution)/shard_map/pallas_call | solution.py:301
  27.6 1.4 %shard_map.51.refs_1_ = bf16[256,1536]{1,0:T(8,128)(2,1)S(1)} custom-call(s32[2]{0:T(128)S(1)} %pad_add_fusion.refs_0_, s32[16,128]{1,0:T(8,128)S(1)} %get-tuple-element.33.refs_1_, bf16[2,24,128,128]{3,2,1,0:T(8,128)(2,1)S(1)} %get-tuple-element.28.refs_1_.refs_2_), custom_call_target="tpu_custom_call" | custom-call | flops 268435456 | bytes 2097152 | tf_op jit(solution)/shard_map/pallas_call | solution.py:309
  29.0 2.1 %collective-permute-start.11 = (f32[160,128]{1,0:T(8,128)S(1)}, f32[160,128]{1,0:T(8,128)S(1)}, u32[]{:S(2)}, u32[]{:S(2)}) collective-permute-start(f32[160,128]{1,0:T(8,128)S(1)} %get-tuple-element.37), channel_id=1, source_target_pairs={{0,2},{1,3},{2,0},{3,1},{4,6},{5,7},{6,4},{7,5},{8,10},{9,11},{10,... | collective-permute-start | bytes 245768 | tf_op jit(solution)/shard_map/ppermute | solution.py:22
  31.1 0.4 shard_map.53
  31.5 0.9 %collective-permute-start.14 = (f32[64,128]{1,0:T(8,128)S(1)}, f32[64,128]{1,0:T(8,128)S(1)}, u32[]{:S(2)}, u32[]{:S(2)}) collective-permute-start(f32[64,128]{1,0:T(8,128)S(1)} %get-tuple-element.40), channel_id=1, source_target_pairs={{0,2},{1,3},{2,0},{3,1},{4,6},{5,7},{6,4},{7,5},{8,10},{9,11},{10,... | collective-permute-start | bytes 98312 | tf_op jit(solution)/shard_map/ppermute | solution.py:22
  32.4 2.1 %collective-permute-start.12 = (f32[96,128]{1,0:T(8,128)S(1)}, f32[96,128]{1,0:T(8,128)S(1)}, u32[]{:S(2)}, u32[]{:S(2)}) collective-permute-start(f32[96,128]{1,0:T(8,128)S(1)} %get-tuple-element.38), channel_id=1, source_target_pairs={{0,2},{1,3},{2,0},{3,1},{4,6},{5,7},{6,4},{7,5},{8,10},{9,11},{10,... | collective-permute-start | bytes 147464 | tf_op jit(solution)/shard_map/ppermute | solution.py:22
  34.5 1.5 %collective-permute-done.9.refs_2_ = bf16[768,128]{1,0:T(8,128)(2,1)S(1)} collective-permute-done((bf16[768,128]{1,0:T(8,128)(2,1)S(1)}, bf16[768,128]{1,0:T(8,128)(2,1)S(1)}, u32[]{:S(2)}, u32[]{:S(2)}) %collective-permute-start.9) | collective-permute-done | bytes 196640 | tf_op jit(solution)/shard_map/ppermute | solution.py:22
  36.0 0.4 shard_map.52
  36.6 3.1 %collective-permute-done.14.refs_6_ = f32[64,128]{1,0:T(8,128)S(1)} collective-permute-done((f32[64,128]{1,0:T(8,128)S(1)}, f32[64,128]{1,0:T(8,128)S(1)}, u32[]{:S(2)}, u32[]{:S(2)}) %collective-permute-start.14) | collective-permute-done | bytes 32800 | tf_op jit(solution)/shard_map/ppermute | solution.py:22
  39.6 1.8 %collective-permute-done.13.refs_5_ = f32[64,128]{1,0:T(8,128)S(1)} collective-permute-done((f32[64,128]{1,0:T(8,128)S(1)}, f32[64,128]{1,0:T(8,128)S(1)}, u32[]{:S(2)}, u32[]{:S(2)}) %collective-permute-start.13) | collective-permute-done | bytes 32800 | tf_op jit(solution)/shard_map/ppermute | solution.py:22
  41.5 0.8 %shard_map.54 = f32[128,384]{1,0:T(8,128)} custom-call(f32[256,128]{1,0:T(8,128)S(1)} %get-tuple-element.30.refs_0_, f32[64,128]{1,0:T(8,128)S(1)} %get-tuple-element.35.refs_1_, f32[64,128]{1,0:T(8,128)S(1)} %get-tuple-element.36.refs_2_, f32[160,128]{1,0:T(8,128)S(1)} %collective-permute-done.11.refs_3_, f32[96,128]{1,0:T(8,128)S(1)} %collective-permute-done.12.refs_4_, ...), custom_call_target="tpu_custom_call" | custom-call | flops 1048576 | bytes 2097152 | tf_op jit(solution)/shard_map/pallas_call | solution.py:323
  (16 shorter events, 0.6 us)
Async XLA Ops:
  0.0 9.1 %collective-permute-start = (bf16[3,128,128]{2,1,0:T(8,128)(2,1)}, bf16[3,128,128]{2,1,0:T(8,128)(2,1)S(1)}, u32[]{:S(2)}, u32[]{:S(2)}) collective-permute-start(bf16[3,128,128]{2,1,0:T(8,128)(2,1)} %amplitudes.1), channel_id=1, source_target_pairs={{0,2},{1,3},{2,0},{3,1},{4,6},{5,7},{6,4},{7,5},{8,10},{9,11},{10,... | collective-permute-start | bytes 294920 | tf_op jit(solution)/shard_map/ppermute | solution.py:22
  5.2 20.7 %collective-permute-start.8 = (bf16[3088,128]{1,0:T(8,128)(2,1)S(1)}, bf16[3088,128]{1,0:T(8,128)(2,1)S(1)}, u32[]{:S(2)}, u32[]{:S(2)}) collective-permute-start(bf16[3088,128]{1,0:T(8,128)(2,1)S(1)} %get-tuple-element.25.refs_10_), channel_id=1, source_target_pairs={{0,1},{1,0},{2,3},{3,2},{4,5},{5,4},{6,7},{7,6},{8,9},{9,8},{10,11... | collective-permute-start | bytes 2371592 | tf_op jit(solution)/shard_map/ppermute | solution.py:22
  9.1 7.6 %collective-permute-start.2 = (bf16[2,3,128,128]{3,2,1,0:T(8,128)(2,1)S(1)}, bf16[2,3,128,128]{3,2,1,0:T(8,128)(2,1)S(1)}, u32[]{:S(2)}, u32[]{:S(2)}) collective-permute-start(bf16[2,3,128,128]{3,2,1,0:T(8,128)(2,1)S(1)} %shard_map.48.refs_2_), channel_id=1, source_target_pairs={{0,8},{4,12},{8,0},{12,4},{16,24},{20,28},{24,16},{28,20},{1,9},{5... | collective-permute-start | bytes 589832 | tf_op jit(solution)/shard_map/ppermute | solution.py:22
  10.9 9.1 %collective-permute-start.4 = (bf16[2,3,128,128]{3,2,1,0:T(8,128)(2,1)S(1)}, bf16[2,3,128,128]{3,2,1,0:T(8,128)(2,1)S(1)}, u32[]{:S(2)}, u32[]{:S(2)}) collective-permute-start(bf16[2,3,128,128]{3,2,1,0:T(8,128)(2,1)S(1)} %shard_map.48.refs_2_), channel_id=1, source_target_pairs={{0,16},{4,20},{8,24},{12,28},{16,0},{20,4},{24,8},{28,12},{1,17},{... | collective-permute-start | bytes 589832 | tf_op jit(solution)/shard_map/ppermute | solution.py:22
  12.4 7.6 %collective-permute-start.6 = (bf16[2,3,128,128]{3,2,1,0:T(8,128)(2,1)S(1)}, bf16[2,3,128,128]{3,2,1,0:T(8,128)(2,1)S(1)}, u32[]{:S(2)}, u32[]{:S(2)}) collective-permute-start(bf16[2,3,128,128]{3,2,1,0:T(8,128)(2,1)S(1)} %shard_map.48.refs_2_), channel_id=1, source_target_pairs={{0,24},{4,28},{8,16},{12,20},{16,8},{20,12},{24,0},{28,4},{1,25},{... | collective-permute-start | bytes 589832 | tf_op jit(solution)/shard_map/ppermute | solution.py:22
  12.6 8.0 %collective-permute-start.1 = (bf16[2,3,128,128]{3,2,1,0:T(8,128)(2,1)S(1)}, bf16[2,3,128,128]{3,2,1,0:T(8,128)(2,1)S(1)}, u32[]{:S(2)}, u32[]{:S(2)}) collective-permute-start(bf16[2,3,128,128]{3,2,1,0:T(8,128)(2,1)S(1)} %shard_map.48.refs_2_), channel_id=1, source_target_pairs={{0,4},{4,0},{8,12},{12,8},{16,20},{20,16},{24,28},{28,24},{1,5},{5... | collective-permute-start | bytes 589832 | tf_op jit(solution)/shard_map/ppermute | solution.py:22
  16.6 6.3 %collective-permute-start.3 = (bf16[2,3,128,128]{3,2,1,0:T(8,128)(2,1)S(1)}, bf16[2,3,128,128]{3,2,1,0:T(8,128)(2,1)S(1)}, u32[]{:S(2)}, u32[]{:S(2)}) collective-permute-start(bf16[2,3,128,128]{3,2,1,0:T(8,128)(2,1)S(1)} %collective-permute-done.2.refs_4_), channel_id=1, source_target_pairs={{0,4},{4,0},{8,12},{12,8},{16,20},{20,16},{24,28},{28,24},{1,5},{5... | collective-permute-start | bytes 589832 | tf_op jit(solution)/shard_map/ppermute | solution.py:22
  20.0 3.0 %collective-permute-start.5 = (bf16[2,3,128,128]{3,2,1,0:T(8,128)(2,1)S(1)}, bf16[2,3,128,128]{3,2,1,0:T(8,128)(2,1)S(1)}, u32[]{:S(2)}, u32[]{:S(2)}) collective-permute-start(bf16[2,3,128,128]{3,2,1,0:T(8,128)(2,1)S(1)} %collective-permute-done.4.refs_6_), channel_id=1, source_target_pairs={{0,4},{4,0},{8,12},{12,8},{16,20},{20,16},{24,28},{28,24},{1,5},{5... | collective-permute-start | bytes 589832 | tf_op jit(solution)/shard_map/ppermute | solution.py:22
  20.0 3.0 %collective-permute-start.7 = (bf16[2,3,128,128]{3,2,1,0:T(8,128)(2,1)S(1)}, bf16[2,3,128,128]{3,2,1,0:T(8,128)(2,1)S(1)}, u32[]{:S(2)}, u32[]{:S(2)}) collective-permute-start(bf16[2,3,128,128]{3,2,1,0:T(8,128)(2,1)S(1)} %collective-permute-done.6.refs_8_), channel_id=1, source_target_pairs={{0,4},{4,0},{8,12},{12,8},{16,20},{20,16},{24,28},{28,24},{1,5},{5... | collective-permute-start | bytes 589832 | tf_op jit(solution)/shard_map/ppermute | solution.py:22
  20.6 10.6 %collective-permute-start.10 = (bf16[768,128]{1,0:T(8,128)(2,1)S(1)}, bf16[768,128]{1,0:T(8,128)(2,1)S(1)}, u32[]{:S(2)}, u32[]{:S(2)}) collective-permute-start(bf16[768,128]{1,0:T(8,128)(2,1)S(1)} %get-tuple-element.27.refs_12_), channel_id=1, source_target_pairs={{0,1},{1,0},{2,3},{3,2},{4,5},{5,4},{6,7},{7,6},{8,9},{9,8},{10,11... | collective-permute-start | bytes 589832 | tf_op jit(solution)/shard_map/ppermute | solution.py:22
  22.9 13.1 %collective-permute-start.9 = (bf16[768,128]{1,0:T(8,128)(2,1)S(1)}, bf16[768,128]{1,0:T(8,128)(2,1)S(1)}, u32[]{:S(2)}, u32[]{:S(2)}) collective-permute-start(bf16[768,128]{1,0:T(8,128)(2,1)S(1)} %get-tuple-element.26.refs_11_), channel_id=1, source_target_pairs={{0,1},{1,0},{2,3},{3,2},{4,5},{5,4},{6,7},{7,6},{8,9},{9,8},{10,11... | collective-permute-start | bytes 589832 | tf_op jit(solution)/shard_map/ppermute | solution.py:22
  29.0 12.5 %collective-permute-start.11 = (f32[160,128]{1,0:T(8,128)S(1)}, f32[160,128]{1,0:T(8,128)S(1)}, u32[]{:S(2)}, u32[]{:S(2)}) collective-permute-start(f32[160,128]{1,0:T(8,128)S(1)} %get-tuple-element.37), channel_id=1, source_target_pairs={{0,2},{1,3},{2,0},{3,1},{4,6},{5,7},{6,4},{7,5},{8,10},{9,11},{10,... | collective-permute-start | bytes 245768 | tf_op jit(solution)/shard_map/ppermute | solution.py:22
  31.5 8.1 %collective-permute-start.14 = (f32[64,128]{1,0:T(8,128)S(1)}, f32[64,128]{1,0:T(8,128)S(1)}, u32[]{:S(2)}, u32[]{:S(2)}) collective-permute-start(f32[64,128]{1,0:T(8,128)S(1)} %get-tuple-element.40), channel_id=1, source_target_pairs={{0,2},{1,3},{2,0},{3,1},{4,6},{5,7},{6,4},{7,5},{8,10},{9,11},{10,... | collective-permute-start | bytes 98312 | tf_op jit(solution)/shard_map/ppermute | solution.py:22
  32.4 9.1 %collective-permute-start.12 = (f32[96,128]{1,0:T(8,128)S(1)}, f32[96,128]{1,0:T(8,128)S(1)}, u32[]{:S(2)}, u32[]{:S(2)}) collective-permute-start(f32[96,128]{1,0:T(8,128)S(1)} %get-tuple-element.38), channel_id=1, source_target_pairs={{0,2},{1,3},{2,0},{3,1},{4,6},{5,7},{6,4},{7,5},{8,10},{9,11},{10,... | collective-permute-start | bytes 147464 | tf_op jit(solution)/shard_map/ppermute | solution.py:22
  36.4 5.1 %collective-permute-start.13 = (f32[64,128]{1,0:T(8,128)S(1)}, f32[64,128]{1,0:T(8,128)S(1)}, u32[]{:S(2)}, u32[]{:S(2)}) collective-permute-start(f32[64,128]{1,0:T(8,128)S(1)} %get-tuple-element.39), channel_id=1, source_target_pairs={{0,2},{1,3},{2,0},{3,1},{4,6},{5,7},{6,4},{7,5},{8,10},{9,11},{10,... | collective-permute-start | bytes 98312 | tf_op jit(solution)/shard_map/ppermute | solution.py:22
